TPU v7x, 32 devices: a whole 2x2x4 slice. The times are simulated.
32 devices in a mesh: tm: 8 (over z, y), space: 4 (over x, core).
Axes of the slice: x: 2, y: 2, z: 4, core: 2. Of those that a mesh axis runs over, the one named last changes fastest.
Arguments:
- frames_in: bfloat16 [8, 256, 128, 128], P('tm', None, 'space'), may hold values from -6 to 6
- conv_weight: bfloat16 [3, 3, 256, 256], replicated, may hold values from -0.125 to 0.125
- out_weight: bfloat16 [256, 256], replicated, may hold values from -0.375 to 0.375
- skip_gain: float32 [256], replicated, may hold values from -4 to 4
- decays: float32 [8, 256], P('tm'), may hold values from 0.25 to 1, as said below
Outputs:
- frames_out: bfloat16 [8, 256, 128, 128], P('tm', None, 'space')
Inputs may be any that keep to these rules, and one draw needn't show every extreme that they name: `decays`: every entry lies strictly below 1.
All inputs are finite; a program needn't handle non-finite values.
Results may differ from a plain program's by a relative error of at most 0.0041.
Values may be sent and summed in bfloat16 or wider, within the bound.
No kernel may reach another device: no remote copies, remote signals or barrier semaphores. Data moves between devices by JAX's collectives and lax.ppermute only.
A program may use at most 320 MiB of HBM per device.

v0:
```python
import jax
import jax.numpy as jnp
from jax import lax
from jax.sharding import PartitionSpec as P


def with_halo(block, sides, width):
    for axis, dim in sides:
        count = lax.axis_size(axis)
        forward = [(i, i + 1) for i in range(count - 1)]
        backward = [(target, source) for source, target in forward]
        low = lax.ppermute(
            lax.slice_in_dim(block, block.shape[dim] - width, None, axis=dim), axis, forward
        )
        high = lax.ppermute(lax.slice_in_dim(block, 0, width, axis=dim), axis, backward)
        block = jnp.concatenate([low, block, high], axis=dim)
    return block


def column_shifts(values):
    zeros_col = jnp.zeros(values.shape[:-1] + (1,), values.dtype)
    left_view = jnp.concatenate([zeros_col, values[..., :-1]], axis=-1)
    right_view = jnp.concatenate([values[..., 1:], zeros_col], axis=-1)
    return (left_view, values, right_view)


def step_forward(memory, inputs):
    frame_rate, frame_input_drive = inputs
    memory = frame_rate[:, None] * memory + frame_input_drive
    return (memory, memory.astype(jnp.bfloat16))


def on_device(frames_in, conv_weight, out_weight, skip_gain, decays):
    frame_total_count = frames_in.shape[0]
    channels = frames_in.shape[1]
    tile_rows = frames_in.shape[2]
    width = frames_in.shape[3]
    states = conv_weight.shape[2]
    cell_count = tile_rows * width
    padded = with_halo(frames_in, (("space", 2),), 1)
    column_views = column_shifts(padded)
    flat_views = [
        view.reshape(frame_total_count, channels, (tile_rows + 2) * width) for view in column_views
    ]
    frame_idx = 0
    accum = jnp.zeros((states, cell_count), jnp.float32)
    for vertical_shift in range(3):
        for col_off in range(3):
            window = flat_views[col_off][
                frame_idx, :, vertical_shift * width : vertical_shift * width + cell_count
            ]
            accum = accum + jnp.dot(
                conv_weight[vertical_shift, col_off], window, preferred_element_type=jnp.float32
            )
    frame_drives = [accum]
    driving = jnp.stack(frame_drives, axis=0).reshape(frame_total_count, states, tile_rows, width)
    in_gain = jnp.sqrt(1.0 - decays * decays)
    scaled_drive = in_gain[:, :, None] * driving.reshape(frame_total_count, states, cell_count)
    by_cells = lax.all_to_all(scaled_drive, "tm", split_axis=2, concat_axis=0, tiled=True)
    all_rates = lax.all_gather(decays, "tm", axis=0, tiled=True)
    zero_state = jnp.zeros((states, by_cells.shape[2]), jnp.float32)
    ending, rounded_all = lax.scan(step_forward, zero_state, (all_rates, by_cells), unroll=8)
    rounded_return = lax.all_to_all(rounded_all, "tm", split_axis=0, concat_axis=2, tiled=True)
    frame_idx = 0
    output = jnp.dot(out_weight, rounded_return[frame_idx], preferred_element_type=jnp.float32)
    output = output.reshape(channels, tile_rows, width) + skip_gain[:, None, None] * frames_in[
        frame_idx
    ].astype(jnp.float32)
    results = [output.astype(jnp.bfloat16)]
    return jnp.stack(results, axis=0)


def solution(mesh):
    placed = (P("tm", None, "space", None), P(), P(), P(), P("tm", None))
    return jax.shard_map(
        on_device,
        mesh=mesh,
        in_specs=placed,
        out_specs=P("tm", None, "space", None),
        check_vma=False,
    )
```

profile of v0, /device:TPU:0, one launch (start us, length us, event | category | flops | bytes accessed | tf_op | source)
XLA Modules:
  0.0 213.9 jit_solution(14980877428293758041)
XLA Ops:
  0.0 0.0 copy-start
  0.0 0.0 copy-start.3
  0.0 3.0 %copy.37 = bf16[1,256,32,128]{1,3,2,0:T(8,128)(2,1)S(1)} copy(bf16[1,256,32,128]{3,2,1,0:T(8,128)(2,1)} %param.5) | data formatting | bytes 4194304 | tf_op args[0]
  3.1 2.4 %collective-permute-start = (bf16[1,256,1,128]{1,3,2,0:T(8,128)(2,1)S(1)}, bf16[1,256,1,128]{1,3,2,0:T(8,128)(2,1)S(1)}, u32[]{:S(2)}, u32[]{:S(2)}) collective-permute-start(bf16[1,256,1,128]{1,3,2,0:T(8,128)(2,1)S(1)} %get-tuple-element.13), channel_id=1, source_target_pairs={{0,1},{1,2},{2,3},{4,5},{5,6},{6,7},{8,9},{9,10},{10,11},{12,13},{... | collective-permute-start | bytes 196616 | tf_op jit(solution)/shard_map/ppermute | solution.py:12
  5.4 1.3 collective-permute-start.1
  6.7 0.0 copy-done.3
  6.8 0.0 collective-permute-done
  6.8 3.9 %collective-permute-done.1 = bf16[1,256,1,128]{1,3,2,0:T(8,128)(2,1)S(1)} collective-permute-done((bf16[1,256,1,128]{1,3,2,0:T(8,128)(2,1)S(1)}, bf16[1,256,1,128]{1,3,2,0:T(8,128)(2,1)S(1)}, u32[]{:S(2)}, u32[]{:S(2)}) %collective-permute-start.1) | collective-permute-done | bytes 65568 | tf_op jit(solution)/shard_map/ppermute | solution.py:15
  10.7 0.3 pad_maximum_fusion
  11.0 1.6 fusion.36
  12.6 0.2 concatenate.14
  12.8 0.0 copy-start.2
  12.8 1.3 concatenate.13
  14.1 0.0 copy-done.2
  14.1 0.7 fusion.2
  14.9 0.7 convolution_add_fusion.7
  15.6 0.8 convolution_add_fusion.6
  16.4 0.7 convolution_add_fusion.5
  17.2 0.7 convolution_add_fusion.4
  17.9 0.8 convolution_add_fusion.3
  18.7 0.7 convolution_add_fusion.2
  19.5 0.7 convolution_add_fusion.1
  20.2 0.7 fusion.1
  20.9 19.2 %copy.40 = f32[1,256,4096]{1,0,2:T(1,128)} copy(f32[1,256,4096]{1,2,0:T(8,128)S(1)} %fusion.1) | data formatting | bytes 8388608 | tf_op jit(solution)/shard_map/mul | solution.py:58
  40.1 5.8 %all-to-all-start = ((f32[1,256,4096]{1,0,2:T(1,128)}), f32[1,256,4096]{1,0,2:T(1,128)}, u32[]{:S(2)}, u32[]{:S(2)}) async-start(f32[1,256,4096]{1,0,2:T(1,128)} %copy.40), calls=%async_computation | async-start | bytes 8388608 | tf_op jit(solution)/shard_map/all_to_all | solution.py:59
  46.0 82.5 %all-gather = f32[8,1,256]{2,1,0:T(1,128)S(1)} all-gather(f32[1,1,256]{2,1,0:T(1,128)S(1)} %bitcast.176), channel_id=1, replica_groups=mesh['tm'=8,'space'=4] {'tm'}, dimensions={0}, use_global_device_ids=true | all-gather | bytes 9216 | tf_op jit(solution)/shard_map/all_gather | solution.py:60
  128.5 10.9 %all-to-all-done = f32[1,256,4096]{1,0,2:T(1,128)} async-done(((f32[1,256,4096]{1,0,2:T(1,128)}), f32[1,256,4096]{1,0,2:T(1,128)}, u32[]{:S(2)}, u32[]{:S(2)}) %all-to-all-start) | async-done | bytes 4194336 | tf_op jit(solution)/shard_map/all_to_all | solution.py:59
  139.4 2.5 %copy.42 = f32[1,256,4096]{1,2,0:T(8,128)S(1)} copy(f32[1,256,4096]{1,0,2:T(1,128)} %all-to-all-done) | data formatting | bytes 8388608
  141.9 0.1 convert_dynamic-update-slice_fusion.5
  142.0 0.1 convert_dynamic-update-slice_fusion.4
  142.1 0.1 convert_dynamic-update-slice_fusion.3
  142.2 0.1 convert_dynamic-update-slice_fusion.2
  142.3 0.1 convert_dynamic-update-slice_fusion.1
  142.4 0.1 convert_dynamic-update-slice_fusion
  142.5 0.1 fusion.14
  142.6 58.8 %all_to_all.30 = bf16[8,256,512]{1,2,0:T(8,128)(2,1)S(1)} all-to-all(bf16[8,256,512]{1,2,0:T(8,128)(2,1)S(1)} %fusion.14), channel_id=1, replica_groups=mesh['tm'=8,'space'=4] {'tm'}, dimensions={0} | all-to-all | bytes 4194304 | tf_op jit(solution)/shard_map/all_to_all | solution.py:63
  201.4 0.0 copy-done
  201.4 2.7 %fusion.39 = f32[4096,256]{1,0:T(8,128)} fusion(bf16[256,4096]{0,1:T(8,128)(2,1)S(1)} %bitcast.162, bf16[256,256]{1,0:T(8,128)(2,1)S(1)} %copy-done), kind=kOutput, calls=%fused_computation.71 | convolution fusion | flops 536870912 | bytes 6422528 | tf_op jit(solution)/shard_map/dot_general | solution.py:65
  204.1 0.0 copy-start.1
  204.1 0.0 copy-start.4
  204.1 5.7 %copy.41 = f32[1,256,32,128]{3,2,1,0:T(8,128)} copy(f32[1,256,32,128]{1,3,2,0:T(8,128)} %bitcast.153) | data formatting | bytes 8388608 | tf_op jit(solution)/shard_map/reshape | solution.py:66
  209.7 0.0 copy-done.1
  209.7 0.0 copy-done.4
  209.7 4.1 %add_convert_fusion = bf16[1,256,32,128]{3,2,1,0:T(8,128)(2,1)} fusion(f32[1,256,32,128]{3,2,1,0:T(8,128)} %copy.41, bf16[1,256,32,128]{3,2,1,0:T(8,128)(2,1)S(1)} %copy-done.1, f32[256]{0:T(256)S(1)} %copy-done.4), kind=kLoop, calls=%fused_computation.10 | loop fusion | flops 4194304 | bytes 8389632 | tf_op jit(solution)/shard_map/convert_element_type | solution.py:69
  (4 shorter events, 0.1 us)
Async XLA Ops:
  0.0 201.4 %copy-start = (bf16[256,256]{1,0:T(8,128)(2,1)S(1)}, bf16[256,256]{1,0:T(8,128)(2,1)}, u32[]{:S(2)}) copy-start(bf16[256,256]{1,0:T(8,128)(2,1)} %param.7) | copy-start | bytes 393220
  0.0 6.7 %copy-start.3 = (f32[1,256]{1,0:T(1,128)S(1)}, f32[1,256]{1,0:T(1,128)}, u32[]{:S(2)}) copy-start(f32[1,256]{1,0:T(1,128)} %param.9) | copy-start | bytes 3076
  3.1 3.7 %collective-permute-start = (bf16[1,256,1,128]{1,3,2,0:T(8,128)(2,1)S(1)}, bf16[1,256,1,128]{1,3,2,0:T(8,128)(2,1)S(1)}, u32[]{:S(2)}, u32[]{:S(2)}) collective-permute-start(bf16[1,256,1,128]{1,3,2,0:T(8,128)(2,1)S(1)} %get-tuple-element.13), channel_id=1, source_target_pairs={{0,1},{1,2},{2,3},{4,5},{5,6},{6,7},{8,9},{9,10},{10,11},{12,13},{... | collective-permute-start | bytes 196616 | tf_op jit(solution)/shard_map/ppermute | solution.py:12
  5.4 5.3 %collective-permute-start.1 = (bf16[1,256,1,128]{1,3,2,0:T(8,128)(2,1)S(1)}, bf16[1,256,1,128]{1,3,2,0:T(8,128)(2,1)S(1)}, u32[]{:S(2)}, u32[]{:S(2)}) collective-permute-start(bf16[1,256,1,128]{1,3,2,0:T(8,128)(2,1)S(1)} %get-tuple-element.14), channel_id=1, source_target_pairs={{1,0},{2,1},{3,2},{5,4},{6,5},{7,6},{9,8},{10,9},{11,10},{13,12},{... | collective-permute-start | bytes 196616 | tf_op jit(solution)/shard_map/ppermute | solution.py:15
  12.8 1.3 copy-start.2
  40.1 99.3 %all-to-all-start = ((f32[1,256,4096]{1,0,2:T(1,128)}), f32[1,256,4096]{1,0,2:T(1,128)}, u32[]{:S(2)}, u32[]{:S(2)}) async-start(f32[1,256,4096]{1,0,2:T(1,128)} %copy.40), calls=%async_computation | async-start | bytes 8388608 | tf_op jit(solution)/shard_map/all_to_all | solution.py:59
  204.1 5.7 %copy-start.1 = (bf16[1,256,32,128]{3,2,1,0:T(8,128)(2,1)S(1)}, bf16[1,256,32,128]{3,2,1,0:T(8,128)(2,1)}, u32[]{:S(2)}) copy-start(bf16[1,256,32,128]{3,2,1,0:T(8,128)(2,1)} %param.5) | copy-start | bytes 6291460
  204.1 5.7 %copy-start.4 = (f32[256]{0:T(256)S(1)}, f32[256]{0:T(256)}, u32[]{:S(2)}) copy-start(f32[256]{0:T(256)} %param.8) | copy-start | bytes 3076
where the time goes:
time: 214 us
  blocking collectives  141 us (66%)
  local copies, waits for them, and re-layouts  33.5 us (16%)
  waiting for transfers between devices  14.8 us (7%)
  starting transfers between devices  9.5 us (4%)
  matrix products  9.45 us (4%)
  other arithmetic  5.11 us (2%)
    all_gather x1, blocking collectives, on_device(): all_rates = lax.all_gather(decays, 'tm', axis=0, tiled=True)  82.5 us
    all_to_all x1, blocking collectives, on_device(): lax.all_to_all(rounded_all, 'tm', split_axis=0, concat_axis=2, tiled=True)  58.8 us
    mul x1, local copies, waits for them, and re-layouts, on_device(): in_gain[:, :, None] * driving.reshape(frame_total_count, states, cell_count)  19.2 us
    all_to_all x1, waiting for transfers between devices, on_device(): lax.all_to_all(scaled_drive, 'tm', split_axis=2, concat_axis=0, tiled=True)  10.9 us
    dot_general x9, matrix products, on_device(): jnp.dot(conv_weight[vertical_shift, col_off], window, preferred_element_t...  6.77 us
    all_to_all x1, starting transfers between devices, on_device(): lax.all_to_all(scaled_drive, 'tm', split_axis=2, concat_axis=0, tiled=True)  5.85 us
    reshape x1, local copies, waits for them, and re-layouts, on_device(): output.reshape(channels, tile_rows, width)  5.67 us
    unnamed x12, local copies, waits for them, and re-layouts  5.52 us
  transfers between devices with their start and end apart: 3, of which 2 were waited for; matrix products, arithmetic and copies ran while one was open for 0% of the time, Pallas kernels for 0%

commit v1 on v0

v1 whole, which is shorter than its diff:
```python
import functools

import jax
import jax.numpy as jnp
from jax import lax
from jax.experimental import pallas as pl
from jax.experimental.pallas import tpu as pltpu
from jax.sharding import PartitionSpec as P

CHUNK = 2
FIRST = 2
MIB = 1 << 20

VMEM = pl.BlockSpec(memory_space=pltpu.VMEM)
ANY = pl.BlockSpec(memory_space=pl.ANY)
SMEM = pl.BlockSpec(memory_space=pltpu.SMEM)


def params(mib):
    return pltpu.CompilerParams(vmem_limit_bytes=mib * MIB)


def conv_kernel(chunks, halo, place, rows_in, *refs):
    refs = list(refs)
    halo_ref = refs.pop(0) if halo else None
    weight, coefs = refs.pop(0), refs.pop(0)
    outs = refs[:chunks]
    rows, shifted, made, sems = refs[chunks:]
    total = rows.shape[0]
    copied = total - 1 if halo else total
    channels, width = rows.shape[1], rows.shape[2]
    main = pltpu.make_async_copy(
        rows_in.at[pl.ds(place[0], copied)], rows.at[pl.ds(place[1], copied)], sems.at[chunks]
    )
    main.start()
    main.wait()
    if halo:
        rows[place[4]] = halo_ref[...]
    lane = lax.broadcasted_iota(jnp.int32, (channels, width), 1)

    def shift(r, _):
        row = rows[r].astype(jnp.float32)
        left = jnp.where(lane == 0, 0.0, pltpu.roll(row, 1, 1))
        right = jnp.where(lane == width - 1, 0.0, pltpu.roll(row, width - 1, 1))
        shifted[r, :channels] = left.astype(jnp.bfloat16)
        shifted[r, channels : 2 * channels] = rows[r]
        shifted[r, 2 * channels :] = right.astype(jnp.bfloat16)
        return _

    lax.fori_loop(0, total, shift, 0, unroll=2)
    gain = coefs[:, 0:1]
    taps = jnp.concatenate([weight[i, j] for i in range(3) for j in range(3)], axis=1)

    def one(k, _):
        r = place[3] + k * place[2]
        window = jnp.concatenate(
            [
                jnp.concatenate([shifted[r + i + q] for q in range(CHUNK)], axis=1)
                for i in range(3)
            ],
            axis=0,
        )
        drive = gain * jnp.dot(taps, window, preferred_element_type=jnp.float32)
        for q in range(CHUNK):
            made[k, q] = drive[:, q * width : (q + 1) * width].astype(made.dtype)
        for n, out in enumerate(outs):

            @pl.when(k == n)
            def start():
                pltpu.make_async_copy(made.at[n], out, sems.at[n]).start()

        return _

    lax.fori_loop(0, chunks, one, 0)
    for n, out in enumerate(outs):
        pltpu.make_async_copy(made.at[n], out, sems.at[n]).wait()


def conv(rows_in, halo, weight, coefs, place, chunks, dtype):
    channels, width = rows_in.shape[1], rows_in.shape[2]
    states = weight.shape[2]
    total = chunks * CHUNK + 2
    shape = (CHUNK, states, width)
    outs = [jax.ShapeDtypeStruct(shape, dtype)] * chunks
    operands = [place, rows_in] + ([halo] if halo is not None else []) + [weight, coefs]
    specs = [SMEM, ANY] + ([VMEM] if halo is not None else []) + [VMEM, VMEM]
    return pl.pallas_call(
        functools.partial(conv_kernel, chunks, halo is not None),
        out_shape=outs,
        in_specs=specs,
        out_specs=[ANY] * chunks,
        scratch_shapes=[
            pltpu.VMEM((total, channels, width), rows_in.dtype),
            pltpu.VMEM((total, 3 * channels, width), rows_in.dtype),
            pltpu.VMEM((chunks,) + shape, dtype),
            pltpu.SemaphoreType.DMA((chunks + 1,)),
        ],
        compiler_params=params(40),
        cost_estimate=pl.CostEstimate(
            flops=2 * 9 * channels * states * width * CHUNK * chunks,
            bytes_accessed=2 * total * channels * width + weight.size * 2,
            transcendentals=0,
        ),
        name="conv_chunks",
    )(*operands)


def pair_kernel(keep, other, coefs, out):
    for q in range(CHUNK):
        out[q] = coefs[:, 2:3] * keep[q] + coefs[:, 3:4] * other[q].astype(jnp.float32)


def pair_drive(keep, other, coefs):
    return pl.pallas_call(
        pair_kernel,
        out_shape=jax.ShapeDtypeStruct(keep.shape, jnp.float32),
        in_specs=[VMEM] * 3,
        out_specs=VMEM,
        compiler_params=params(8),
        name="pair_drive",
    )(keep, other, coefs)


def pick(place, values, q):
    out = values[-1][q]
    for j in range(len(values) - 1):
        out = jnp.where(place[0] == j, values[j][q], out)
    return out.astype(jnp.float32)


def carry_kernel(drives, with_carry, place, coefs, *refs):
    out = refs[-1]
    for q in range(CHUNK):
        total = pick(place, refs[:drives], q)
        if with_carry:
            total = total + coefs[:, 1:2] * refs[drives][q].astype(jnp.float32)
        out[q] = total.astype(jnp.bfloat16)


def carry_on(place, coefs, drives, carry):
    operands = list(drives) + ([carry] if carry is not None else [])
    return pl.pallas_call(
        functools.partial(carry_kernel, len(drives), carry is not None),
        out_shape=jax.ShapeDtypeStruct(drives[0].shape, jnp.bfloat16),
        in_specs=[SMEM, VMEM] + [VMEM] * len(operands),
        out_specs=VMEM,
        compiler_params=params(16),
        name="carry_on",
    )(place, coefs, *operands)


def states_kernel(place, coefs, keep, other, *refs):
    carries, (own, back) = refs[:-2], refs[-2:]
    for q in range(CHUNK):
        held, sent = keep[q], other[q].astype(jnp.float32)
        carry = pick(place, carries, q)
        own[q] = (held + coefs[:, 5:6] * sent + coefs[:, 4:5] * carry).astype(jnp.bfloat16)
        back[q] = (coefs[:, 7:8] * held + sent + coefs[:, 6:7] * carry).astype(jnp.bfloat16)


def states_of(place, coefs, keep, other, carries):
    out = jax.ShapeDtypeStruct(keep.shape, jnp.bfloat16)
    return pl.pallas_call(
        states_kernel,
        out_shape=[out, out],
        in_specs=[SMEM] + [VMEM] * (3 + len(carries)),
        out_specs=[VMEM, VMEM],
        compiler_params=params(16),
        name="states_of",
    )(place, coefs, keep, other, *carries)


def output_kernel(chunks, place, rows_in, weight, skip, *refs):
    states, (out, held, total, sems) = refs[:-4], refs[-4:]
    channels, tile_rows, width = out.shape
    for n, chunk in enumerate(states):
        pltpu.make_async_copy(chunk, held.at[n], sems.at[n]).start()
    for n, chunk in enumerate(states):
        pltpu.make_async_copy(chunk, held.at[n], sems.at[n]).wait()
    gain = skip[:, 0:1]

    def one(n, _):
        second = n // chunks
        k = n - second * chunks
        r = jnp.where(second == 0, place[0] + k * place[1], place[2] + k * place[3])
        value = jnp.dot(
            weight[...],
            jnp.concatenate([held[n, q] for q in range(CHUNK)], axis=1),
            preferred_element_type=jnp.float32,
        )
        for q in range(CHUNK):
            total[pl.ds(r + q, channels, stride=tile_rows), :] = value[
                :, q * width : (q + 1) * width
            ] + gain * rows_in[r + q].astype(jnp.float32)
        return _

    lax.fori_loop(0, 2 * chunks, one, 0)
    block = 16

    def settle(n, _):
        values = total[pl.ds(pl.multiple_of(n * block * tile_rows, 8), block * tile_rows), :]
        out[pl.ds(n * block, block)] = values.reshape(block, tile_rows, width).astype(out.dtype)
        return _

    lax.fori_loop(0, channels // block, settle, 0)


def output_of(place, rows_in, weight, skip, states, chunks, dtype):
    tile_rows, channels, width = rows_in.shape
    return pl.pallas_call(
        functools.partial(output_kernel, chunks),
        out_shape=jax.ShapeDtypeStruct((channels, tile_rows, width), dtype),
        in_specs=[SMEM] + [VMEM] * 3 + [ANY] * len(states),
        out_specs=VMEM,
        scratch_shapes=[
            pltpu.VMEM((len(states),) + states[0].shape, states[0].dtype),
            pltpu.VMEM((channels * tile_rows, width), jnp.float32),
            pltpu.SemaphoreType.DMA((len(states),)),
        ],
        compiler_params=params(40),
        name="output_of",
    )(place, rows_in, weight, skip, *states)


def on_device(frames_in, conv_weight, out_weight, skip_gain, decays):
    tile_rows = frames_in.shape[2]
    frames = lax.axis_size("tm")
    spaces = lax.axis_size("space")
    groups = frames // 2
    me = lax.axis_index("tm")
    group, odd = me // 2, me % 2
    even = odd == 0
    half = tile_rows // 2
    chunks = half // CHUNK
    swap = [(i, i + 1 - 2 * (i % 2)) for i in range(frames)]
    onward = [(i, i + 2) for i in range(frames - 2)]
    down = [(i, i + 1) for i in range(spaces - 1)]
    up = [(i + 1, i) for i in range(spaces - 1)]

    rows = jnp.transpose(frames_in[0], (1, 0, 2))
    own_decay = decays[0]
    other_decay = lax.ppermute(own_decay, "tm", swap)
    from_low = lax.ppermute(rows[tile_rows - 1], "space", down)
    from_high = lax.ppermute(rows[0], "space", up)

    gain = jnp.sqrt(1.0 - own_decay * own_decay)
    decay_even = jnp.where(even, own_decay, other_decay)
    decay_odd = jnp.where(even, other_decay, own_decay)
    later = jnp.where(group > 0, 1.0, 0.0)
    both = decay_even * decay_odd * later
    first = decay_even * later
    one, zero = jnp.ones_like(gain), jnp.zeros_like(gain)
    coefs = jnp.stack(
        [
            gain,
            both,
            jnp.where(even, decay_odd, one),
            jnp.where(even, one, decay_odd),
            jnp.where(even, first, both),
            jnp.where(even, zero, decay_odd),
            jnp.where(even, both, first),
            jnp.where(even, decay_odd, zero),
        ],
        axis=1,
    )
    gains = jnp.stack([gain] * 8, axis=1)

    def place_of(lower, start, count):
        whole = start + count == chunks
        top = jnp.where(lower, half + CHUNK * start, half - CHUNK * (start + count)) - 1
        if whole:
            top = jnp.where(lower, top, 0)
            slot = jnp.where(lower, 0, 1)
        else:
            slot = jnp.zeros((), jnp.int32)
        step = jnp.where(lower, CHUNK, -CHUNK)
        begin = jnp.where(lower, 0, CHUNK * (count - 1))
        halo = jnp.where(lower, CHUNK * count + 1, 0)
        return jnp.stack([top, slot, step, begin, halo]).astype(jnp.int32)

    halo_sent = jnp.where(even, from_high, from_low)
    halo_kept = jnp.where(even, from_low, from_high)
    send = conv(
        rows, None, conv_weight, gains, place_of(even, 0, FIRST), FIRST, jnp.bfloat16
    )
    send += conv(
        rows, halo_sent, conv_weight, gains,
        place_of(even, FIRST, chunks - FIRST), chunks - FIRST, jnp.bfloat16,
    )
    kept = conv(
        rows, halo_kept, conv_weight, gains, place_of(~even, 0, chunks), chunks, jnp.float32
    )
    others = [lax.ppermute(value, "tm", swap) for value in send]

    where = jnp.stack([group, group - 1]).astype(jnp.int32)
    carries, drives, own, back = [], [], [], []
    for step in range(chunks + groups - 1):
        if step < chunks:
            drives.append(pair_drive(kept[step], others[step], coefs))
        if step < chunks + groups - 2:
            ready = [
                drives[min(max(step - g, 0), chunks - 1)] for g in range(groups)
            ]
            sum_out = carry_on(where[:1], coefs, ready, carries[-1] if carries else None)
            carries.append(lax.ppermute(sum_out, "tm", onward))
        k = step - (groups - 1)
        if k >= 0:
            mine, theirs = states_of(
                where[1:], coefs, kept[k], others[k], carries[k : k + groups - 1]
            )
            own.append(mine)
            back.append(lax.ppermute(theirs, "tm", swap))

    place = jnp.where(
        even,
        jnp.array([half - CHUNK, -CHUNK, half, CHUNK], jnp.int32),
        jnp.array([half, CHUNK, half - CHUNK, -CHUNK], jnp.int32),
    )
    skip = jnp.stack([skip_gain] * 8, axis=1)
    result = output_of(place, rows, out_weight, skip, own + back, chunks, frames_in.dtype)
    return result[None]


def solution(mesh):
    placed = (P("tm", None, "space", None), P(), P(), P(), P("tm", None))
    return jax.shard_map(
        on_device,
        mesh=mesh,
        in_specs=placed,
        out_specs=P("tm", None, "space", None),
        check_vma=False,
    )
```

time: 214 us -> 136 us (0.64)
  blocking collectives: 141 us -> 0 us
  starting transfers between devices: 9.5 us -> 69.6 us
  Pallas kernels: 0 us -> 35.4 us
  local copies, waits for them, and re-layouts: 33.5 us -> 10.7 us
  matrix products: 9.45 us -> 0 us
  other arithmetic: 5.11 us -> 0.88 us
  waiting for transfers between devices: 14.8 us -> 18.1 us
    all_gather x1 -> x0, blocking collectives: 82.5 us -> none  [on_device(): all_rates = lax.all_gather(decays, 'tm', axis=0, tiled=True)]
    ppermute x2 -> x29, starting transfers between devices: 3.65 us -> 69.6 us  [the longest x10 42.6 us: on_device(): carries.append(lax.ppermute(sum_out, 'tm', onward))]
    all_to_all x1 -> x0, blocking collectives: 58.8 us -> none  [on_device(): lax.all_to_all(rounded_all, 'tm', split_axis=0, concat_axis=2, tiled=True)]
    pallas_call x0 -> x30, Pallas kernels: none -> 35.4 us  [the longest x3 14.9 us: conv(): pl.pallas_call(functools.partial(conv_kernel, chunks, halo is not None),...]
    mul x1 -> x0, local copies, waits for them, and re-layouts: 19.2 us -> none  [on_device(): in_gain[:, :, None] * driving.reshape(frame_total_count, states, cell_count)]
    ppermute x2 -> x29, waiting for transfers between devices: 3.92 us -> 18.1 us  [the longest x10 12.9 us: on_device(): carries.append(lax.ppermute(sum_out, 'tm', onward))]
    all_to_all x1 -> x0, waiting for transfers between devices: 10.9 us -> none  [on_device(): lax.all_to_all(scaled_drive, 'tm', split_axis=2, concat_axis=0, tiled=True)]
    dot_general x10 -> x0, matrix products: 9.45 us -> none  [the longest x9 6.77 us: on_device(): jnp.dot(conv_weight[vertical_shift, col_off], window, preferred_element_t...]
  transfers between devices with their start and end apart: 3 -> 29, of which waited for: 2 -> 12; matrix products, arithmetic and copies ran while one was open for 0% -> 4% of each run, Pallas kernels for 0% -> 16%
where the time goes in v1:
time: 136 us; the launch traced here: 135 us
  starting transfers between devices  69.6 us (51%)
  Pallas kernels  35.4 us (26%)
  waiting for transfers between devices  18.1 us (13%)
  local copies, waits for them, and re-layouts  10.7 us (8%)
    ppermute x10, starting transfers between devices, on_device(): carries.append(lax.ppermute(sum_out, 'tm', onward))  42.6 us
    pallas_call x3, Pallas kernels, conv(): pl.pallas_call(functools.partial(conv_kernel, chunks, halo is not None),...  14.9 us
    ppermute x10, waiting for transfers between devices, on_device(): carries.append(lax.ppermute(sum_out, 'tm', onward))  12.9 us
    pallas_call x1, Pallas kernels, output_of(): pl.pallas_call(functools.partial(output_kernel, chunks), out_shape=jax.Sh...  11 us
    ppermute x8, starting transfers between devices, on_device(): others = [lax.ppermute(value, 'tm', swap) for value in send]  10.6 us
    ppermute x8, starting transfers between devices, on_device(): back.append(lax.ppermute(theirs, 'tm', swap))  8.5 us
    unnamed x87, local copies, waits for them, and re-layouts  8.22 us
    ppermute x8, waiting for transfers between devices, on_device(): back.append(lax.ppermute(theirs, 'tm', swap))  5.22 us
  transfers between devices with their start and end apart: 29, of which 12 were waited for; matrix products, arithmetic and copies ran while one was open for 4% of the time, Pallas kernels for 16%

profile of v1, /device:TPU:0, one launch (start us, length us, event | category | flops | bytes accessed | tf_op | source)
XLA Modules:
  0.0 135.4 jit_solution(16796064767008011384)
XLA Ops:
  0.0 3.0 %collective-permute-start = (f32[256]{0:T(256)}, f32[256]{0:T(256)S(1)}, u32[]{:S(2)}, u32[]{:S(2)}) collective-permute-start(f32[256]{0:T(256)} %bitcast.47), channel_id=1, source_target_pairs={{0,4},{4,0},{8,12},{12,8},{16,20},{20,16},{24,28},{28,24},{1,5},{5... | collective-permute-start | bytes 3080 | tf_op jit(solution)/shard_map/ppermute | solution.py:242
  3.0 2.4 %copy.46 = bf16[1,256,32,128]{3,1,2,0:T(8,128)(2,1)S(1)} copy(bf16[1,256,32,128]{3,2,1,0:T(8,128)(2,1)} %param.7) | data formatting | bytes 4194304 | tf_op args[0]
  5.4 0.6 slice_bitcast_fusion
  6.0 1.3 collective-permute-start.2
  7.3 3.7 %collective-permute-start.1 = (bf16[256,128]{1,0:T(8,128)(2,1)S(1)}, bf16[256,128]{1,0:T(8,128)(2,1)}, u32[]{:S(2)}, u32[]{:S(2)}) collective-permute-start(bf16[256,128]{1,0:T(8,128)(2,1)S(1)} %get-tuple-element.70), channel_id=1, source_target_pairs={{0,1},{1,2},{2,3},{4,5},{5,6},{6,7},{8,9},{9,10},{10,11},{12,13},{... | collective-permute-start | bytes 196616 | tf_op jit(solution)/shard_map/ppermute | solution.py:243
  11.3 0.6 stack.111
  11.9 0.8 copy.25.coefs
  12.9 2.6 %conv_chunks.4 = (bf16[2,256,128]{2,1,0:T(8,128)(2,1)S(1)}, bf16[2,256,128]{2,1,0:T(8,128)(2,1)S(1)}) custom-call(s32[5]{0:T(128)S(1)} %stack.123.place, bf16[32,256,128]{2,1,0:T(8,128)(2,1)S(1)} %bitcast.36, bf16[3,3,256,256]{3,2,1,0:T(8,128)(2,1)S(1)} %copy-done, f32[256,8]{1,0:T(8,128)S(1)} %stack.118.refs_2_.refs_1_), custom_call_target="tpu_custom_call" | custom-call | flops 603979776 | bytes 1572864 | tf_op jit(solution)/shard_map/conv_chunks/pallas_call | solution.py:87
  15.6 1.9 %collective-permute-start.5 = (bf16[2,256,128]{2,1,0:T(8,128)(2,1)S(1)}, bf16[2,256,128]{2,1,0:T(8,128)(2,1)S(1)}, u32[]{:S(2)}, u32[]{:S(2)}) collective-permute-start(bf16[2,256,128]{2,1,0:T(8,128)(2,1)S(1)} %get-tuple-element.40), channel_id=1, source_target_pairs={{0,4},{4,0},{8,12},{12,8},{16,20},{20,16},{24,28},{28,24},{1,5},{5... | collective-permute-start | bytes 393224 | tf_op jit(solution)/shard_map/ppermute | solution.py:293
  17.5 0.9 broadcast_select_fusion
  18.4 6.5 %conv_chunks.3 = (f32[2,256,128]{2,1,0:T(8,128)S(1)}, f32[2,256,128]{2,1,0:T(8,128)S(1)}, f32[2,256,128]{2,1,0:T(8,128)S(1)}, f32[2,256,128]{2,1,0:T(8,128)S(1)}...) custom-call(s32[5]{0:T(128)S(1)} %stack.117.place, ...), custom_call_target="tpu_custom_call" | custom-call | flops 2415919104 | bytes 2359296 | tf_op jit(solution)/shard_map/conv_chunks/pallas_call | solution.py:87
  25.2 0.9 copy-done.18
  26.1 0.6 copy-done.22
  26.8 3.5 %collective-permute-start.4 = (bf16[2,256,128]{2,1,0:T(8,128)(2,1)S(1)}, bf16[2,256,128]{2,1,0:T(8,128)(2,1)S(1)}, u32[]{:S(2)}, u32[]{:S(2)}) collective-permute-start(bf16[2,256,128]{2,1,0:T(8,128)(2,1)S(1)} %carry_on.10), channel_id=1, source_target_pairs={{0,8},{4,12},{8,16},{12,20},{16,24},{20,28},{1,9},{5,13},{9,17},{1... | collective-permute-start | bytes 393224 | tf_op jit(solution)/shard_map/ppermute | solution.py:305
  30.3 5.9 %conv_chunks.5 = (bf16[2,256,128]{2,1,0:T(8,128)(2,1)S(1)}, bf16[2,256,128]{2,1,0:T(8,128)(2,1)S(1)}, bf16[2,256,128]{2,1,0:T(8,128)(2,1)S(1)}, bf16[2,256,128]{...) custom-call(s32[5]{0:T(128)S(1)} %stack.129.place, ...), custom_call_target="tpu_custom_call" | custom-call | flops 1811939328 | bytes 2097152 | tf_op jit(solution)/shard_map/conv_chunks/pallas_call | solution.py:87
  36.2 0.6 collective-permute-start.7
  37.1 3.5 %collective-permute-start.6 = (bf16[2,256,128]{2,1,0:T(8,128)(2,1)S(1)}, bf16[2,256,128]{2,1,0:T(8,128)(2,1)S(1)}, u32[]{:S(2)}, u32[]{:S(2)}) collective-permute-start(bf16[2,256,128]{2,1,0:T(8,128)(2,1)S(1)} %carry_on.11), channel_id=1, source_target_pairs={{0,8},{4,12},{8,16},{12,20},{16,24},{20,28},{1,9},{5,13},{9,17},{1... | collective-permute-start | bytes 393224 | tf_op jit(solution)/shard_map/ppermute | solution.py:305
  40.6 1.6 %collective-permute-start.9 = (bf16[2,256,128]{2,1,0:T(8,128)(2,1)S(1)}, bf16[2,256,128]{2,1,0:T(8,128)(2,1)S(1)}, u32[]{:S(2)}, u32[]{:S(2)}) collective-permute-start(bf16[2,256,128]{2,1,0:T(8,128)(2,1)S(1)} %get-tuple-element.45), channel_id=1, source_target_pairs={{0,4},{4,0},{8,12},{12,8},{16,20},{20,16},{24,28},{28,24},{1,5},{5... | collective-permute-start | bytes 393224 | tf_op jit(solution)/shard_map/ppermute | solution.py:293
  42.5 0.7 collective-permute-done.6.refs_4_.refs_1_.refs_0_
  43.3 4.4 %collective-permute-start.8 = (bf16[2,256,128]{2,1,0:T(8,128)(2,1)S(1)}, bf16[2,256,128]{2,1,0:T(8,128)(2,1)S(1)}, u32[]{:S(2)}, u32[]{:S(2)}) collective-permute-start(bf16[2,256,128]{2,1,0:T(8,128)(2,1)S(1)} %carry_on.12), channel_id=1, source_target_pairs={{0,8},{4,12},{8,16},{12,20},{16,24},{20,28},{1,9},{5,13},{9,17},{1... | collective-permute-start | bytes 393224 | tf_op jit(solution)/shard_map/ppermute | solution.py:305
  47.7 1.6 %collective-permute-start.11 = (bf16[2,256,128]{2,1,0:T(8,128)(2,1)S(1)}, bf16[2,256,128]{2,1,0:T(8,128)(2,1)S(1)}, u32[]{:S(2)}, u32[]{:S(2)}) collective-permute-start(bf16[2,256,128]{2,1,0:T(8,128)(2,1)S(1)} %get-tuple-element.48), channel_id=1, source_target_pairs={{0,4},{4,0},{8,12},{12,8},{16,20},{20,16},{24,28},{28,24},{1,5},{5... | collective-permute-start | bytes 393224 | tf_op jit(solution)/shard_map/ppermute | solution.py:293
  49.5 0.7 collective-permute-done.8.refs_2_.refs_4_.refs_1_.refs_0_
  50.3 4.4 %collective-permute-start.10 = (bf16[2,256,128]{2,1,0:T(8,128)(2,1)S(1)}, bf16[2,256,128]{2,1,0:T(8,128)(2,1)S(1)}, u32[]{:S(2)}, u32[]{:S(2)}) collective-permute-start(bf16[2,256,128]{2,1,0:T(8,128)(2,1)S(1)} %carry_on.13), channel_id=1, source_target_pairs={{0,8},{4,12},{8,16},{12,20},{16,24},{20,28},{1,9},{5,13},{9,17},{1... | collective-permute-start | bytes 393224 | tf_op jit(solution)/shard_map/ppermute | solution.py:305
  54.7 1.6 %collective-permute-start.13 = (bf16[2,256,128]{2,1,0:T(8,128)(2,1)S(1)}, bf16[2,256,128]{2,1,0:T(8,128)(2,1)S(1)}, u32[]{:S(2)}, u32[]{:S(2)}) collective-permute-start(bf16[2,256,128]{2,1,0:T(8,128)(2,1)S(1)} %get-tuple-element.51), channel_id=1, source_target_pairs={{0,4},{4,0},{8,12},{12,8},{16,20},{20,16},{24,28},{28,24},{1,5},{5... | collective-permute-start | bytes 393224 | tf_op jit(solution)/shard_map/ppermute | solution.py:293
  56.5 0.4 copy-done.28
  57.3 4.4 %collective-permute-start.12 = (bf16[2,256,128]{2,1,0:T(8,128)(2,1)S(1)}, bf16[2,256,128]{2,1,0:T(8,128)(2,1)S(1)}, u32[]{:S(2)}, u32[]{:S(2)}) collective-permute-start(bf16[2,256,128]{2,1,0:T(8,128)(2,1)S(1)} %carry_on.14), channel_id=1, source_target_pairs={{0,8},{4,12},{8,16},{12,20},{16,24},{20,28},{1,9},{5,13},{9,17},{1... | collective-permute-start | bytes 393224 | tf_op jit(solution)/shard_map/ppermute | solution.py:305
  61.7 1.6 %collective-permute-start.15 = (bf16[2,256,128]{2,1,0:T(8,128)(2,1)S(1)}, bf16[2,256,128]{2,1,0:T(8,128)(2,1)S(1)}, u32[]{:S(2)}, u32[]{:S(2)}) collective-permute-start(bf16[2,256,128]{2,1,0:T(8,128)(2,1)S(1)} %get-tuple-element.54), channel_id=1, source_target_pairs={{0,4},{4,0},{8,12},{12,8},{16,20},{20,16},{24,28},{28,24},{1,5},{5... | collective-permute-start | bytes 393224 | tf_op jit(solution)/shard_map/ppermute | solution.py:293
  63.5 1.2 collective-permute-done.12.refs_2_.refs_4_.refs_1_.refs_0_
  64.8 4.4 %collective-permute-start.14 = (bf16[2,256,128]{2,1,0:T(8,128)(2,1)S(1)}, bf16[2,256,128]{2,1,0:T(8,128)(2,1)S(1)}, u32[]{:S(2)}, u32[]{:S(2)}) collective-permute-start(bf16[2,256,128]{2,1,0:T(8,128)(2,1)S(1)} %carry_on.15), channel_id=1, source_target_pairs={{0,8},{4,12},{8,16},{12,20},{16,24},{20,28},{1,9},{5,13},{9,17},{1... | collective-permute-start | bytes 393224 | tf_op jit(solution)/shard_map/ppermute | solution.py:305
  69.2 1.6 %collective-permute-start.17 = (bf16[2,256,128]{2,1,0:T(8,128)(2,1)S(1)}, bf16[2,256,128]{2,1,0:T(8,128)(2,1)S(1)}, u32[]{:S(2)}, u32[]{:S(2)}) collective-permute-start(bf16[2,256,128]{2,1,0:T(8,128)(2,1)S(1)} %get-tuple-element.57), channel_id=1, source_target_pairs={{0,4},{4,0},{8,12},{12,8},{16,20},{20,16},{24,28},{28,24},{1,5},{5... | collective-permute-start | bytes 393224 | tf_op jit(solution)/shard_map/ppermute | solution.py:293
  71.1 2.0 %collective-permute-done.14.refs_2_.refs_4_.refs_1_.refs_0_ = bf16[2,256,128]{2,1,0:T(8,128)(2,1)S(1)} collective-permute-done((bf16[2,256,128]{2,1,0:T(8,128)(2,1)S(1)}, bf16[2,256,128]{2,1,0:T(8,128)(2,1)S(1)}, u32[]{:S(2)}, u32[]{:S(2)}) %collective-permute-start.14) | collective-permute-done | bytes 131104 | tf_op jit(solution)/shard_map/ppermute | solution.py:305
  73.3 4.4 %collective-permute-start.16 = (bf16[2,256,128]{2,1,0:T(8,128)(2,1)S(1)}, bf16[2,256,128]{2,1,0:T(8,128)(2,1)S(1)}, u32[]{:S(2)}, u32[]{:S(2)}) collective-permute-start(bf16[2,256,128]{2,1,0:T(8,128)(2,1)S(1)} %carry_on.16), channel_id=1, source_target_pairs={{0,8},{4,12},{8,16},{12,20},{16,24},{20,28},{1,9},{5,13},{9,17},{1... | collective-permute-start | bytes 393224 | tf_op jit(solution)/shard_map/ppermute | solution.py:305
  77.9 2.8 %collective-permute-done.16.refs_2_.refs_4_.refs_1_.refs_0_ = bf16[2,256,128]{2,1,0:T(8,128)(2,1)S(1)} collective-permute-done((bf16[2,256,128]{2,1,0:T(8,128)(2,1)S(1)}, bf16[2,256,128]{2,1,0:T(8,128)(2,1)S(1)}, u32[]{:S(2)}, u32[]{:S(2)}) %collective-permute-start.16) | collective-permute-done | bytes 131104 | tf_op jit(solution)/shard_map/ppermute | solution.py:305
  80.9 4.4 %collective-permute-start.18 = (bf16[2,256,128]{2,1,0:T(8,128)(2,1)S(1)}, bf16[2,256,128]{2,1,0:T(8,128)(2,1)S(1)}, u32[]{:S(2)}, u32[]{:S(2)}) collective-permute-start(bf16[2,256,128]{2,1,0:T(8,128)(2,1)S(1)} %carry_on.17), channel_id=1, source_target_pairs={{0,8},{4,12},{8,16},{12,20},{16,24},{20,28},{1,9},{5,13},{9,17},{1... | collective-permute-start | bytes 393224 | tf_op jit(solution)/shard_map/ppermute | solution.py:305
  85.3 3.0 %collective-permute-done.18.refs_2_.refs_4_.refs_1_.refs_0_ = bf16[2,256,128]{2,1,0:T(8,128)(2,1)S(1)} collective-permute-done((bf16[2,256,128]{2,1,0:T(8,128)(2,1)S(1)}, bf16[2,256,128]{2,1,0:T(8,128)(2,1)S(1)}, u32[]{:S(2)}, u32[]{:S(2)}) %collective-permute-start.18) | collective-permute-done | bytes 131104 | tf_op jit(solution)/shard_map/ppermute | solution.py:305
  88.3 0.8 carry_on.18
  89.1 5.0 %collective-permute-start.19 = (bf16[2,256,128]{2,1,0:T(8,128)(2,1)}, bf16[2,256,128]{2,1,0:T(8,128)(2,1)}, u32[]{:S(2)}, u32[]{:S(2)}) collective-permute-start(bf16[2,256,128]{2,1,0:T(8,128)(2,1)} %carry_on.18), channel_id=1, source_target_pairs={{0,8},{4,12},{8,16},{12,20},{16,24},{20,28},{1,9},{5,13},{9,17},{1... | collective-permute-start | bytes 393224 | tf_op jit(solution)/shard_map/ppermute | solution.py:305
  94.2 2.2 %collective-permute-done.19.refs_2_.refs_4_.refs_1_ = bf16[2,256,128]{2,1,0:T(8,128)(2,1)} collective-permute-done((bf16[2,256,128]{2,1,0:T(8,128)(2,1)}, bf16[2,256,128]{2,1,0:T(8,128)(2,1)}, u32[]{:S(2)}, u32[]{:S(2)}) %collective-permute-start.19) | collective-permute-done | bytes 131104 | tf_op jit(solution)/shard_map/ppermute | solution.py:305
  96.3 1.1 carry_on.19
  97.4 4.4 %collective-permute-start.20 = (bf16[2,256,128]{2,1,0:T(8,128)(2,1)S(1)}, bf16[2,256,128]{2,1,0:T(8,128)(2,1)S(1)}, u32[]{:S(2)}, u32[]{:S(2)}) collective-permute-start(bf16[2,256,128]{2,1,0:T(8,128)(2,1)S(1)} %carry_on.19), channel_id=1, source_target_pairs={{0,8},{4,12},{8,16},{12,20},{16,24},{20,28},{1,9},{5,13},{9,17},{1... | collective-permute-start | bytes 393224 | tf_op jit(solution)/shard_map/ppermute | solution.py:305
  101.8 0.9 copy-done.2
  102.7 0.9 copy-done.19
  103.6 0.9 copy-done.23
  104.5 0.9 copy-done.37
  105.8 1.6 %collective-permute-start.21 = (bf16[2,256,128]{2,1,0:T(8,128)(2,1)S(1)}, bf16[2,256,128]{2,1,0:T(8,128)(2,1)S(1)}, u32[]{:S(2)}, u32[]{:S(2)}) collective-permute-start(bf16[2,256,128]{2,1,0:T(8,128)(2,1)S(1)} %get-tuple-element.61), channel_id=1, source_target_pairs={{0,4},{4,0},{8,12},{12,8},{16,20},{20,16},{24,28},{28,24},{1,5},{5... | collective-permute-start | bytes 393224 | tf_op jit(solution)/shard_map/ppermute | solution.py:312
  107.4 0.4 states_of.9
  107.8 0.6 collective-permute-start.22
  108.4 0.4 states_of.10
  108.9 1.6 %collective-permute-start.23 = (bf16[2,256,128]{2,1,0:T(8,128)(2,1)S(1)}, bf16[2,256,128]{2,1,0:T(8,128)(2,1)S(1)}, u32[]{:S(2)}, u32[]{:S(2)}) collective-permute-start(bf16[2,256,128]{2,1,0:T(8,128)(2,1)S(1)} %get-tuple-element.63), channel_id=1, source_target_pairs={{0,4},{4,0},{8,12},{12,8},{16,20},{20,16},{24,28},{28,24},{1,5},{5... | collective-permute-start | bytes 393224 | tf_op jit(solution)/shard_map/ppermute | solution.py:312
  110.4 0.4 states_of.11
  110.8 0.6 collective-permute-start.24
  111.4 0.4 states_of.12
  111.8 0.4 states_of.13
  112.3 1.3 states_of.14
  113.5 1.6 %collective-permute-start.25 = (bf16[2,256,128]{2,1,0:T(8,128)(2,1)S(1)}, bf16[2,256,128]{2,1,0:T(8,128)(2,1)S(1)}, u32[]{:S(2)}, u32[]{:S(2)}) collective-permute-start(bf16[2,256,128]{2,1,0:T(8,128)(2,1)S(1)} %get-tuple-element.65), channel_id=1, source_target_pairs={{0,4},{4,0},{8,12},{12,8},{16,20},{20,16},{24,28},{28,24},{1,5},{5... | collective-permute-start | bytes 393224 | tf_op jit(solution)/shard_map/ppermute | solution.py:312
  115.1 1.3 states_of.15
  116.4 0.6 collective-permute-start.26
  117.0 1.5 %collective-permute-start.27 = (bf16[2,256,128]{2,1,0:T(8,128)(2,1)S(1)}, bf16[2,256,128]{2,1,0:T(8,128)(2,1)S(1)}, u32[]{:S(2)}, u32[]{:S(2)}) collective-permute-start(bf16[2,256,128]{2,1,0:T(8,128)(2,1)S(1)} %get-tuple-element.67), channel_id=1, source_target_pairs={{0,4},{4,0},{8,12},{12,8},{16,20},{20,16},{24,28},{28,24},{1,5},{5... | collective-permute-start | bytes 393224 | tf_op jit(solution)/shard_map/ppermute | solution.py:312
  118.5 0.5 collective-permute-start.28
  119.1 0.9 collective-permute-done.25.refs_12_
  120.0 1.5 %collective-permute-done.26.refs_13_ = bf16[2,256,128]{2,1,0:T(8,128)(2,1)S(1)} collective-permute-done((bf16[2,256,128]{2,1,0:T(8,128)(2,1)S(1)}, bf16[2,256,128]{2,1,0:T(8,128)(2,1)S(1)}, u32[]{:S(2)}, u32[]{:S(2)}) %collective-permute-start.26) | collective-permute-done | bytes 131104 | tf_op jit(solution)/shard_map/ppermute | solution.py:312
  121.4 1.4 %collective-permute-done.27.refs_14_ = bf16[2,256,128]{2,1,0:T(8,128)(2,1)S(1)} collective-permute-done((bf16[2,256,128]{2,1,0:T(8,128)(2,1)S(1)}, bf16[2,256,128]{2,1,0:T(8,128)(2,1)S(1)}, u32[]{:S(2)}, u32[]{:S(2)}) %collective-permute-start.27) | collective-permute-done | bytes 131104 | tf_op jit(solution)/shard_map/ppermute | solution.py:312
  122.9 1.4 %collective-permute-done.28.refs_15_ = bf16[2,256,128]{2,1,0:T(8,128)(2,1)S(1)} collective-permute-done((bf16[2,256,128]{2,1,0:T(8,128)(2,1)S(1)}, bf16[2,256,128]{2,1,0:T(8,128)(2,1)S(1)}, u32[]{:S(2)}, u32[]{:S(2)}) %collective-permute-start.28) | collective-permute-done | bytes 131104 | tf_op jit(solution)/shard_map/ppermute | solution.py:312
  124.4 11.0 %output_of.1 = bf16[256,32,128]{2,1,0:T(8,128)(2,1)} custom-call(s32[4]{0:T(128)S(1)} %broadcast_select_fusion.10.place, bf16[32,256,128]{2,1,0:T(8,128)(2,1)S(1)} %bitcast.39, bf16[256,256]{1,0:T(8,128)(2,1)S(1)} %copy-done.38, f32[256,8]{1,0:T(8,128)S(1)} %stack.102.skip, bf16[2,256,128]{2,1,0:T(8,128)(2,1)S(1)} %get-tuple-element.43.refs_0_, ...), custom_call_target="tpu_custom_call" | custom-call | tf_op jit(solution)/shard_map/output_of/pallas_call | solution.py:210
  (123 shorter events, 4.2 us)
Async XLA Ops:
  0.0 11.0 %copy-start.39 = (f32[1,256]{1,0:T(1,128)S(1)}, f32[1,256]{1,0:T(1,128)}, u32[]{:S(2)}) copy-start(f32[1,256]{1,0:T(1,128)} %param.11) | copy-start | bytes 3076
  0.0 12.8 %copy-start = (bf16[3,3,256,256]{3,2,1,0:T(8,128)(2,1)S(1)}, bf16[3,3,256,256]{3,2,1,0:T(8,128)(2,1)}, u32[]{:S(2)}) copy-start(bf16[3,3,256,256]{3,2,1,0:T(8,128)(2,1)} %refs_1_.3) | copy-start | bytes 3538948
  0.0 11.3 %collective-permute-start = (f32[256]{0:T(256)}, f32[256]{0:T(256)S(1)}, u32[]{:S(2)}, u32[]{:S(2)}) collective-permute-start(f32[256]{0:T(256)} %bitcast.47), channel_id=1, source_target_pairs={{0,4},{4,0},{8,12},{12,8},{16,20},{20,16},{24,28},{28,24},{1,5},{5... | collective-permute-start | bytes 3080 | tf_op jit(solution)/shard_map/ppermute | solution.py:242
  6.0 11.5 %collective-permute-start.2 = (bf16[256,128]{1,0:T(8,128)(2,1)}, bf16[256,128]{1,0:T(8,128)(2,1)S(1)}, u32[]{:S(2)}, u32[]{:S(2)}) collective-permute-start(bf16[256,128]{1,0:T(8,128)(2,1)} %get-tuple-element.69), channel_id=1, source_target_pairs={{1,0},{2,1},{3,2},{5,4},{6,5},{7,6},{9,8},{10,9},{11,10},{13,12},{... | collective-permute-start | bytes 196616 | tf_op jit(solution)/shard_map/ppermute | solution.py:244
  7.3 10.2 %collective-permute-start.1 = (bf16[256,128]{1,0:T(8,128)(2,1)S(1)}, bf16[256,128]{1,0:T(8,128)(2,1)}, u32[]{:S(2)}, u32[]{:S(2)}) collective-permute-start(bf16[256,128]{1,0:T(8,128)(2,1)S(1)} %get-tuple-element.70), channel_id=1, source_target_pairs={{0,1},{1,2},{2,3},{4,5},{5,6},{6,7},{8,9},{9,10},{10,11},{12,13},{... | collective-permute-start | bytes 196616 | tf_op jit(solution)/shard_map/ppermute | solution.py:243
  15.4 9.5 %collective-permute-start.3 = (bf16[2,256,128]{2,1,0:T(8,128)(2,1)S(1)}, bf16[2,256,128]{2,1,0:T(8,128)(2,1)S(1)}, u32[]{:S(2)}, u32[]{:S(2)}) collective-permute-start(bf16[2,256,128]{2,1,0:T(8,128)(2,1)S(1)} %get-tuple-element.38), channel_id=1, source_target_pairs={{0,4},{4,0},{8,12},{12,8},{16,20},{20,16},{24,28},{28,24},{1,5},{5... | collective-permute-start | bytes 393224 | tf_op jit(solution)/shard_map/ppermute | solution.py:293
  15.6 21.2 %collective-permute-start.5 = (bf16[2,256,128]{2,1,0:T(8,128)(2,1)S(1)}, bf16[2,256,128]{2,1,0:T(8,128)(2,1)S(1)}, u32[]{:S(2)}, u32[]{:S(2)}) collective-permute-start(bf16[2,256,128]{2,1,0:T(8,128)(2,1)S(1)} %get-tuple-element.40), channel_id=1, source_target_pairs={{0,4},{4,0},{8,12},{12,8},{16,20},{20,16},{24,28},{28,24},{1,5},{5... | collective-permute-start | bytes 393224 | tf_op jit(solution)/shard_map/ppermute | solution.py:293
  24.9 11.9 %copy-start.16 = (f32[2,256,128]{2,1,0:T(8,128)}, f32[2,256,128]{2,1,0:T(8,128)S(1)}, u32[]{:S(2)}) copy-start(f32[2,256,128]{2,1,0:T(8,128)S(1)} %get-tuple-element.39.keep) | copy-start | bytes 786436
  24.9 17.4 %copy-start.14 = (f32[2,256,128]{2,1,0:T(8,128)}, f32[2,256,128]{2,1,0:T(8,128)S(1)}, u32[]{:S(2)}) copy-start(f32[2,256,128]{2,1,0:T(8,128)S(1)} %get-tuple-element.41.keep) | copy-start | bytes 786436
  24.9 24.4 %copy-start.12 = (f32[2,256,128]{2,1,0:T(8,128)}, f32[2,256,128]{2,1,0:T(8,128)S(1)}, u32[]{:S(2)}) copy-start(f32[2,256,128]{2,1,0:T(8,128)S(1)} %get-tuple-element.44.keep) | copy-start | bytes 786436
  24.9 31.4 %copy-start.10 = (f32[2,256,128]{2,1,0:T(8,128)}, f32[2,256,128]{2,1,0:T(8,128)S(1)}, u32[]{:S(2)}) copy-start(f32[2,256,128]{2,1,0:T(8,128)S(1)} %get-tuple-element.47.keep) | copy-start | bytes 786436
  24.9 38.4 %copy-start.8 = (f32[2,256,128]{2,1,0:T(8,128)}, f32[2,256,128]{2,1,0:T(8,128)S(1)}, u32[]{:S(2)}) copy-start(f32[2,256,128]{2,1,0:T(8,128)S(1)} %get-tuple-element.50.keep) | copy-start | bytes 786436
  24.9 45.9 %copy-start.6 = (f32[2,256,128]{2,1,0:T(8,128)}, f32[2,256,128]{2,1,0:T(8,128)S(1)}, u32[]{:S(2)}) copy-start(f32[2,256,128]{2,1,0:T(8,128)S(1)} %get-tuple-element.53.keep) | copy-start | bytes 786436
  24.9 52.8 %copy-start.4 = (f32[2,256,128]{2,1,0:T(8,128)}, f32[2,256,128]{2,1,0:T(8,128)S(1)}, u32[]{:S(2)}) copy-start(f32[2,256,128]{2,1,0:T(8,128)S(1)} %get-tuple-element.56.keep) | copy-start | bytes 786436
  26.8 10.2 %collective-permute-start.4 = (bf16[2,256,128]{2,1,0:T(8,128)(2,1)S(1)}, bf16[2,256,128]{2,1,0:T(8,128)(2,1)S(1)}, u32[]{:S(2)}, u32[]{:S(2)}) collective-permute-start(bf16[2,256,128]{2,1,0:T(8,128)(2,1)S(1)} %carry_on.10), channel_id=1, source_target_pairs={{0,8},{4,12},{8,16},{12,20},{16,24},{20,28},{1,9},{5,13},{9,17},{1... | collective-permute-start | bytes 393224 | tf_op jit(solution)/shard_map/ppermute | solution.py:305
  36.2 6.0 %collective-permute-start.7 = (bf16[2,256,128]{2,1,0:T(8,128)(2,1)S(1)}, bf16[2,256,128]{2,1,0:T(8,128)(2,1)S(1)}, u32[]{:S(2)}, u32[]{:S(2)}) collective-permute-start(bf16[2,256,128]{2,1,0:T(8,128)(2,1)S(1)} %get-tuple-element.42), channel_id=1, source_target_pairs={{0,4},{4,0},{8,12},{12,8},{16,20},{20,16},{24,28},{28,24},{1,5},{5... | collective-permute-start | bytes 393224 | tf_op jit(solution)/shard_map/ppermute | solution.py:293
  36.8 6.5 %copy-start.20 = (bf16[2,256,128]{2,1,0:T(8,128)(2,1)}, bf16[2,256,128]{2,1,0:T(8,128)(2,1)S(1)}, u32[]{:S(2)}) copy-start(bf16[2,256,128]{2,1,0:T(8,128)(2,1)S(1)} %collective-permute-done.5.other) | copy-start | bytes 393220
  37.0 5.2 %copy-start.36 = (bf16[2,256,128]{2,1,0:T(8,128)(2,1)}, bf16[2,256,128]{2,1,0:T(8,128)(2,1)S(1)}, u32[]{:S(2)}) copy-start(bf16[2,256,128]{2,1,0:T(8,128)(2,1)S(1)} %collective-permute-done.4.refs_4_.refs_0_) | copy-start | bytes 393220
  37.1 6.0 %collective-permute-start.6 = (bf16[2,256,128]{2,1,0:T(8,128)(2,1)S(1)}, bf16[2,256,128]{2,1,0:T(8,128)(2,1)S(1)}, u32[]{:S(2)}, u32[]{:S(2)}) collective-permute-start(bf16[2,256,128]{2,1,0:T(8,128)(2,1)S(1)} %carry_on.11), channel_id=1, source_target_pairs={{0,8},{4,12},{8,16},{12,20},{16,24},{20,28},{1,9},{5,13},{9,17},{1... | collective-permute-start | bytes 393224 | tf_op jit(solution)/shard_map/ppermute | solution.py:305
  40.6 8.6 %collective-permute-start.9 = (bf16[2,256,128]{2,1,0:T(8,128)(2,1)S(1)}, bf16[2,256,128]{2,1,0:T(8,128)(2,1)S(1)}, u32[]{:S(2)}, u32[]{:S(2)}) collective-permute-start(bf16[2,256,128]{2,1,0:T(8,128)(2,1)S(1)} %get-tuple-element.45), channel_id=1, source_target_pairs={{0,4},{4,0},{8,12},{12,8},{16,20},{20,16},{24,28},{28,24},{1,5},{5... | collective-permute-start | bytes 393224 | tf_op jit(solution)/shard_map/ppermute | solution.py:293
  42.2 8.1 %copy-start.24 = (bf16[2,256,128]{2,1,0:T(8,128)(2,1)}, bf16[2,256,128]{2,1,0:T(8,128)(2,1)S(1)}, u32[]{:S(2)}) copy-start(bf16[2,256,128]{2,1,0:T(8,128)(2,1)S(1)} %collective-permute-done.7.other) | copy-start | bytes 393220
  43.1 6.1 %copy-start.1 = (bf16[2,256,128]{2,1,0:T(8,128)(2,1)}, bf16[2,256,128]{2,1,0:T(8,128)(2,1)S(1)}, u32[]{:S(2)}) copy-start(bf16[2,256,128]{2,1,0:T(8,128)(2,1)S(1)} %collective-permute-done.6.refs_4_.refs_1_.refs_0_) | copy-start | bytes 393220
  43.3 6.9 %collective-permute-start.8 = (bf16[2,256,128]{2,1,0:T(8,128)(2,1)S(1)}, bf16[2,256,128]{2,1,0:T(8,128)(2,1)S(1)}, u32[]{:S(2)}, u32[]{:S(2)}) collective-permute-start(bf16[2,256,128]{2,1,0:T(8,128)(2,1)S(1)} %carry_on.12), channel_id=1, source_target_pairs={{0,8},{4,12},{8,16},{12,20},{16,24},{20,28},{1,9},{5,13},{9,17},{1... | collective-permute-start | bytes 393224 | tf_op jit(solution)/shard_map/ppermute | solution.py:305
  47.7 8.6 %collective-permute-start.11 = (bf16[2,256,128]{2,1,0:T(8,128)(2,1)S(1)}, bf16[2,256,128]{2,1,0:T(8,128)(2,1)S(1)}, u32[]{:S(2)}, u32[]{:S(2)}) collective-permute-start(bf16[2,256,128]{2,1,0:T(8,128)(2,1)S(1)} %get-tuple-element.48), channel_id=1, source_target_pairs={{0,4},{4,0},{8,12},{12,8},{16,20},{20,16},{24,28},{28,24},{1,5},{5... | collective-permute-start | bytes 393224 | tf_op jit(solution)/shard_map/ppermute | solution.py:293
  49.2 8.1 %copy-start.26 = (bf16[2,256,128]{2,1,0:T(8,128)(2,1)}, bf16[2,256,128]{2,1,0:T(8,128)(2,1)S(1)}, u32[]{:S(2)}) copy-start(bf16[2,256,128]{2,1,0:T(8,128)(2,1)S(1)} %collective-permute-done.9.other) | copy-start | bytes 393220
  50.3 6.9 %collective-permute-start.10 = (bf16[2,256,128]{2,1,0:T(8,128)(2,1)S(1)}, bf16[2,256,128]{2,1,0:T(8,128)(2,1)S(1)}, u32[]{:S(2)}, u32[]{:S(2)}) collective-permute-start(bf16[2,256,128]{2,1,0:T(8,128)(2,1)S(1)} %carry_on.13), channel_id=1, source_target_pairs={{0,8},{4,12},{8,16},{12,20},{16,24},{20,28},{1,9},{5,13},{9,17},{1... | collective-permute-start | bytes 393224 | tf_op jit(solution)/shard_map/ppermute | solution.py:305
  54.7 8.6 %collective-permute-start.13 = (bf16[2,256,128]{2,1,0:T(8,128)(2,1)S(1)}, bf16[2,256,128]{2,1,0:T(8,128)(2,1)S(1)}, u32[]{:S(2)}, u32[]{:S(2)}) collective-permute-start(bf16[2,256,128]{2,1,0:T(8,128)(2,1)S(1)} %get-tuple-element.51), channel_id=1, source_target_pairs={{0,4},{4,0},{8,12},{12,8},{16,20},{20,16},{24,28},{28,24},{1,5},{5... | collective-permute-start | bytes 393224 | tf_op jit(solution)/shard_map/ppermute | solution.py:293
  57.3 7.4 %collective-permute-start.12 = (bf16[2,256,128]{2,1,0:T(8,128)(2,1)S(1)}, bf16[2,256,128]{2,1,0:T(8,128)(2,1)S(1)}, u32[]{:S(2)}, u32[]{:S(2)}) collective-permute-start(bf16[2,256,128]{2,1,0:T(8,128)(2,1)S(1)} %carry_on.14), channel_id=1, source_target_pairs={{0,8},{4,12},{8,16},{12,20},{16,24},{20,28},{1,9},{5,13},{9,17},{1... | collective-permute-start | bytes 393224 | tf_op jit(solution)/shard_map/ppermute | solution.py:305
  61.7 9.2 %collective-permute-start.15 = (bf16[2,256,128]{2,1,0:T(8,128)(2,1)S(1)}, bf16[2,256,128]{2,1,0:T(8,128)(2,1)S(1)}, u32[]{:S(2)}, u32[]{:S(2)}) collective-permute-start(bf16[2,256,128]{2,1,0:T(8,128)(2,1)S(1)} %get-tuple-element.54), channel_id=1, source_target_pairs={{0,4},{4,0},{8,12},{12,8},{16,20},{20,16},{24,28},{28,24},{1,5},{5... | collective-permute-start | bytes 393224 | tf_op jit(solution)/shard_map/ppermute | solution.py:293
  63.3 10.0 %copy-start.30 = (bf16[2,256,128]{2,1,0:T(8,128)(2,1)}, bf16[2,256,128]{2,1,0:T(8,128)(2,1)S(1)}, u32[]{:S(2)}) copy-start(bf16[2,256,128]{2,1,0:T(8,128)(2,1)S(1)} %collective-permute-done.13.other) | copy-start | bytes 393220
  64.8 8.2 %collective-permute-start.14 = (bf16[2,256,128]{2,1,0:T(8,128)(2,1)S(1)}, bf16[2,256,128]{2,1,0:T(8,128)(2,1)S(1)}, u32[]{:S(2)}, u32[]{:S(2)}) collective-permute-start(bf16[2,256,128]{2,1,0:T(8,128)(2,1)S(1)} %carry_on.15), channel_id=1, source_target_pairs={{0,8},{4,12},{8,16},{12,20},{16,24},{20,28},{1,9},{5,13},{9,17},{1... | collective-permute-start | bytes 393224 | tf_op jit(solution)/shard_map/ppermute | solution.py:305
  69.2 8.4 %collective-permute-start.17 = (bf16[2,256,128]{2,1,0:T(8,128)(2,1)S(1)}, bf16[2,256,128]{2,1,0:T(8,128)(2,1)S(1)}, u32[]{:S(2)}, u32[]{:S(2)}) collective-permute-start(bf16[2,256,128]{2,1,0:T(8,128)(2,1)S(1)} %get-tuple-element.57), channel_id=1, source_target_pairs={{0,4},{4,0},{8,12},{12,8},{16,20},{20,16},{24,28},{28,24},{1,5},{5... | collective-permute-start | bytes 393224 | tf_op jit(solution)/shard_map/ppermute | solution.py:293
  70.8 10.0 %copy-start.32 = (bf16[2,256,128]{2,1,0:T(8,128)(2,1)}, bf16[2,256,128]{2,1,0:T(8,128)(2,1)S(1)}, u32[]{:S(2)}) copy-start(bf16[2,256,128]{2,1,0:T(8,128)(2,1)S(1)} %collective-permute-done.15.other) | copy-start | bytes 393220
  73.3 7.4 %collective-permute-start.16 = (bf16[2,256,128]{2,1,0:T(8,128)(2,1)S(1)}, bf16[2,256,128]{2,1,0:T(8,128)(2,1)S(1)}, u32[]{:S(2)}, u32[]{:S(2)}) collective-permute-start(bf16[2,256,128]{2,1,0:T(8,128)(2,1)S(1)} %carry_on.16), channel_id=1, source_target_pairs={{0,8},{4,12},{8,16},{12,20},{16,24},{20,28},{1,9},{5,13},{9,17},{1... | collective-permute-start | bytes 393224 | tf_op jit(solution)/shard_map/ppermute | solution.py:305
  77.7 11.4 %copy-start.34 = (bf16[2,256,128]{2,1,0:T(8,128)(2,1)}, bf16[2,256,128]{2,1,0:T(8,128)(2,1)S(1)}, u32[]{:S(2)}) copy-start(bf16[2,256,128]{2,1,0:T(8,128)(2,1)S(1)} %collective-permute-done.17.other) | copy-start | bytes 393220
  80.9 7.4 %collective-permute-start.18 = (bf16[2,256,128]{2,1,0:T(8,128)(2,1)S(1)}, bf16[2,256,128]{2,1,0:T(8,128)(2,1)S(1)}, u32[]{:S(2)}, u32[]{:S(2)}) collective-permute-start(bf16[2,256,128]{2,1,0:T(8,128)(2,1)S(1)} %carry_on.17), channel_id=1, source_target_pairs={{0,8},{4,12},{8,16},{12,20},{16,24},{20,28},{1,9},{5,13},{9,17},{1... | collective-permute-start | bytes 393224 | tf_op jit(solution)/shard_map/ppermute | solution.py:305
  89.1 7.2 %collective-permute-start.19 = (bf16[2,256,128]{2,1,0:T(8,128)(2,1)}, bf16[2,256,128]{2,1,0:T(8,128)(2,1)}, u32[]{:S(2)}, u32[]{:S(2)}) collective-permute-start(bf16[2,256,128]{2,1,0:T(8,128)(2,1)} %carry_on.18), channel_id=1, source_target_pairs={{0,8},{4,12},{8,16},{12,20},{16,24},{20,28},{1,9},{5,13},{9,17},{1... | collective-permute-start | bytes 393224 | tf_op jit(solution)/shard_map/ppermute | solution.py:305
  94.1 13.3 %copy-start.3 = (bf16[2,256,128]{2,1,0:T(8,128)(2,1)S(1)}, bf16[2,256,128]{2,1,0:T(8,128)(2,1)}, u32[]{:S(2)}) copy-start(bf16[2,256,128]{2,1,0:T(8,128)(2,1)} %copy-done.1) | copy-start | bytes 393220
  94.1 13.3 %copy-start.17 = (f32[2,256,128]{2,1,0:T(8,128)S(1)}, f32[2,256,128]{2,1,0:T(8,128)}, u32[]{:S(2)}) copy-start(f32[2,256,128]{2,1,0:T(8,128)} %copy-done.16) | copy-start | bytes 786436
  94.1 13.3 %copy-start.21 = (bf16[2,256,128]{2,1,0:T(8,128)(2,1)S(1)}, bf16[2,256,128]{2,1,0:T(8,128)(2,1)}, u32[]{:S(2)}) copy-start(bf16[2,256,128]{2,1,0:T(8,128)(2,1)} %copy-done.20) | copy-start | bytes 393220
  94.1 14.3 %copy-start.15 = (f32[2,256,128]{2,1,0:T(8,128)S(1)}, f32[2,256,128]{2,1,0:T(8,128)}, u32[]{:S(2)}) copy-start(f32[2,256,128]{2,1,0:T(8,128)} %copy-done.14) | copy-start | bytes 786436
  94.1 14.3 %copy-start.25 = (bf16[2,256,128]{2,1,0:T(8,128)(2,1)S(1)}, bf16[2,256,128]{2,1,0:T(8,128)(2,1)}, u32[]{:S(2)}) copy-start(bf16[2,256,128]{2,1,0:T(8,128)(2,1)} %copy-done.24) | copy-start | bytes 393220
  94.2 16.3 %copy-start.13 = (f32[2,256,128]{2,1,0:T(8,128)S(1)}, f32[2,256,128]{2,1,0:T(8,128)}, u32[]{:S(2)}) copy-start(f32[2,256,128]{2,1,0:T(8,128)} %copy-done.12) | copy-start | bytes 786436
  96.3 15.1 %copy-start.11 = (f32[2,256,128]{2,1,0:T(8,128)S(1)}, f32[2,256,128]{2,1,0:T(8,128)}, u32[]{:S(2)}) copy-start(f32[2,256,128]{2,1,0:T(8,128)} %copy-done.10) | copy-start | bytes 786436
  97.4 16.1 %collective-permute-start.20 = (bf16[2,256,128]{2,1,0:T(8,128)(2,1)S(1)}, bf16[2,256,128]{2,1,0:T(8,128)(2,1)S(1)}, u32[]{:S(2)}, u32[]{:S(2)}) collective-permute-start(bf16[2,256,128]{2,1,0:T(8,128)(2,1)S(1)} %carry_on.19), channel_id=1, source_target_pairs={{0,8},{4,12},{8,16},{12,20},{16,24},{20,28},{1,9},{5,13},{9,17},{1... | collective-permute-start | bytes 393224 | tf_op jit(solution)/shard_map/ppermute | solution.py:305
  105.4 6.0 %copy-start.29 = (bf16[2,256,128]{2,1,0:T(8,128)(2,1)S(1)}, bf16[2,256,128]{2,1,0:T(8,128)(2,1)}, u32[]{:S(2)}) copy-start(bf16[2,256,128]{2,1,0:T(8,128)(2,1)} %copy-done.28) | copy-start | bytes 393220
  105.4 6.4 %copy-start.9 = (f32[2,256,128]{2,1,0:T(8,128)S(1)}, f32[2,256,128]{2,1,0:T(8,128)}, u32[]{:S(2)}) copy-start(f32[2,256,128]{2,1,0:T(8,128)} %copy-done.8) | copy-start | bytes 786436
  105.4 6.4 %copy-start.31 = (bf16[2,256,128]{2,1,0:T(8,128)(2,1)S(1)}, bf16[2,256,128]{2,1,0:T(8,128)(2,1)}, u32[]{:S(2)}) copy-start(bf16[2,256,128]{2,1,0:T(8,128)(2,1)} %copy-done.30) | copy-start | bytes 393220
  105.8 6.4 %copy-start.7 = (f32[2,256,128]{2,1,0:T(8,128)S(1)}, f32[2,256,128]{2,1,0:T(8,128)}, u32[]{:S(2)}) copy-start(f32[2,256,128]{2,1,0:T(8,128)} %copy-done.6) | copy-start | bytes 786436
  105.8 6.4 %copy-start.33 = (bf16[2,256,128]{2,1,0:T(8,128)(2,1)S(1)}, bf16[2,256,128]{2,1,0:T(8,128)(2,1)}, u32[]{:S(2)}) copy-start(bf16[2,256,128]{2,1,0:T(8,128)(2,1)} %copy-done.32) | copy-start | bytes 393220
  105.8 10.6 %collective-permute-start.21 = (bf16[2,256,128]{2,1,0:T(8,128)(2,1)S(1)}, bf16[2,256,128]{2,1,0:T(8,128)(2,1)S(1)}, u32[]{:S(2)}, u32[]{:S(2)}) collective-permute-start(bf16[2,256,128]{2,1,0:T(8,128)(2,1)S(1)} %get-tuple-element.61), channel_id=1, source_target_pairs={{0,4},{4,0},{8,12},{12,8},{16,20},{20,16},{24,28},{28,24},{1,5},{5... | collective-permute-start | bytes 393224 | tf_op jit(solution)/shard_map/ppermute | solution.py:312
  107.8 7.3 %copy-start.5 = (f32[2,256,128]{2,1,0:T(8,128)S(1)}, f32[2,256,128]{2,1,0:T(8,128)}, u32[]{:S(2)}) copy-start(f32[2,256,128]{2,1,0:T(8,128)} %copy-done.4) | copy-start | bytes 786436
  107.8 7.3 %copy-start.35 = (bf16[2,256,128]{2,1,0:T(8,128)(2,1)S(1)}, bf16[2,256,128]{2,1,0:T(8,128)(2,1)}, u32[]{:S(2)}) copy-start(bf16[2,256,128]{2,1,0:T(8,128)(2,1)} %copy-done.34) | copy-start | bytes 393220
  107.8 9.2 %collective-permute-start.22 = (bf16[2,256,128]{2,1,0:T(8,128)(2,1)S(1)}, bf16[2,256,128]{2,1,0:T(8,128)(2,1)S(1)}, u32[]{:S(2)}, u32[]{:S(2)}) collective-permute-start(bf16[2,256,128]{2,1,0:T(8,128)(2,1)S(1)} %get-tuple-element.62), channel_id=1, source_target_pairs={{0,4},{4,0},{8,12},{12,8},{16,20},{20,16},{24,28},{28,24},{1,5},{5... | collective-permute-start | bytes 393224 | tf_op jit(solution)/shard_map/ppermute | solution.py:312
  108.8 10.2 %copy-start.41 = (s32[4]{0:T(128)S(1)}, s32[4]{0:T(128)}, u32[]{:S(2)}) copy-start(s32[4]{0:T(128)} %constant.67.clone) | copy-start | bytes 52
  108.8 10.2 %copy-start.42 = (s32[4]{0:T(128)S(1)}, s32[4]{0:T(128)}, u32[]{:S(2)}) copy-start(s32[4]{0:T(128)} %constant.66.clone) | copy-start | bytes 52
  108.8 15.4 %copy-start.40 = (f32[256]{0:T(256)S(1)}, f32[256]{0:T(256)}, u32[]{:S(2)}) copy-start(f32[256]{0:T(256)} %param.10) | copy-start | bytes 3076
  108.9 9.7 %collective-permute-start.23 = (bf16[2,256,128]{2,1,0:T(8,128)(2,1)S(1)}, bf16[2,256,128]{2,1,0:T(8,128)(2,1)S(1)}, u32[]{:S(2)}, u32[]{:S(2)}) collective-permute-start(bf16[2,256,128]{2,1,0:T(8,128)(2,1)S(1)} %get-tuple-element.63), channel_id=1, source_target_pairs={{0,4},{4,0},{8,12},{12,8},{16,20},{20,16},{24,28},{28,24},{1,5},{5... | collective-permute-start | bytes 393224 | tf_op jit(solution)/shard_map/ppermute | solution.py:312
  110.8 13.5 %copy-start.38 = (bf16[256,256]{1,0:T(8,128)(2,1)S(1)}, bf16[256,256]{1,0:T(8,128)(2,1)}, u32[]{:S(2)}) copy-start(bf16[256,256]{1,0:T(8,128)(2,1)} %weight.1) | copy-start | bytes 393220
  110.8 8.2 %collective-permute-start.24 = (bf16[2,256,128]{2,1,0:T(8,128)(2,1)S(1)}, bf16[2,256,128]{2,1,0:T(8,128)(2,1)S(1)}, u32[]{:S(2)}, u32[]{:S(2)}) collective-permute-start(bf16[2,256,128]{2,1,0:T(8,128)(2,1)S(1)} %get-tuple-element.64), channel_id=1, source_target_pairs={{0,4},{4,0},{8,12},{12,8},{16,20},{20,16},{24,28},{28,24},{1,5},{5... | collective-permute-start | bytes 393224 | tf_op jit(solution)/shard_map/ppermute | solution.py:312
  113.5 6.4 %collective-permute-start.25 = (bf16[2,256,128]{2,1,0:T(8,128)(2,1)S(1)}, bf16[2,256,128]{2,1,0:T(8,128)(2,1)S(1)}, u32[]{:S(2)}, u32[]{:S(2)}) collective-permute-start(bf16[2,256,128]{2,1,0:T(8,128)(2,1)S(1)} %get-tuple-element.65), channel_id=1, source_target_pairs={{0,4},{4,0},{8,12},{12,8},{16,20},{20,16},{24,28},{28,24},{1,5},{5... | collective-permute-start | bytes 393224 | tf_op jit(solution)/shard_map/ppermute | solution.py:312
  116.4 5.0 %collective-permute-start.26 = (bf16[2,256,128]{2,1,0:T(8,128)(2,1)S(1)}, bf16[2,256,128]{2,1,0:T(8,128)(2,1)S(1)}, u32[]{:S(2)}, u32[]{:S(2)}) collective-permute-start(bf16[2,256,128]{2,1,0:T(8,128)(2,1)S(1)} %get-tuple-element.66), channel_id=1, source_target_pairs={{0,4},{4,0},{8,12},{12,8},{16,20},{20,16},{24,28},{28,24},{1,5},{5... | collective-permute-start | bytes 393224 | tf_op jit(solution)/shard_map/ppermute | solution.py:312
  117.0 5.9 %collective-permute-start.27 = (bf16[2,256,128]{2,1,0:T(8,128)(2,1)S(1)}, bf16[2,256,128]{2,1,0:T(8,128)(2,1)S(1)}, u32[]{:S(2)}, u32[]{:S(2)}) collective-permute-start(bf16[2,256,128]{2,1,0:T(8,128)(2,1)S(1)} %get-tuple-element.67), channel_id=1, source_target_pairs={{0,4},{4,0},{8,12},{12,8},{16,20},{20,16},{24,28},{28,24},{1,5},{5... | collective-permute-start | bytes 393224 | tf_op jit(solution)/shard_map/ppermute | solution.py:312
  118.5 5.7 %collective-permute-start.28 = (bf16[2,256,128]{2,1,0:T(8,128)(2,1)S(1)}, bf16[2,256,128]{2,1,0:T(8,128)(2,1)S(1)}, u32[]{:S(2)}, u32[]{:S(2)}) collective-permute-start(bf16[2,256,128]{2,1,0:T(8,128)(2,1)S(1)} %get-tuple-element.68), channel_id=1, source_target_pairs={{0,4},{4,0},{8,12},{12,8},{16,20},{20,16},{24,28},{28,24},{1,5},{5... | collective-permute-start | bytes 393224 | tf_op jit(solution)/shard_map/ppermute | solution.py:312
  (8 other events, 10.9 us)

commit v2 on v0

v2 whole, which is shorter than its diff:
```python
import functools

import jax
import jax.numpy as jnp
from jax import lax
from jax.experimental import pallas as pl
from jax.experimental.pallas import tpu as pltpu
from jax.sharding import PartitionSpec as P

MIB = 1 << 20
VMEM = pl.BlockSpec(memory_space=pltpu.VMEM)
ANY = pl.BlockSpec(memory_space=pl.ANY)
SMEM = pl.BlockSpec(memory_space=pltpu.SMEM)
BF16, F32 = jnp.bfloat16, jnp.float32


def params(mib):
    return pltpu.CompilerParams(vmem_limit_bytes=mib * MIB)


def sizes_of(half):
    if half % 4 or half < 8:
        return [2] * (half // 2)
    return [2] + [4] * (half // 4 - 1) + [2]


def columns(*rows):
    rows = list(rows) + [rows[0]] * (8 - len(rows))
    return jnp.transpose(jnp.concatenate(rows, axis=0))


def call(kernel, out_shape, scalars, operands, after, name, mib=16, scratch=(), specs=None, **more):
    specs = specs or [VMEM] * len(operands)
    n = len(scalars) + len(operands)

    def body(*refs):
        kernel(*refs[:n], *refs[n + len(after) :])

    return pl.pallas_call(
        body,
        out_shape=out_shape,
        in_specs=[SMEM] * len(scalars) + specs + [ANY] * len(after),
        scratch_shapes=list(scratch),
        compiler_params=params(mib),
        name=name,
        **more,
    )(*scalars, *operands, *after)


def conv(rows_in, halo, weight, decays, lower, edge, sizes, start, count, dtype, after, edges=False):
    tile_rows, channels, width = rows_in.shape
    states = weight.shape[2]
    half = tile_rows // 2
    mine = sizes[start : start + count]
    before, total = sum(sizes[:start]), sum(mine)
    whole = start + count == len(sizes)
    assert whole == (halo is not None)
    out_shape = [jax.ShapeDtypeStruct((n, states, width), dtype) for n in mine]
    if edges:
        out_shape += [jax.ShapeDtypeStruct((channels, width), rows_in.dtype)] * 2
        out_shape += [jax.ShapeDtypeStruct(decays.shape, decays.dtype)]

    def kernel(lower_ref, edge_ref, rows_ref, weight_ref, decays_ref, *refs):
        refs = list(refs)
        halo_ref = refs.pop(0) if whole else None
        outs, (rows, shifted, sems) = refs[:-3], refs[-3:]
        low = lower_ref[0]
        copied = total + 1 if whole else total + 2
        first_low = half + before - 1
        first_up = 0 if whole else half - before - total - 1
        main = pltpu.make_async_copy(
            rows_ref.at[pl.ds(first_up + low * (first_low - first_up), copied)],
            rows.at[pl.ds((1 - low) if whole else 0, copied)],
            sems.at[0],
        )
        main.start()
        if edges:
            top = pltpu.make_async_copy(rows_ref.at[0], outs[count], sems.at[1])
            bottom = pltpu.make_async_copy(rows_ref.at[tile_rows - 1], outs[count + 1], sems.at[2])
            top.start()
            bottom.start()
            outs[count + 2][...] = decays_ref[...]
        main.wait()
        if whole:
            slot = low * (total + 1)
            rows[slot] = jnp.where(edge_ref[0] == 1, jnp.zeros_like(halo_ref), halo_ref[...])
        lane = lax.broadcasted_iota(jnp.int32, (channels, width), 1)

        def shift(r, carry):
            row = rows[r].astype(F32)
            left = jnp.where(lane == 0, 0.0, pltpu.roll(row, 1, 1))
            right = jnp.where(lane == width - 1, 0.0, pltpu.roll(row, width - 1, 1))
            shifted[r, :channels] = left.astype(rows.dtype)
            shifted[r, channels : 2 * channels] = rows[r]
            shifted[r, 2 * channels :] = right.astype(rows.dtype)
            return carry

        lax.fori_loop(0, total + 2, shift, 0, unroll=2)
        decay = decays_ref[...]
        gain = columns(jnp.sqrt(1.0 - decay * decay))[:, 0:1]
        taps = jnp.concatenate([weight_ref[i, j] for i in range(3) for j in range(3)], axis=1)
        done = 0
        for n, size in enumerate(mine):
            at_low, at_up = done, total - done - size
            for q in range(0, size, 2):
                r = at_up + q + low * (at_low - at_up)
                window = jnp.concatenate(
                    [
                        jnp.concatenate([shifted[r + i], shifted[r + i + 1]], axis=1)
                        for i in range(3)
                    ],
                    axis=0,
                )
                drive = gain * jnp.dot(taps, window, preferred_element_type=F32)
                outs[n][q] = drive[:, :width].astype(dtype)
                outs[n][q + 1] = drive[:, width:].astype(dtype)
            done += size
        if edges:
            top.wait()
            bottom.wait()

    out_specs = [VMEM] * count + ([ANY, ANY, VMEM] if edges else [])
    return call(
        kernel, out_shape, [lower, edge],
        [rows_in, weight, decays] + ([halo] if whole else []), after, "conv_chunks", 40,
        scratch=[
            pltpu.VMEM((total + 2, channels, width), rows_in.dtype),
            pltpu.VMEM((total + 2, 3 * channels, width), rows_in.dtype),
            pltpu.SemaphoreType.DMA((3,)),
        ],
        specs=[ANY, VMEM, VMEM] + ([VMEM] if whole else []),
        out_specs=out_specs,
        cost_estimate=pl.CostEstimate(
            flops=18 * channels * states * width * total,
            bytes_accessed=4 * total * channels * width + weight.size * 2,
            transcendentals=0,
        ),
    )


def coefficients(odd, own_decay, other_decay, after):
    def kernel(odd_ref, own_ref, other_ref, out):
        is_odd = jnp.full(own_ref.shape, odd_ref[0], jnp.int32) == 1
        own, other = own_ref[...], other_ref[...]
        both = own * other
        one, zero = jnp.ones_like(own), jnp.zeros_like(own)
        out[...] = columns(
            both,
            jnp.where(is_odd, one, other),
            jnp.where(is_odd, own, one),
            jnp.where(is_odd, both, own),
            jnp.where(is_odd, other, both),
            jnp.where(is_odd, own, zero),
            jnp.where(is_odd, zero, other),
        )

    shape = jax.ShapeDtypeStruct((own_decay.shape[1], 8), F32)
    return call(kernel, shape, [odd], [own_decay, other_decay], after, "coefficients")


def pair_drive(keep, other, coefs, after):
    def kernel(keep_ref, other_ref, coefs_ref, out):
        for q in range(keep.shape[0]):
            out[q] = coefs_ref[:, 1:2] * keep_ref[q] + coefs_ref[:, 2:3] * other_ref[q].astype(F32)

    shape = jax.ShapeDtypeStruct(keep.shape, F32)
    return call(kernel, shape, [], [keep, other, coefs], after, "pair_drive")


def carry_on(group, coefs, drives, carry, after):
    groups = sorted(drives)
    most = max(drives[g].shape[0] for g in groups)
    shape = jax.ShapeDtypeStruct((most,) + drives[groups[0]].shape[1:], BF16)

    def kernel(group_ref, coefs_ref, *refs):
        out = refs[-1]
        out[...] = jnp.zeros_like(out)
        for g, ref in zip(groups, refs):

            @pl.when(group_ref[0] == g)
            def one(g=g, ref=ref):
                for q in range(ref.shape[0]):
                    total = ref[q]
                    if g > 0:
                        total = total + coefs_ref[:, 0:1] * refs[len(groups)][q].astype(F32)
                    out[q] = total.astype(BF16)

    operands = [coefs] + [drives[g] for g in groups] + ([carry] if carry is not None else [])
    return call(kernel, shape, [group], operands, after, "carry_on")


def states_of(group, coefs, keep, other, carries, after):
    shape = jax.ShapeDtypeStruct(keep.shape, BF16)

    def kernel(group_ref, coefs_ref, keep_ref, other_ref, *refs):
        own, back = refs[-2:]

        def settle(carry_ref):
            for q in range(keep.shape[0]):
                held, sent = keep_ref[q], other_ref[q].astype(F32)
                mine = held + coefs_ref[:, 5:6] * sent
                theirs = coefs_ref[:, 6:7] * held + sent
                if carry_ref is not None:
                    carry = carry_ref[q].astype(F32)
                    mine = mine + coefs_ref[:, 3:4] * carry
                    theirs = theirs + coefs_ref[:, 4:5] * carry
                own[q] = mine.astype(BF16)
                back[q] = theirs.astype(BF16)

        for g in range(len(carries) + 1):
            pl.when(group_ref[0] == g)(functools.partial(settle, refs[g - 1] if g else None))

    return call(
        kernel, [shape, shape], [group], [coefs, keep, other] + list(carries), after, "states_of"
    )


def output_half(lower, rows_in, weight, skip, states, earlier, after, dtype):
    tile_rows, channels, width = rows_in.shape
    half = tile_rows // 2
    pitch = channels + 1
    count = len(states)
    sizes = [value.shape[0] for value in states]

    def kernel(lower_ref, rows_ref, weight_ref, skip_ref, *refs):
        chunks = refs[:count]
        out, rows, held, total, tile, sems = refs[-6:]
        low = lower_ref[0]
        begin = pl.multiple_of(low * half, half)
        main = pltpu.make_async_copy(rows_ref.at[pl.ds(begin, half)], rows, sems.at[0])
        main.start()
        copies = []
        done = 0
        for n, chunk in enumerate(chunks):
            at_up = half - done - sizes[n]
            r = at_up + low * (done - at_up)
            copies.append(
                pltpu.make_async_copy(chunk, held.at[pl.ds(r, sizes[n])], sems.at[n + 1])
            )
            done += sizes[n]
        for copy in copies:
            copy.start()
        gain = columns(skip_ref[...])[:, 0:1]
        main.wait()
        for copy in copies:
            copy.wait()

        def one(p, carry):
            r = 2 * p
            value = jnp.dot(
                weight_ref[...],
                jnp.concatenate([held[r], held[r + 1]], axis=1),
                preferred_element_type=F32,
            )
            for q in range(2):
                total[pl.ds((r + q) * pitch, channels), :] = value[
                    :, q * width : (q + 1) * width
                ] + gain * rows[r + q].astype(F32)
            return carry

        lax.fori_loop(0, half // 2, one, 0)

        def settle(n, carry):
            for i in range(8):
                tile[n * 8 + i] = total[pl.ds(n * 8 + i, half, stride=pitch), :].astype(dtype)
            return carry

        lax.fori_loop(0, channels // 8, settle, 0, unroll=2)
        last = pltpu.make_async_copy(tile, out.at[:, pl.ds(begin, half), :], sems.at[count + 1])
        last.start()
        last.wait()

    operands = [rows_in, weight, skip] + list(states)
    more = {}
    if earlier is not None:
        operands.append(earlier)
        more["input_output_aliases"] = {len(operands): 0}
    return call(
        kernel,
        jax.ShapeDtypeStruct((channels, tile_rows, width), dtype),
        [lower], operands, after, "output_half", 40,
        scratch=[
            pltpu.VMEM((half, channels, width), rows_in.dtype),
            pltpu.VMEM((half, channels, width), BF16),
            pltpu.VMEM((half * pitch + 8, width), F32),
            pltpu.VMEM((channels, half, width), dtype),
            pltpu.SemaphoreType.DMA((count + 2,)),
        ],
        specs=[ANY, VMEM, VMEM] + [ANY] * (len(operands) - 3),
        out_specs=ANY,
        **more,
    )


def on_device(frames_in, conv_weight, out_weight, skip_gain, decays):
    tile_rows = frames_in.shape[2]
    frames = lax.axis_size("tm")
    spaces = lax.axis_size("space")
    groups = frames // 2
    me, at = lax.axis_index("tm"), lax.axis_index("space")
    scalar = lambda value: jnp.asarray(value, jnp.int32).reshape(1)
    group, odd, even = scalar(me // 2), scalar(me % 2), scalar(1 - me % 2)
    is_top, is_bottom = scalar(at == 0), scalar(at == spaces - 1)
    is_even = me % 2 == 0
    sizes = sizes_of(tile_rows // 2)
    chunks = len(sizes)

    swap = [(i, i + 1 - 2 * (i % 2)) for i in range(frames)]
    even_hop = [(i, i + 2 if (i // 2) % 2 == 0 else i - 2) for i in range(frames)]
    odd_hop = [
        (i, i if i // 2 in (0, groups - 1) else (i + 2 if (i // 2) % 2 else i - 2))
        for i in range(frames)
    ]
    down = [(i, (i + 1) % spaces) for i in range(spaces)]
    up = [(i, (i - 1) % spaces) for i in range(spaces)]

    rows = jnp.transpose(frames_in[0], (1, 0, 2))
    sent = functools.partial(
        conv, rows, weight=conv_weight, decays=decays, lower=even,
        edge=jnp.where(is_even, is_bottom, is_top), sizes=sizes, dtype=BF16,
    )
    kept = functools.partial(
        conv, rows, weight=conv_weight, decays=decays, lower=odd,
        edge=jnp.where(is_even, is_top, is_bottom), sizes=sizes, dtype=F32,
    )
    first, top, bottom, decay = sent(halo=None, start=0, count=1, after=[], edges=True)
    others = [lax.ppermute(first, "tm", swap)]
    other_decay = lax.ppermute(decay, "tm", swap)
    from_low = lax.ppermute(bottom, "space", down)
    from_high = lax.ppermute(top, "space", up)
    halo_sent = jnp.where(is_even, from_high, from_low)
    halo_kept = jnp.where(is_even, from_low, from_high)
    rest = sent(halo=halo_sent, start=1, count=chunks - 1, after=[])
    others += [lax.ppermute(value, "tm", swap) for value in rest]
    held = list(kept(halo=None, start=0, count=1, after=[rest[-1]]))
    coefs = coefficients(odd, decays, other_decay, [held[-1]])

    lag = 3 * ((groups - 2) // 2) + 1
    drives, evens, odds, own, back = [], {}, {}, [], []
    drives.append(pair_drive(held[0], others[0], coefs, []))
    after = [drives[0]]
    for step in range(chunks + lag):
        ready = {
            g: drives[step - 3 * (g // 2)]
            for g in range(0, groups - 1, 2)
            if 0 <= step - 3 * (g // 2) < chunks
        }
        if ready:
            value = carry_on(group, coefs, ready, odds.get(step - 2), after)
            evens[step] = lax.ppermute(value, "tm", even_hop)
            after = [value]
        if step == 0:
            held += kept(halo=halo_kept, start=1, count=chunks - 1, after=after)
            after = [held[-1]]
        k = step - lag
        if k >= 0:
            carries = [
                evens[k + 3 * ((g - 1) // 2)] if g % 2 else odds[k + 1 + 3 * ((g - 2) // 2)]
                for g in range(1, groups)
            ]
            mine, theirs = states_of(group, coefs, held[k], others[k], carries, after)
            own.append(mine)
            back.append(lax.ppermute(theirs, "tm", swap))
            after = [theirs]
        ready = {
            g: drives[step - 1 - 3 * ((g - 1) // 2)]
            for g in range(1, groups - 1, 2)
            if 0 <= step - 1 - 3 * ((g - 1) // 2) < chunks
        }
        if ready:
            value = carry_on(group, coefs, ready, evens[step - 1], after)
            odds[step] = lax.ppermute(value, "tm", odd_hop)
            after = [value]
        if step + 1 < chunks:
            drives.append(pair_drive(held[step + 1], others[step + 1], coefs, after))
            after = [drives[-1]]

    skip = skip_gain[None]
    dtype = frames_in.dtype
    half_done = output_half(odd, rows, out_weight, skip, own, None, after, dtype)
    result = output_half(even, rows, out_weight, skip, back, half_done, [], dtype)
    return result[None]


def solution(mesh):
    placed = (P("tm", None, "space", None), P(), P(), P(), P("tm", None))
    return jax.shard_map(
        on_device,
        mesh=mesh,
        in_specs=placed,
        out_specs=P("tm", None, "space", None),
        check_vma=False,
    )
```

time: 214 us -> 94.6 us (0.44)
  the two profiles are of different devices: /device:TPU:0 before, /device:TPU:14 now
where the time goes in v2:
time: 94.6 us; the launch traced here: 94.4 us
  waiting for transfers between devices  39 us (41%)
  starting transfers between devices  24.8 us (26%)
  Pallas kernels  24.3 us (26%)
  local copies, waits for them, and re-layouts  4.99 us (5%)
    pallas_call x30, Pallas kernels, call(): pl.pallas_call(body, out_shape=out_shape, in_specs=[SMEM] * len(scalars)...  24.3 us
    ppermute x8, waiting for transfers between devices, on_device(): evens[step] = lax.ppermute(value, 'tm', even_hop)  17 us
    ppermute x5, starting transfers between devices, on_device(): odds[step] = lax.ppermute(value, 'tm', odd_hop)  13.9 us
    ppermute x5, waiting for transfers between devices, on_device(): back.append(lax.ppermute(theirs, 'tm', swap))  7.77 us
    ppermute x5, waiting for transfers between devices, on_device(): odds[step] = lax.ppermute(value, 'tm', odd_hop)  5.94 us
    unnamed x23, local copies, waits for them, and re-layouts  4.99 us
    ppermute x1, waiting for transfers between devices, on_device(): other_decay = lax.ppermute(decay, 'tm', swap)  4.9 us
    ppermute x5, starting transfers between devices, on_device(): back.append(lax.ppermute(theirs, 'tm', swap))  3.85 us
  transfers between devices with their start and end apart: 26, of which 16 were waited for; matrix products, arithmetic and copies ran while one was open for 1% of the time, Pallas kernels for 20%

profile of v2, /device:TPU:14, one launch (start us, length us, event | category | flops | bytes accessed | tf_op | source)
XLA Modules:
  0.0 94.4 jit_solution(4603889286761242850)
XLA Ops:
  0.0 2.5 %copy.9 = bf16[1,256,32,128]{3,1,2,0:T(8,128)(2,1)S(1)} copy(bf16[1,256,32,128]{3,2,1,0:T(8,128)(2,1)} %param.5) | data formatting | bytes 4194304 | tf_op args[0]
  2.5 1.7 %conv_chunks.4 = (bf16[2,256,128]{2,1,0:T(8,128)(2,1)}, bf16[256,128]{1,0:T(8,128)(2,1)S(1)}, bf16[256,128]{1,0:T(8,128)(2,1)S(1)}, f32[1,256]{1,0:T(1,128)S(1)}) custom-call(s32[1]{0:T(128)} %bitcast.refs_0_, s32[1]{0:T(128)} %bitcast.6.refs_1_, bf16[32,256,128]{2,1,0:T(8,128)(2,1)S(1)} %bitcast.12, bf16[3,3,256,256]{3,2,1,0:T(8,128)(2,1)S(1)} %copy-done, ...), custom_call_target="tpu_custom_call" | custom-call | flops 301989888 | bytes 1441792 | tf_op jit(solution)/shard_map/conv_chunks/pallas_call | solution.py:39
  4.3 0.5 collective-permute-start.2
  4.8 0.5 collective-permute-start.3
  5.3 0.9 collective-permute-done.1
  6.2 2.5 %collective-permute-done.2 = bf16[256,128]{1,0:T(8,128)(2,1)S(1)} collective-permute-done((bf16[256,128]{1,0:T(8,128)(2,1)S(1)}, bf16[256,128]{1,0:T(8,128)(2,1)S(1)}, u32[]{:S(2)}, u32[]{:S(2)}) %collective-permute-start.2) | collective-permute-done | bytes 65568 | tf_op jit(solution)/shard_map/ppermute | solution.py:329
  8.7 0.6 broadcast_select_fusion
  9.3 3.8 %conv_chunks.5 = (bf16[4,256,128]{2,1,0:T(8,128)(2,1)}, bf16[4,256,128]{2,1,0:T(8,128)(2,1)S(1)}, bf16[4,256,128]{2,1,0:T(8,128)(2,1)S(1)}, bf16[2,256,128]{2,1,0:T(8,128)(2,1)S(1)}) custom-call(s32[1]{0:T(128)} %bitcast.refs_0_, s32[1]{0:T(128)} %bitcast.6.refs_1_, bf16[32,256,128]{2,1,0:T(8,128)(2,1)S(1)} %bitcast.13, ...), custom_call_target="tpu_custom_call" | custom-call | flops 2113929216 | bytes 3014656 | tf_op jit(solution)/shard_map/conv_chunks/pallas_call | solution.py:39
  13.1 0.6 copy-done.2
  13.8 0.7 copy-done.8
  14.5 0.5 collective-permute-start.5
  15.0 0.2 copy-done.10
  15.2 1.3 %collective-permute-start = (f32[1,256]{1,0:T(1,128)S(1)}, f32[1,256]{1,0:T(1,128)S(1)}, u32[]{:S(2)}, u32[]{:S(2)}) collective-permute-start(f32[1,256]{1,0:T(1,128)S(1)} %get-tuple-element.27), channel_id=1, source_target_pairs={{0,4},{4,0},{8,12},{12,8},{16,20},{20,16},{24,28},{28,24},{1,5},{5... | collective-permute-start | bytes 3080 | tf_op jit(solution)/shard_map/ppermute | solution.py:328
  16.5 0.7 collective-permute-start.9
  17.2 0.9 copy-done.3
  18.1 0.9 conv_chunks.6.refs_3_.refs_0_.refs_2_
  19.0 4.9 %collective-permute-done.refs_2_ = f32[1,256]{1,0:T(1,128)S(1)} collective-permute-done((f32[1,256]{1,0:T(1,128)S(1)}, f32[1,256]{1,0:T(1,128)S(1)}, u32[]{:S(2)}, u32[]{:S(2)}) %collective-permute-start) | collective-permute-done | bytes 1056 | tf_op jit(solution)/shard_map/ppermute | solution.py:328
  23.9 0.1 coefficients.1.refs_2_.refs_1_
  24.1 1.1 %pair_drive.5.refs_2_.refs_3_ = f32[2,256,128]{2,1,0:T(8,128)S(1)} custom-call(f32[2,256,128]{2,1,0:T(8,128)S(1)} %conv_chunks.6.refs_3_.refs_0_.refs_2_, bf16[2,256,128]{2,1,0:T(8,128)(2,1)} %collective-permute-done.3.refs_1_.refs_3_, f32[256,8]{1,0:T(8,128)S(1)} %coefficients.1.refs_2_.refs_1_), custom_call_target="tpu_custom_call" | custom-call | tf_op jit(solution)/shard_map/pair_drive/pallas_call | solution.py:39
  25.2 3.8 %conv_chunks.7 = (f32[4,256,128]{2,1,0:T(8,128)S(1)}, f32[4,256,128]{2,1,0:T(8,128)S(1)}, f32[4,256,128]{2,1,0:T(8,128)S(1)}, f32[2,256,128]{2,1,0:T(8,128)S(1)}) custom-call(s32[1]{0:T(128)} %bitcast.5.refs_0_, s32[1]{0:T(128)} %bitcast.8.refs_1_, bf16[32,256,128]{2,1,0:T(8,128)(2,1)S(1)} %bitcast.15, bf16[3,3,256,256]{3,2,1,0:T(8,128)(2,1)S(1)} %copy-done, ...), custom_call_target="tpu_custom_call" | custom-call | flops 2113929216 | bytes 3014656 | tf_op jit(solution)/shard_map/conv_chunks/pallas_call | solution.py:39
  29.1 0.4 pair_drive.6.refs_2_.refs_3_
  29.5 0.5 collective-permute-start.8
  30.0 0.5 collective-permute-start.7
  30.5 1.5 %collective-permute-start.4 = (bf16[2,256,128]{2,1,0:T(8,128)(2,1)S(1)}, bf16[2,256,128]{2,1,0:T(8,128)(2,1)S(1)}, u32[]{:S(2)}, u32[]{:S(2)}) collective-permute-start(bf16[2,256,128]{2,1,0:T(8,128)(2,1)S(1)} %carry_on.13.refs_6_), channel_id=1, source_target_pairs={{0,8},{4,12},{8,0},{12,4},{16,24},{20,28},{24,16},{28,20},{1,9},{5... | collective-permute-start | bytes 393224 | tf_op jit(solution)/shard_map/ppermute | solution.py:350
  32.1 7.0 %collective-permute-done.4.refs_3_.refs_4_ = bf16[2,256,128]{2,1,0:T(8,128)(2,1)S(1)} collective-permute-done((bf16[2,256,128]{2,1,0:T(8,128)(2,1)S(1)}, bf16[2,256,128]{2,1,0:T(8,128)(2,1)S(1)}, u32[]{:S(2)}, u32[]{:S(2)}) %collective-permute-start.4) | collective-permute-done | bytes 131104 | tf_op jit(solution)/shard_map/ppermute | solution.py:350
  39.1 0.1 carry_on.15.refs_3_
  39.2 3.3 %collective-permute-start.6 = (bf16[2,256,128]{2,1,0:T(8,128)(2,1)S(1)}, bf16[2,256,128]{2,1,0:T(8,128)(2,1)S(1)}, u32[]{:S(2)}, u32[]{:S(2)}) collective-permute-start(bf16[2,256,128]{2,1,0:T(8,128)(2,1)S(1)} %carry_on.15.refs_3_), channel_id=1, source_target_pairs={{0,0},{4,4},{8,16},{12,20},{16,8},{20,12},{24,24},{28,28},{1,1},{5... | collective-permute-start | bytes 393224 | tf_op jit(solution)/shard_map/ppermute | solution.py:372
  42.6 0.4 pair_drive.7.refs_2_.refs_3_
  43.1 0.2 carry_on.17.refs_3_
  43.3 2.5 %collective-permute-start.13 = (bf16[4,256,128]{2,1,0:T(8,128)(2,1)S(1)}, bf16[4,256,128]{2,1,0:T(8,128)(2,1)S(1)}, u32[]{:S(2)}, u32[]{:S(2)}) collective-permute-start(bf16[4,256,128]{2,1,0:T(8,128)(2,1)S(1)} %carry_on.17.refs_3_), channel_id=1, source_target_pairs={{0,0},{4,4},{8,16},{12,20},{16,8},{20,12},{24,24},{28,28},{1,1},{5... | collective-permute-start | bytes 786440 | tf_op jit(solution)/shard_map/ppermute | solution.py:372
  45.8 0.4 pair_drive.8.refs_2_.refs_5_
  46.2 0.9 collective-permute-done.6.refs_4_.refs_5_
  47.1 0.1 collective-permute-start.10
  47.2 0.4 collective-permute-start.11
  47.6 4.0 %collective-permute-done.12.refs_3_.refs_4_ = bf16[4,256,128]{2,1,0:T(8,128)(2,1)S(1)} collective-permute-done((bf16[4,256,128]{2,1,0:T(8,128)(2,1)S(1)}, bf16[4,256,128]{2,1,0:T(8,128)(2,1)S(1)}, u32[]{:S(2)}, u32[]{:S(2)}) %collective-permute-start.12) | collective-permute-done | bytes 262176 | tf_op jit(solution)/shard_map/ppermute | solution.py:350
  51.6 0.2 carry_on.19.refs_3_
  51.8 2.7 %collective-permute-start.16 = (bf16[4,256,128]{2,1,0:T(8,128)(2,1)S(1)}, bf16[4,256,128]{2,1,0:T(8,128)(2,1)S(1)}, u32[]{:S(2)}, u32[]{:S(2)}) collective-permute-start(bf16[4,256,128]{2,1,0:T(8,128)(2,1)S(1)} %carry_on.19.refs_3_), channel_id=1, source_target_pairs={{0,0},{4,4},{8,16},{12,20},{16,8},{20,12},{24,24},{28,28},{1,1},{5... | collective-permute-start | bytes 786440 | tf_op jit(solution)/shard_map/ppermute | solution.py:372
  54.5 0.2 pair_drive.9.refs_2_.refs_5_
  54.8 2.1 %collective-permute-done.10.refs_6_.refs_3_.refs_4_ = bf16[4,256,128]{2,1,0:T(8,128)(2,1)S(1)} collective-permute-done((bf16[4,256,128]{2,1,0:T(8,128)(2,1)S(1)}, bf16[4,256,128]{2,1,0:T(8,128)(2,1)S(1)}, u32[]{:S(2)}, u32[]{:S(2)}) %collective-permute-start.10) | collective-permute-done | bytes 262176 | tf_op jit(solution)/shard_map/ppermute | solution.py:350
  57.0 1.3 %states_of.5 = (bf16[2,256,128]{2,1,0:T(8,128)(2,1)S(1)}, bf16[2,256,128]{2,1,0:T(8,128)(2,1)S(1)}) custom-call(s32[1]{0:T(128)} %bitcast.4.refs_0_, f32[256,8]{1,0:T(8,128)S(1)} %coefficients.1.refs_2_.refs_1_, f32[2,256,128]{2,1,0:T(8,128)S(1)} %conv_chunks.6.refs_3_.refs_0_.refs_2_, bf16[2,256,128]{2,1,0:T(8,128)(2,1)} %collective-permute-done.3.refs_1_.refs_3_, ...), custom_call_target="tpu_custom_call" | custom-call | tf_op jit(solution)/shard_map/states_of/pallas_call | solution.py:39
  58.2 0.2 carry_on.21.refs_4_
  58.5 2.6 %collective-permute-start.19 = (bf16[4,256,128]{2,1,0:T(8,128)(2,1)S(1)}, bf16[4,256,128]{2,1,0:T(8,128)(2,1)S(1)}, u32[]{:S(2)}, u32[]{:S(2)}) collective-permute-start(bf16[4,256,128]{2,1,0:T(8,128)(2,1)S(1)} %carry_on.21.refs_4_), channel_id=1, source_target_pairs={{0,0},{4,4},{8,16},{12,20},{16,8},{20,12},{24,24},{28,28},{1,1},{5... | collective-permute-start | bytes 786440 | tf_op jit(solution)/shard_map/ppermute | solution.py:372
  61.1 1.7 %collective-permute-done.16.refs_3_.refs_5_ = bf16[4,256,128]{2,1,0:T(8,128)(2,1)S(1)} collective-permute-done((bf16[4,256,128]{2,1,0:T(8,128)(2,1)S(1)}, bf16[4,256,128]{2,1,0:T(8,128)(2,1)S(1)}, u32[]{:S(2)}, u32[]{:S(2)}) %collective-permute-start.16) | collective-permute-done | bytes 262176 | tf_op jit(solution)/shard_map/ppermute | solution.py:372
  62.9 0.8 collective-permute-done.15.refs_6_.refs_3_.refs_4_
  63.7 0.7 states_of.6
  64.4 0.1 carry_on.23.refs_4_
  64.5 2.2 %collective-permute-done.19.refs_3_.refs_5_ = bf16[4,256,128]{2,1,0:T(8,128)(2,1)S(1)} collective-permute-done((bf16[4,256,128]{2,1,0:T(8,128)(2,1)S(1)}, bf16[4,256,128]{2,1,0:T(8,128)(2,1)S(1)}, u32[]{:S(2)}, u32[]{:S(2)}) %collective-permute-start.19) | collective-permute-done | bytes 262176 | tf_op jit(solution)/shard_map/ppermute | solution.py:372
  66.8 2.8 %collective-permute-start.22 = (bf16[2,256,128]{2,1,0:T(8,128)(2,1)S(1)}, bf16[2,256,128]{2,1,0:T(8,128)(2,1)S(1)}, u32[]{:S(2)}, u32[]{:S(2)}) collective-permute-start(bf16[2,256,128]{2,1,0:T(8,128)(2,1)S(1)} %carry_on.23.refs_4_), channel_id=1, source_target_pairs={{0,0},{4,4},{8,16},{12,20},{16,8},{20,12},{24,24},{28,28},{1,1},{5... | collective-permute-start | bytes 393224 | tf_op jit(solution)/shard_map/ppermute | solution.py:372
  69.6 0.6 collective-permute-start.17
  70.3 0.9 collective-permute-done.18.refs_6_
  71.1 0.7 states_of.7
  71.8 0.7 collective-permute-start.20
  72.5 1.2 %collective-permute-done.22.refs_3_.refs_5_ = bf16[2,256,128]{2,1,0:T(8,128)(2,1)S(1)} collective-permute-done((bf16[2,256,128]{2,1,0:T(8,128)(2,1)S(1)}, bf16[2,256,128]{2,1,0:T(8,128)(2,1)S(1)}, u32[]{:S(2)}, u32[]{:S(2)}) %collective-permute-start.22) | collective-permute-done | bytes 131104 | tf_op jit(solution)/shard_map/ppermute | solution.py:372
  73.8 1.5 %collective-permute-done.21.refs_6_ = bf16[4,256,128]{2,1,0:T(8,128)(2,1)S(1)} collective-permute-done((bf16[4,256,128]{2,1,0:T(8,128)(2,1)S(1)}, bf16[4,256,128]{2,1,0:T(8,128)(2,1)S(1)}, u32[]{:S(2)}, u32[]{:S(2)}) %collective-permute-start.21) | collective-permute-done | bytes 262176 | tf_op jit(solution)/shard_map/ppermute | solution.py:350
  75.3 0.7 states_of.8
  76.0 0.4 collective-permute-start.23
  76.4 1.7 %collective-permute-start.14 = (bf16[2,256,128]{2,1,0:T(8,128)(2,1)S(1)}, bf16[2,256,128]{2,1,0:T(8,128)(2,1)S(1)}, u32[]{:S(2)}, u32[]{:S(2)}) collective-permute-start(bf16[2,256,128]{2,1,0:T(8,128)(2,1)S(1)} %get-tuple-element.39.refs_4_), channel_id=1, source_target_pairs={{0,4},{4,0},{8,12},{12,8},{16,20},{20,16},{24,28},{28,24},{1,5},{5... | collective-permute-start | bytes 393224 | tf_op jit(solution)/shard_map/ppermute | solution.py:363
  78.1 0.6 collective-permute-done.24.refs_6_
  78.8 0.4 states_of.9
  79.1 0.5 collective-permute-start.25
  79.6 3.4 %output_half.2.refs_9_ = bf16[256,32,128]{2,1,0:T(8,128)(2,1)} custom-call(s32[1]{0:T(128)} %bitcast.5.refs_0_, bf16[32,256,128]{2,1,0:T(8,128)(2,1)S(1)} %bitcast.16, bf16[256,256]{1,0:T(8,128)(2,1)S(1)} %copy-done.1, f32[1,256]{1,0:T(1,128)S(1)} %bitcast.18, bf16[2,256,128]{2,1,0:T(8,128)(2,1)S(1)} %get-tuple-element.44.refs_4_, ...), custom_call_target="tpu_custom_call" | custom-call | tf_op jit(solution)/shard_map/output_half/pallas_call | solution.py:39
  83.0 6.4 %collective-permute-done.14.refs_4_ = bf16[2,256,128]{2,1,0:T(8,128)(2,1)S(1)} collective-permute-done((bf16[2,256,128]{2,1,0:T(8,128)(2,1)S(1)}, bf16[2,256,128]{2,1,0:T(8,128)(2,1)S(1)}, u32[]{:S(2)}, u32[]{:S(2)}) %collective-permute-start.14) | collective-permute-done | bytes 131104 | tf_op jit(solution)/shard_map/ppermute | solution.py:363
  89.4 1.4 %collective-permute-done.25.refs_8_ = bf16[2,256,128]{2,1,0:T(8,128)(2,1)S(1)} collective-permute-done((bf16[2,256,128]{2,1,0:T(8,128)(2,1)S(1)}, bf16[2,256,128]{2,1,0:T(8,128)(2,1)S(1)}, u32[]{:S(2)}, u32[]{:S(2)}) %collective-permute-start.25) | collective-permute-done | bytes 131104 | tf_op jit(solution)/shard_map/ppermute | solution.py:363
  90.8 3.4 %output_half.3 = bf16[256,32,128]{2,1,0:T(8,128)(2,1)} custom-call(s32[1]{0:T(128)} %bitcast.refs_0_, bf16[32,256,128]{2,1,0:T(8,128)(2,1)S(1)} %bitcast.17, bf16[256,256]{1,0:T(8,128)(2,1)S(1)} %copy-done.1, f32[1,256]{1,0:T(1,128)S(1)} %bitcast.19, bf16[2,256,128]{2,1,0:T(8,128)(2,1)S(1)} %collective-permute-done.14.refs_4_, ...), custom_call_target="tpu_custom_call", output_to_operand_aliasing={{}: (9, {})} | custom-call | tf_op jit(solution)/shard_map/output_half/pallas_call | solution.py:39
  (42 shorter events, 0.8 us)
Async XLA Ops:
  0.0 2.5 %copy-start = (bf16[3,3,256,256]{3,2,1,0:T(8,128)(2,1)S(1)}, bf16[3,3,256,256]{3,2,1,0:T(8,128)(2,1)}, u32[]{:S(2)}) copy-start(bf16[3,3,256,256]{3,2,1,0:T(8,128)(2,1)} %refs_3_.7) | copy-start | bytes 3538948
  0.0 2.5 %copy-start.6 = (f32[1,256]{1,0:T(1,128)S(1)}, f32[1,256]{1,0:T(1,128)}, u32[]{:S(2)}) copy-start(f32[1,256]{1,0:T(1,128)} %refs_4_.7) | copy-start | bytes 3076
  4.2 2.0 %collective-permute-start.1 = (bf16[256,128]{1,0:T(8,128)(2,1)S(1)}, bf16[256,128]{1,0:T(8,128)(2,1)S(1)}, u32[]{:S(2)}, u32[]{:S(2)}) collective-permute-start(bf16[256,128]{1,0:T(8,128)(2,1)S(1)} %get-tuple-element.28), channel_id=1, source_target_pairs={{0,3},{1,0},{2,1},{3,2},{4,7},{5,4},{6,5},{7,6},{8,11},{9,8},{10,9... | collective-permute-start | bytes 196616 | tf_op jit(solution)/shard_map/ppermute | solution.py:330
  4.3 4.4 %collective-permute-start.2 = (bf16[256,128]{1,0:T(8,128)(2,1)S(1)}, bf16[256,128]{1,0:T(8,128)(2,1)S(1)}, u32[]{:S(2)}, u32[]{:S(2)}) collective-permute-start(bf16[256,128]{1,0:T(8,128)(2,1)S(1)} %get-tuple-element.29), channel_id=1, source_target_pairs={{0,1},{1,2},{2,3},{3,0},{4,5},{5,6},{6,7},{7,4},{8,9},{9,10},{10,1... | collective-permute-start | bytes 196616 | tf_op jit(solution)/shard_map/ppermute | solution.py:329
  4.8 19.3 %collective-permute-start.3 = (bf16[2,256,128]{2,1,0:T(8,128)(2,1)}, bf16[2,256,128]{2,1,0:T(8,128)(2,1)}, u32[]{:S(2)}, u32[]{:S(2)}) collective-permute-start(bf16[2,256,128]{2,1,0:T(8,128)(2,1)} %get-tuple-element.31), channel_id=1, source_target_pairs={{0,4},{4,0},{8,12},{12,8},{16,20},{20,16},{24,28},{28,24},{1,5},{5... | collective-permute-start | bytes 393224 | tf_op jit(solution)/shard_map/ppermute | solution.py:327
  13.1 0.7 copy-start.2
  13.8 0.7 copy-start.8
  14.5 0.7 copy-start.10
  14.5 14.6 %collective-permute-start.5 = (bf16[4,256,128]{2,1,0:T(8,128)(2,1)}, bf16[4,256,128]{2,1,0:T(8,128)(2,1)S(1)}, u32[]{:S(2)}, u32[]{:S(2)}) collective-permute-start(bf16[4,256,128]{2,1,0:T(8,128)(2,1)} %get-tuple-element.33), channel_id=1, source_target_pairs={{0,4},{4,0},{8,12},{12,8},{16,20},{20,16},{24,28},{28,24},{1,5},{5... | collective-permute-start | bytes 786440 | tf_op jit(solution)/shard_map/ppermute | solution.py:334
  15.2 8.7 %collective-permute-start = (f32[1,256]{1,0:T(1,128)S(1)}, f32[1,256]{1,0:T(1,128)S(1)}, u32[]{:S(2)}, u32[]{:S(2)}) collective-permute-start(f32[1,256]{1,0:T(1,128)S(1)} %get-tuple-element.27), channel_id=1, source_target_pairs={{0,4},{4,0},{8,12},{12,8},{16,20},{20,16},{24,28},{28,24},{1,5},{5... | collective-permute-start | bytes 3080 | tf_op jit(solution)/shard_map/ppermute | solution.py:328
  16.5 26.1 %collective-permute-start.9 = (bf16[4,256,128]{2,1,0:T(8,128)(2,1)}, bf16[4,256,128]{2,1,0:T(8,128)(2,1)S(1)}, u32[]{:S(2)}, u32[]{:S(2)}) collective-permute-start(bf16[4,256,128]{2,1,0:T(8,128)(2,1)} %copy-done.10), channel_id=1, source_target_pairs={{0,4},{4,0},{8,12},{12,8},{16,20},{20,16},{24,28},{28,24},{1,5},{5... | collective-permute-start | bytes 786440 | tf_op jit(solution)/shard_map/ppermute | solution.py:334
  17.2 0.9 copy-start.3
  18.1 7.1 %copy-start.5 = (bf16[256,128]{1,0:T(8,128)(2,1)S(1)}, bf16[256,128]{1,0:T(8,128)(2,1)}, u32[]{:S(2)}) copy-start(bf16[256,128]{1,0:T(8,128)(2,1)} %get-tuple-element.49.refs_5_) | copy-start | bytes 196612
  29.0 1.0 %copy-start.9 = (bf16[4,256,128]{2,1,0:T(8,128)(2,1)S(1)}, bf16[4,256,128]{2,1,0:T(8,128)(2,1)}, u32[]{:S(2)}) copy-start(bf16[4,256,128]{2,1,0:T(8,128)(2,1)} %copy-done.8) | copy-start | bytes 786436
  29.5 13.6 %collective-permute-start.8 = (bf16[4,256,128]{2,1,0:T(8,128)(2,1)S(1)}, bf16[4,256,128]{2,1,0:T(8,128)(2,1)S(1)}, u32[]{:S(2)}, u32[]{:S(2)}) collective-permute-start(bf16[4,256,128]{2,1,0:T(8,128)(2,1)S(1)} %carry_on.14.refs_4_), channel_id=1, source_target_pairs={{0,8},{4,12},{8,0},{12,4},{16,24},{20,28},{24,16},{28,20},{1,9},{5... | collective-permute-start | bytes 786440 | tf_op jit(solution)/shard_map/ppermute | solution.py:350
  30.0 15.8 %collective-permute-start.7 = (bf16[4,256,128]{2,1,0:T(8,128)(2,1)S(1)}, bf16[4,256,128]{2,1,0:T(8,128)(2,1)S(1)}, u32[]{:S(2)}, u32[]{:S(2)}) collective-permute-start(bf16[4,256,128]{2,1,0:T(8,128)(2,1)S(1)} %copy-done.9), channel_id=1, source_target_pairs={{0,4},{4,0},{8,12},{12,8},{16,20},{20,16},{24,28},{28,24},{1,5},{5... | collective-permute-start | bytes 786440 | tf_op jit(solution)/shard_map/ppermute | solution.py:334
  30.5 8.6 %collective-permute-start.4 = (bf16[2,256,128]{2,1,0:T(8,128)(2,1)S(1)}, bf16[2,256,128]{2,1,0:T(8,128)(2,1)S(1)}, u32[]{:S(2)}, u32[]{:S(2)}) collective-permute-start(bf16[2,256,128]{2,1,0:T(8,128)(2,1)S(1)} %carry_on.13.refs_6_), channel_id=1, source_target_pairs={{0,8},{4,12},{8,0},{12,4},{16,24},{20,28},{24,16},{28,20},{1,9},{5... | collective-permute-start | bytes 393224 | tf_op jit(solution)/shard_map/ppermute | solution.py:350
  39.2 7.8 %collective-permute-start.6 = (bf16[2,256,128]{2,1,0:T(8,128)(2,1)S(1)}, bf16[2,256,128]{2,1,0:T(8,128)(2,1)S(1)}, u32[]{:S(2)}, u32[]{:S(2)}) collective-permute-start(bf16[2,256,128]{2,1,0:T(8,128)(2,1)S(1)} %carry_on.15.refs_3_), channel_id=1, source_target_pairs={{0,0},{4,4},{8,16},{12,20},{16,8},{20,12},{24,24},{28,28},{1,1},{5... | collective-permute-start | bytes 393224 | tf_op jit(solution)/shard_map/ppermute | solution.py:372
  43.0 8.6 %collective-permute-start.12 = (bf16[4,256,128]{2,1,0:T(8,128)(2,1)S(1)}, bf16[4,256,128]{2,1,0:T(8,128)(2,1)S(1)}, u32[]{:S(2)}, u32[]{:S(2)}) collective-permute-start(bf16[4,256,128]{2,1,0:T(8,128)(2,1)S(1)} %carry_on.16.refs_4_), channel_id=1, source_target_pairs={{0,8},{4,12},{8,0},{12,4},{16,24},{20,28},{24,16},{28,20},{1,9},{5... | collective-permute-start | bytes 786440 | tf_op jit(solution)/shard_map/ppermute | solution.py:350
  43.3 3.8 %copy-start.4 = (bf16[2,256,128]{2,1,0:T(8,128)(2,1)S(1)}, bf16[2,256,128]{2,1,0:T(8,128)(2,1)}, u32[]{:S(2)}) copy-start(bf16[2,256,128]{2,1,0:T(8,128)(2,1)} %copy-done.2) | copy-start | bytes 393220
  43.3 11.4 %collective-permute-start.13 = (bf16[4,256,128]{2,1,0:T(8,128)(2,1)S(1)}, bf16[4,256,128]{2,1,0:T(8,128)(2,1)S(1)}, u32[]{:S(2)}, u32[]{:S(2)}) collective-permute-start(bf16[4,256,128]{2,1,0:T(8,128)(2,1)S(1)} %carry_on.17.refs_3_), channel_id=1, source_target_pairs={{0,0},{4,4},{8,16},{12,20},{16,8},{20,12},{24,24},{28,28},{1,1},{5... | collective-permute-start | bytes 786440 | tf_op jit(solution)/shard_map/ppermute | solution.py:372
  47.1 9.9 %collective-permute-start.10 = (bf16[4,256,128]{2,1,0:T(8,128)(2,1)S(1)}, bf16[4,256,128]{2,1,0:T(8,128)(2,1)S(1)}, u32[]{:S(2)}, u32[]{:S(2)}) collective-permute-start(bf16[4,256,128]{2,1,0:T(8,128)(2,1)S(1)} %carry_on.18.refs_4_), channel_id=1, source_target_pairs={{0,8},{4,12},{8,0},{12,4},{16,24},{20,28},{24,16},{28,20},{1,9},{5... | collective-permute-start | bytes 786440 | tf_op jit(solution)/shard_map/ppermute | solution.py:350
  47.2 7.3 %collective-permute-start.11 = (bf16[2,256,128]{2,1,0:T(8,128)(2,1)S(1)}, bf16[2,256,128]{2,1,0:T(8,128)(2,1)S(1)}, u32[]{:S(2)}, u32[]{:S(2)}) collective-permute-start(bf16[2,256,128]{2,1,0:T(8,128)(2,1)S(1)} %copy-done.4), channel_id=1, source_target_pairs={{0,4},{4,0},{8,12},{12,8},{16,20},{20,16},{24,28},{28,24},{1,5},{5... | collective-permute-start | bytes 393224 | tf_op jit(solution)/shard_map/ppermute | solution.py:334
  51.8 11.0 %collective-permute-start.16 = (bf16[4,256,128]{2,1,0:T(8,128)(2,1)S(1)}, bf16[4,256,128]{2,1,0:T(8,128)(2,1)S(1)}, u32[]{:S(2)}, u32[]{:S(2)}) collective-permute-start(bf16[4,256,128]{2,1,0:T(8,128)(2,1)S(1)} %carry_on.19.refs_3_), channel_id=1, source_target_pairs={{0,0},{4,4},{8,16},{12,20},{16,8},{20,12},{24,24},{28,28},{1,1},{5... | collective-permute-start | bytes 786440 | tf_op jit(solution)/shard_map/ppermute | solution.py:372
  54.8 8.9 %collective-permute-start.15 = (bf16[4,256,128]{2,1,0:T(8,128)(2,1)S(1)}, bf16[4,256,128]{2,1,0:T(8,128)(2,1)S(1)}, u32[]{:S(2)}, u32[]{:S(2)}) collective-permute-start(bf16[4,256,128]{2,1,0:T(8,128)(2,1)S(1)} %carry_on.20.refs_7_), channel_id=1, source_target_pairs={{0,8},{4,12},{8,0},{12,4},{16,24},{20,28},{24,16},{28,20},{1,9},{5... | collective-permute-start | bytes 786440 | tf_op jit(solution)/shard_map/ppermute | solution.py:350
  58.5 8.3 %collective-permute-start.19 = (bf16[4,256,128]{2,1,0:T(8,128)(2,1)S(1)}, bf16[4,256,128]{2,1,0:T(8,128)(2,1)S(1)}, u32[]{:S(2)}, u32[]{:S(2)}) collective-permute-start(bf16[4,256,128]{2,1,0:T(8,128)(2,1)S(1)} %carry_on.21.refs_4_), channel_id=1, source_target_pairs={{0,0},{4,4},{8,16},{12,20},{16,8},{20,12},{24,24},{28,28},{1,1},{5... | collective-permute-start | bytes 786440 | tf_op jit(solution)/shard_map/ppermute | solution.py:372
  62.8 8.3 %collective-permute-start.18 = (bf16[4,256,128]{2,1,0:T(8,128)(2,1)S(1)}, bf16[4,256,128]{2,1,0:T(8,128)(2,1)S(1)}, u32[]{:S(2)}, u32[]{:S(2)}) collective-permute-start(bf16[4,256,128]{2,1,0:T(8,128)(2,1)S(1)} %carry_on.22.refs_7_), channel_id=1, source_target_pairs={{0,8},{4,12},{8,0},{12,4},{16,24},{20,28},{24,16},{28,20},{1,9},{5... | collective-permute-start | bytes 786440 | tf_op jit(solution)/shard_map/ppermute | solution.py:350
  66.8 8.6 %collective-permute-start.21 = (bf16[4,256,128]{2,1,0:T(8,128)(2,1)S(1)}, bf16[4,256,128]{2,1,0:T(8,128)(2,1)S(1)}, u32[]{:S(2)}, u32[]{:S(2)}) collective-permute-start(bf16[4,256,128]{2,1,0:T(8,128)(2,1)S(1)} %carry_on.24.refs_7_), channel_id=1, source_target_pairs={{0,8},{4,12},{8,0},{12,4},{16,24},{20,28},{24,16},{28,20},{1,9},{5... | collective-permute-start | bytes 786440 | tf_op jit(solution)/shard_map/ppermute | solution.py:350
  66.8 6.9 %collective-permute-start.22 = (bf16[2,256,128]{2,1,0:T(8,128)(2,1)S(1)}, bf16[2,256,128]{2,1,0:T(8,128)(2,1)S(1)}, u32[]{:S(2)}, u32[]{:S(2)}) collective-permute-start(bf16[2,256,128]{2,1,0:T(8,128)(2,1)S(1)} %carry_on.23.refs_4_), channel_id=1, source_target_pairs={{0,0},{4,4},{8,16},{12,20},{16,8},{20,12},{24,24},{28,28},{1,1},{5... | collective-permute-start | bytes 393224 | tf_op jit(solution)/shard_map/ppermute | solution.py:372
  69.6 19.7 %collective-permute-start.17 = (bf16[4,256,128]{2,1,0:T(8,128)(2,1)S(1)}, bf16[4,256,128]{2,1,0:T(8,128)(2,1)S(1)}, u32[]{:S(2)}, u32[]{:S(2)}) collective-permute-start(bf16[4,256,128]{2,1,0:T(8,128)(2,1)S(1)} %get-tuple-element.40.refs_4_), channel_id=1, source_target_pairs={{0,4},{4,0},{8,12},{12,8},{16,20},{20,16},{24,28},{28,24},{1,5},{5... | collective-permute-start | bytes 786440 | tf_op jit(solution)/shard_map/ppermute | solution.py:363
  71.8 7.8 %copy-start.1 = (bf16[256,256]{1,0:T(8,128)(2,1)S(1)}, bf16[256,256]{1,0:T(8,128)(2,1)}, u32[]{:S(2)}) copy-start(bf16[256,256]{1,0:T(8,128)(2,1)} %refs_2_.3) | copy-start | bytes 393220
  71.8 7.8 %copy-start.7 = (f32[256]{0:T(256)S(1)}, f32[256]{0:T(256)}, u32[]{:S(2)}) copy-start(f32[256]{0:T(256)} %param.8) | copy-start | bytes 3076
  71.8 17.6 %collective-permute-start.20 = (bf16[4,256,128]{2,1,0:T(8,128)(2,1)S(1)}, bf16[4,256,128]{2,1,0:T(8,128)(2,1)S(1)}, u32[]{:S(2)}, u32[]{:S(2)}) collective-permute-start(bf16[4,256,128]{2,1,0:T(8,128)(2,1)S(1)} %get-tuple-element.41.refs_4_), channel_id=1, source_target_pairs={{0,4},{4,0},{8,12},{12,8},{16,20},{20,16},{24,28},{28,24},{1,5},{5... | collective-permute-start | bytes 786440 | tf_op jit(solution)/shard_map/ppermute | solution.py:363
  73.7 5.0 %collective-permute-start.24 = (bf16[2,256,128]{2,1,0:T(8,128)(2,1)S(1)}, bf16[2,256,128]{2,1,0:T(8,128)(2,1)S(1)}, u32[]{:S(2)}, u32[]{:S(2)}) collective-permute-start(bf16[2,256,128]{2,1,0:T(8,128)(2,1)S(1)} %carry_on.25.refs_7_), channel_id=1, source_target_pairs={{0,8},{4,12},{8,0},{12,4},{16,24},{20,28},{24,16},{28,20},{1,9},{5... | collective-permute-start | bytes 393224 | tf_op jit(solution)/shard_map/ppermute | solution.py:350
  76.0 14.8 %collective-permute-start.23 = (bf16[4,256,128]{2,1,0:T(8,128)(2,1)S(1)}, bf16[4,256,128]{2,1,0:T(8,128)(2,1)S(1)}, u32[]{:S(2)}, u32[]{:S(2)}) collective-permute-start(bf16[4,256,128]{2,1,0:T(8,128)(2,1)S(1)} %get-tuple-element.42.refs_7_), channel_id=1, source_target_pairs={{0,4},{4,0},{8,12},{12,8},{16,20},{20,16},{24,28},{28,24},{1,5},{5... | collective-permute-start | bytes 786440 | tf_op jit(solution)/shard_map/ppermute | solution.py:363
  76.4 12.9 %collective-permute-start.14 = (bf16[2,256,128]{2,1,0:T(8,128)(2,1)S(1)}, bf16[2,256,128]{2,1,0:T(8,128)(2,1)S(1)}, u32[]{:S(2)}, u32[]{:S(2)}) collective-permute-start(bf16[2,256,128]{2,1,0:T(8,128)(2,1)S(1)} %get-tuple-element.39.refs_4_), channel_id=1, source_target_pairs={{0,4},{4,0},{8,12},{12,8},{16,20},{20,16},{24,28},{28,24},{1,5},{5... | collective-permute-start | bytes 393224 | tf_op jit(solution)/shard_map/ppermute | solution.py:363
  79.1 11.7 %collective-permute-start.25 = (bf16[2,256,128]{2,1,0:T(8,128)(2,1)S(1)}, bf16[2,256,128]{2,1,0:T(8,128)(2,1)S(1)}, u32[]{:S(2)}, u32[]{:S(2)}) collective-permute-start(bf16[2,256,128]{2,1,0:T(8,128)(2,1)S(1)} %get-tuple-element.43.refs_9_), channel_id=1, source_target_pairs={{0,4},{4,0},{8,12},{12,8},{16,20},{20,16},{24,28},{28,24},{1,5},{5... | collective-permute-start | bytes 393224 | tf_op jit(solution)/shard_map/ppermute | solution.py:363

commit v3 on v2

--- a/solution.py
+++ b/solution.py
@@ -19,9 +19,34 @@
 
 
 def sizes_of(half):
-    if half % 4 or half < 8:
-        return [2] * (half // 2)
-    return [2] + [4] * (half // 4 - 1) + [2]
+    rows = 4 if half % 4 == 0 else 2
+    return [rows] * (half // rows)
+
+
+def row(ref, q, channels):
+    return ref[q * channels : (q + 1) * channels] if len(ref.shape) == 2 else ref[q]
+
+
+PAD = 16
+LANES = 128
+
+
+def split_decays(decay):
+    pieces = []
+    rest = decay
+    for _ in range(3):
+        part = rest.astype(BF16).astype(F32)
+        rest = rest - part
+        pieces += [part[:, i : i + LANES] for i in range(0, decay.shape[1], LANES)]
+    pieces += [jnp.zeros_like(pieces[0])] * (PAD - len(pieces))
+    return jnp.concatenate(pieces, axis=0).astype(BF16)
+
+
+def join_decays(block, count):
+    block = block.astype(F32)
+    n = count // LANES
+    parts = [block[i : i + 1] + block[n + i : n + i + 1] + block[2 * n + i : 2 * n + i + 1] for i in range(n)]
+    return jnp.concatenate(parts, axis=1)
 
 
 def columns(*rows):
@@ -29,40 +54,49 @@
     return jnp.transpose(jnp.concatenate(rows, axis=0))
 
 
-def call(kernel, out_shape, scalars, operands, after, name, mib=16, scratch=(), specs=None, **more):
+TOKEN = jax.ShapeDtypeStruct((8, 128), F32)
+
+
+def call(kernel, out_shape, scalars, operands, after, name, mib=8, scratch=(), specs=None,
+         out_specs=None, **more):
     specs = specs or [VMEM] * len(operands)
-    n = len(scalars) + len(operands)
+    out_specs = out_specs or [VMEM] * len(out_shape)
+    n, outs = len(scalars) + len(operands), len(out_shape)
 
     def body(*refs):
-        kernel(*refs[:n], *refs[n + len(after) :])
+        rest = refs[n + len(after) :]
+        rest[outs][...] = jnp.zeros(TOKEN.shape, TOKEN.dtype)
+        kernel(*refs[:n], *rest[:outs], *rest[outs + 1 :])
 
     return pl.pallas_call(
         body,
-        out_shape=out_shape,
+        out_shape=list(out_shape) + [TOKEN],
         in_specs=[SMEM] * len(scalars) + specs + [ANY] * len(after),
+        out_specs=list(out_specs) + [VMEM],
         scratch_shapes=list(scratch),
         compiler_params=params(mib),
+        cost_estimate=pl.CostEstimate(flops=1, bytes_accessed=1, transcendentals=0),
         name=name,
         **more,
     )(*scalars, *operands, *after)
 
 
-def conv(rows_in, halo, weight, decays, lower, edge, sizes, start, count, dtype, after, edges=False):
+def conv(rows_in, halos, weight, decays, lower, edge, sizes, start, count, dtype, after, edges=False):
     tile_rows, channels, width = rows_in.shape
     states = weight.shape[2]
     half = tile_rows // 2
     mine = sizes[start : start + count]
     before, total = sum(sizes[:start]), sum(mine)
     whole = start + count == len(sizes)
-    assert whole == (halo is not None)
+    assert whole == bool(halos)
     out_shape = [jax.ShapeDtypeStruct((n, states, width), dtype) for n in mine]
     if edges:
         out_shape += [jax.ShapeDtypeStruct((channels, width), rows_in.dtype)] * 2
-        out_shape += [jax.ShapeDtypeStruct(decays.shape, decays.dtype)]
+        out_shape[0] = jax.ShapeDtypeStruct((mine[0] * states + PAD, width), dtype)
 
     def kernel(lower_ref, edge_ref, rows_ref, weight_ref, decays_ref, *refs):
         refs = list(refs)
-        halo_ref = refs.pop(0) if whole else None
+        above, below = (refs.pop(0), refs.pop(0)) if whole else (None, None)
         outs, (rows, shifted, sems) = refs[:-3], refs[-3:]
         low = lower_ref[0]
         copied = total + 1 if whole else total + 2
@@ -79,11 +113,12 @@
             bottom = pltpu.make_async_copy(rows_ref.at[tile_rows - 1], outs[count + 1], sems.at[2])
             top.start()
             bottom.start()
-            outs[count + 2][...] = decays_ref[...]
+            outs[0][mine[0] * states :] = split_decays(decays_ref[...])
         main.wait()
         if whole:
             slot = low * (total + 1)
-            rows[slot] = jnp.where(edge_ref[0] == 1, jnp.zeros_like(halo_ref), halo_ref[...])
+            halo = jnp.where(low == 1, below[...].astype(F32), above[...].astype(F32))
+            rows[slot] = jnp.where(edge_ref[0] == 1, 0.0, halo).astype(rows.dtype)
         lane = lax.broadcasted_iota(jnp.int32, (channels, width), 1)
 
         def shift(r, carry):
@@ -112,36 +147,36 @@
                     axis=0,
                 )
                 drive = gain * jnp.dot(taps, window, preferred_element_type=F32)
-                outs[n][q] = drive[:, :width].astype(dtype)
-                outs[n][q + 1] = drive[:, width:].astype(dtype)
+                for i in range(2):
+                    value = drive[:, i * width : (i + 1) * width].astype(dtype)
+                    if len(outs[n].shape) == 2:
+                        outs[n][(q + i) * states : (q + i + 1) * states] = value
+                    else:
+                        outs[n][q + i] = value
             done += size
         if edges:
             top.wait()
             bottom.wait()
 
-    out_specs = [VMEM] * count + ([ANY, ANY, VMEM] if edges else [])
+    out_specs = [VMEM] * count + ([ANY, ANY] if edges else [])
     return call(
         kernel, out_shape, [lower, edge],
-        [rows_in, weight, decays] + ([halo] if whole else []), after, "conv_chunks", 40,
+        [rows_in, weight, decays] + list(halos), after, "conv_chunks", 14,
         scratch=[
             pltpu.VMEM((total + 2, channels, width), rows_in.dtype),
             pltpu.VMEM((total + 2, 3 * channels, width), rows_in.dtype),
             pltpu.SemaphoreType.DMA((3,)),
         ],
-        specs=[ANY, VMEM, VMEM] + ([VMEM] if whole else []),
+        specs=[ANY, VMEM, VMEM] + [VMEM] * len(halos),
         out_specs=out_specs,
-        cost_estimate=pl.CostEstimate(
-            flops=18 * channels * states * width * total,
-            bytes_accessed=4 * total * channels * width + weight.size * 2,
-            transcendentals=0,
-        ),
-    )
-
-
-def coefficients(odd, own_decay, other_decay, after):
-    def kernel(odd_ref, own_ref, other_ref, out):
+    )
+
+
+def coefficients(odd, own_decay, first, after):
+    def kernel(odd_ref, own_ref, first_ref, out):
         is_odd = jnp.full(own_ref.shape, odd_ref[0], jnp.int32) == 1
-        own, other = own_ref[...], other_ref[...]
+        own = own_ref[...]
+        other = join_decays(first_ref[first.shape[0] - PAD :], own.shape[1])
         both = own * other
         one, zero = jnp.ones_like(own), jnp.zeros_like(own)
         out[...] = columns(
@@ -155,16 +190,18 @@
         )
 
     shape = jax.ShapeDtypeStruct((own_decay.shape[1], 8), F32)
-    return call(kernel, shape, [odd], [own_decay, other_decay], after, "coefficients")
+    return call(kernel, [shape], [odd], [own_decay, first], after, "coefficients")
 
 
 def pair_drive(keep, other, coefs, after):
     def kernel(keep_ref, other_ref, coefs_ref, out):
         for q in range(keep.shape[0]):
-            out[q] = coefs_ref[:, 1:2] * keep_ref[q] + coefs_ref[:, 2:3] * other_ref[q].astype(F32)
+            out[q] = coefs_ref[:, 1:2] * keep_ref[q] + coefs_ref[:, 2:3] * row(
+                other_ref, q, keep.shape[1]
+            ).astype(F32)
 
     shape = jax.ShapeDtypeStruct(keep.shape, F32)
-    return call(kernel, shape, [], [keep, other, coefs], after, "pair_drive")
+    return call(kernel, [shape], [], [keep, other, coefs], after, "pair_drive")
 
 
 def carry_on(group, coefs, drives, carry, after):
@@ -186,7 +223,7 @@
                     out[q] = total.astype(BF16)
 
     operands = [coefs] + [drives[g] for g in groups] + ([carry] if carry is not None else [])
-    return call(kernel, shape, [group], operands, after, "carry_on")
+    return call(kernel, [shape], [group], operands, after, "carry_on")
 
 
 def states_of(group, coefs, keep, other, carries, after):
@@ -197,7 +234,7 @@
 
         def settle(carry_ref):
             for q in range(keep.shape[0]):
-                held, sent = keep_ref[q], other_ref[q].astype(F32)
+                held, sent = keep_ref[q], row(other_ref, q, keep.shape[1]).astype(F32)
                 mine = held + coefs_ref[:, 5:6] * sent
                 theirs = coefs_ref[:, 6:7] * held + sent
                 if carry_ref is not None:
@@ -277,8 +314,8 @@
         more["input_output_aliases"] = {len(operands): 0}
     return call(
         kernel,
-        jax.ShapeDtypeStruct((channels, tile_rows, width), dtype),
-        [lower], operands, after, "output_half", 40,
+        [jax.ShapeDtypeStruct((channels, tile_rows, width), dtype)],
+        [lower], operands, after, "output_half", 10,
         scratch=[
             pltpu.VMEM((half, channels, width), rows_in.dtype),
             pltpu.VMEM((half, channels, width), BF16),
@@ -287,7 +324,7 @@
             pltpu.SemaphoreType.DMA((count + 2,)),
         ],
         specs=[ANY, VMEM, VMEM] + [ANY] * (len(operands) - 3),
-        out_specs=ANY,
+        out_specs=[ANY],
         **more,
     )
 
@@ -308,8 +345,11 @@
     swap = [(i, i + 1 - 2 * (i % 2)) for i in range(frames)]
     even_hop = [(i, i + 2 if (i // 2) % 2 == 0 else i - 2) for i in range(frames)]
     odd_hop = [
-        (i, i if i // 2 in (0, groups - 1) else (i + 2 if (i // 2) % 2 else i - 2))
+        (i * spaces + j, i * spaces + j + 1 - 2 * (j % 2))
+        if i // 2 in (0, groups - 1)
+        else (i * spaces + j, (i + 2 if (i // 2) % 2 else i - 2) * spaces + j)
         for i in range(frames)
+        for j in range(spaces)
     ]
     down = [(i, (i + 1) % spaces) for i in range(spaces)]
     up = [(i, (i - 1) % spaces) for i in range(spaces)]
@@ -323,22 +363,19 @@
         conv, rows, weight=conv_weight, decays=decays, lower=odd,
         edge=jnp.where(is_even, is_top, is_bottom), sizes=sizes, dtype=F32,
     )
-    first, top, bottom, decay = sent(halo=None, start=0, count=1, after=[], edges=True)
-    others = [lax.ppermute(first, "tm", swap)]
-    other_decay = lax.ppermute(decay, "tm", swap)
-    from_low = lax.ppermute(bottom, "space", down)
-    from_high = lax.ppermute(top, "space", up)
-    halo_sent = jnp.where(is_even, from_high, from_low)
-    halo_kept = jnp.where(is_even, from_low, from_high)
-    rest = sent(halo=halo_sent, start=1, count=chunks - 1, after=[])
+    early = 2
+    *mine, top, bottom, token = sent(halos=[], start=0, count=early, after=[], edges=True)
+    others = [lax.ppermute(value, "tm", swap) for value in mine]
+    halos = [lax.ppermute(bottom, "space", down), lax.ppermute(top, "space", up)]
+    *held, token = kept(halos=[], start=0, count=1, after=[token])
+    *rest, token = sent(halos=halos, start=early, count=chunks - early, after=[token])
     others += [lax.ppermute(value, "tm", swap) for value in rest]
-    held = list(kept(halo=None, start=0, count=1, after=[rest[-1]]))
-    coefs = coefficients(odd, decays, other_decay, [held[-1]])
+    coefs, token = coefficients(odd, decays, others[0], [token])
 
     lag = 3 * ((groups - 2) // 2) + 1
     drives, evens, odds, own, back = [], {}, {}, [], []
-    drives.append(pair_drive(held[0], others[0], coefs, []))
-    after = [drives[0]]
+    drive, token = pair_drive(held[0], others[0], coefs, [token])
+    drives.append(drive)
     for step in range(chunks + lag):
         ready = {
             g: drives[step - 3 * (g // 2)]
@@ -346,39 +383,37 @@
             if 0 <= step - 3 * (g // 2) < chunks
         }
         if ready:
-            value = carry_on(group, coefs, ready, odds.get(step - 2), after)
+            value, token = carry_on(group, coefs, ready, odds.get(step - 2), [token])
             evens[step] = lax.ppermute(value, "tm", even_hop)
-            after = [value]
         if step == 0:
-            held += kept(halo=halo_kept, start=1, count=chunks - 1, after=after)
-            after = [held[-1]]
+            *more, token = kept(halos=halos, start=1, count=chunks - 1, after=[token])
+            held += more
+        if step + 1 < chunks:
+            drive, token = pair_drive(held[step + 1], others[step + 1], coefs, [token])
+            drives.append(drive)
         k = step - lag
         if k >= 0:
             carries = [
                 evens[k + 3 * ((g - 1) // 2)] if g % 2 else odds[k + 1 + 3 * ((g - 2) // 2)]
                 for g in range(1, groups)
             ]
-            mine, theirs = states_of(group, coefs, held[k], others[k], carries, after)
+            after = [token] + ([back[k - 2]] if k >= 2 else [])
+            mine, theirs, token = states_of(group, coefs, held[k], others[k], carries, after)
             own.append(mine)
             back.append(lax.ppermute(theirs, "tm", swap))
-            after = [theirs]
         ready = {
             g: drives[step - 1 - 3 * ((g - 1) // 2)]
             for g in range(1, groups - 1, 2)
             if 0 <= step - 1 - 3 * ((g - 1) // 2) < chunks
         }
         if ready:
-            value = carry_on(group, coefs, ready, evens[step - 1], after)
-            odds[step] = lax.ppermute(value, "tm", odd_hop)
-            after = [value]
-        if step + 1 < chunks:
-            drives.append(pair_drive(held[step + 1], others[step + 1], coefs, after))
-            after = [drives[-1]]
+            value, token = carry_on(group, coefs, ready, evens[step - 1], [token])
+            odds[step] = lax.ppermute(value, ("tm", "space"), odd_hop)
 
     skip = skip_gain[None]
     dtype = frames_in.dtype
-    half_done = output_half(odd, rows, out_weight, skip, own, None, after, dtype)
-    result = output_half(even, rows, out_weight, skip, back, half_done, [], dtype)
+    half_done, token = output_half(odd, rows, out_weight, skip, own, None, [token], dtype)
+    result, token = output_half(even, rows, out_weight, skip, back, half_done, [token], dtype)
     return result[None]
 
 

time: 94.6 us -> 76.6 us (0.81)
  the two profiles are of different devices: /device:TPU:14 before, /device:TPU:0 now
where the time goes in v3:
time: 76.6 us; the launch traced here: 76.4 us
  starting transfers between devices  27.9 us (36%)
  Pallas kernels  23.8 us (31%)
  waiting for transfers between devices  20.8 us (27%)
  local copies, waits for them, and re-layouts  3.31 us (4%)
    pallas_call x26, Pallas kernels, call(): pl.pallas_call(body, out_shape=list(out_shape) + [TOKEN], in_specs=[SMEM]...  23.8 us
    ppermute x7, starting transfers between devices, on_device(): evens[step] = lax.ppermute(value, 'tm', even_hop)  18.1 us
    ppermute x7, waiting for transfers between devices, on_device(): evens[step] = lax.ppermute(value, 'tm', even_hop)  9.99 us
    ppermute x4, waiting for transfers between devices, on_device(): back.append(lax.ppermute(theirs, 'tm', swap))  9.13 us
    unnamed x13, local copies, waits for them, and re-layouts  3.31 us
    ppermute x2, starting transfers between devices, on_device(): others = [lax.ppermute(value, 'tm', swap) for value in mine]  3.1 us
    ppermute x2, starting transfers between devices, on_device(): others += [lax.ppermute(value, 'tm', swap) for value in rest]  2.53 us
    ppermute x4, starting transfers between devices, on_device(): back.append(lax.ppermute(theirs, 'tm', swap))  2.14 us
  transfers between devices with their start and end apart: 21, of which 10 were waited for; matrix products, arithmetic and copies ran while one was open for 0% of the time, Pallas kernels for 22%

profile of v3, /device:TPU:0, one launch (start us, length us, event | category | flops | bytes accessed | tf_op | source)
XLA Modules:
  0.0 76.4 jit_solution(2626330047129753413)
XLA Ops:
  0.0 2.5 %copy.9 = bf16[1,256,32,128]{3,1,2,0:T(8,128)(2,1)S(1)} copy(bf16[1,256,32,128]{3,2,1,0:T(8,128)(2,1)} %param.5) | data formatting | bytes 4194304 | tf_op args[0]
  2.5 3.1 %conv_chunks.4 = (bf16[1040,128]{1,0:T(8,128)(2,1)}, bf16[4,256,128]{2,1,0:T(8,128)(2,1)}, bf16[256,128]{1,0:T(8,128)(2,1)}, bf16[256,128]{1,0:T(8,128)(2,1)}, f32[8,128]{1,0:T(8,128)S(1)}) custom-call(s32[1]{0:T(128)} %bitcast.refs_0_, s32[1]{0:T(128)} %bitcast.6.refs_1_, bf16[32,256,128]{2,1,0:T(8,128)(2,1)S(1)} %bitcast.12, ...), custom_call_target="tpu_custom_call" | custom-call | flops 1 | bytes 1 | tf_op jit(solution)/shard_map/conv_chunks/pallas_call | solution.py:71
  5.7 3.0 %collective-permute-start = (bf16[1040,128]{1,0:T(8,128)(2,1)}, bf16[1040,128]{1,0:T(8,128)(2,1)S(1)}, u32[]{:S(2)}, u32[]{:S(2)}) collective-permute-start(bf16[1040,128]{1,0:T(8,128)(2,1)} %get-tuple-element.66), channel_id=1, source_target_pairs={{0,4},{4,0},{8,12},{12,8},{16,20},{20,16},{24,28},{28,24},{1,5},{5... | collective-permute-start | bytes 798728 | tf_op jit(solution)/shard_map/ppermute | solution.py:368
  8.7 0.0 collective-permute-start.1
  8.7 1.7 %collective-permute-start.2 = (bf16[256,128]{1,0:T(8,128)(2,1)}, bf16[256,128]{1,0:T(8,128)(2,1)}, u32[]{:S(2)}, u32[]{:S(2)}) collective-permute-start(bf16[256,128]{1,0:T(8,128)(2,1)} %get-tuple-element.68), channel_id=1, source_target_pairs={{0,3},{1,0},{2,1},{3,2},{4,7},{5,4},{6,5},{7,6},{8,11},{9,8},{10,9... | collective-permute-start | bytes 196616 | tf_op jit(solution)/shard_map/ppermute | solution.py:369
  10.5 0.1 collective-permute-start.5
  10.5 1.4 %conv_chunks.5 = (f32[4,256,128]{2,1,0:T(8,128)S(1)}, f32[8,128]{1,0:T(8,128)S(1)}) custom-call(s32[1]{0:T(128)} %bitcast.5.refs_0_, s32[1]{0:T(128)} %bitcast.8.refs_1_, bf16[32,256,128]{2,1,0:T(8,128)(2,1)S(1)} %bitcast.13, bf16[3,3,256,256]{3,2,1,0:T(8,128)(2,1)S(1)} %copy-done, f32[1,256]{1,0:T(1,128)S(1)} %copy-done.4, ...), custom_call_target="tpu_custom_call" | custom-call | flops 1 | bytes 1 | tf_op jit(solution)/shard_map/conv_chunks/pallas_call | solution.py:71
  11.9 0.0 copy-start.1
  12.0 0.8 %copy-done.1 = f32[4,256,128]{2,1,0:T(8,128)} copy-done((f32[4,256,128]{2,1,0:T(8,128)}, f32[4,256,128]{2,1,0:T(8,128)S(1)}, u32[]{:S(2)}) %copy-start.1) | copy-done | bytes 524312
  12.7 0.0 collective-permute-done.1.refs_5_
  12.8 3.2 %conv_chunks.6 = (bf16[4,256,128]{2,1,0:T(8,128)(2,1)S(1)}, bf16[4,256,128]{2,1,0:T(8,128)(2,1)S(1)}, f32[8,128]{1,0:T(8,128)S(1)}) custom-call(s32[1]{0:T(128)} %bitcast.refs_0_, s32[1]{0:T(128)} %bitcast.6.refs_1_, bf16[32,256,128]{2,1,0:T(8,128)(2,1)S(1)} %bitcast.14, bf16[3,3,256,256]{3,2,1,0:T(8,128)(2,1)S(1)} %copy-done, f32[1,256]{1,0:T(1,128)S(1)} %copy-done.4, ...), custom_call_target="tpu_custom_call" | custom-call | flops 1 | bytes 1 | tf_op jit(solution)/shard_map/conv_chunks/pallas_call | solution.py:71
  15.9 2.0 %collective-permute-start.4 = (bf16[4,256,128]{2,1,0:T(8,128)(2,1)S(1)}, bf16[4,256,128]{2,1,0:T(8,128)(2,1)S(1)}, u32[]{:S(2)}, u32[]{:S(2)}) collective-permute-start(bf16[4,256,128]{2,1,0:T(8,128)(2,1)S(1)} %get-tuple-element.80), channel_id=1, source_target_pairs={{0,4},{4,0},{8,12},{12,8},{16,20},{20,16},{24,28},{28,24},{1,5},{5... | collective-permute-start | bytes 786440 | tf_op jit(solution)/shard_map/ppermute | solution.py:372
  18.0 0.0 collective-permute-done.refs_2_.refs_1_.refs_3_
  18.0 0.1 coefficients.1
  18.1 0.3 pair_drive.4
  18.5 0.1 carry_on.11
  18.5 1.6 %collective-permute-start.3 = (bf16[4,256,128]{2,1,0:T(8,128)(2,1)S(1)}, bf16[4,256,128]{2,1,0:T(8,128)(2,1)S(1)}, u32[]{:S(2)}, u32[]{:S(2)}) collective-permute-start(bf16[4,256,128]{2,1,0:T(8,128)(2,1)S(1)} %get-tuple-element.77), channel_id=1, source_target_pairs={{0,8},{4,12},{8,0},{12,4},{16,24},{20,28},{24,16},{28,20},{1,9},{5... | collective-permute-start | bytes 786440 | tf_op jit(solution)/shard_map/ppermute | solution.py:387
  20.2 0.5 collective-permute-start.7
  20.7 4.0 %conv_chunks.7 = (f32[4,256,128]{2,1,0:T(8,128)S(1)}, f32[4,256,128]{2,1,0:T(8,128)S(1)}, f32[4,256,128]{2,1,0:T(8,128)S(1)}, f32[8,128]{1,0:T(8,128)S(1)}) custom-call(s32[1]{0:T(128)} %bitcast.5.refs_0_, s32[1]{0:T(128)} %bitcast.8.refs_1_, bf16[32,256,128]{2,1,0:T(8,128)(2,1)S(1)} %bitcast.15, bf16[3,3,256,256]{3,2,1,0:T(8,128)(2,1)S(1)} %copy-done, ...), custom_call_target="tpu_custom_call" | custom-call | flops 1 | bytes 1 | tf_op jit(solution)/shard_map/conv_chunks/pallas_call | solution.py:71
  24.7 0.0 collective-permute-done.5.refs_1_.refs_3_
  24.7 1.3 %pair_drive.5 = (f32[4,256,128]{2,1,0:T(8,128)S(1)}, f32[8,128]{1,0:T(8,128)S(1)}) custom-call(f32[4,256,128]{2,1,0:T(8,128)S(1)} %get-tuple-element.81.refs_0_.refs_2_, bf16[4,256,128]{2,1,0:T(8,128)(2,1)} %collective-permute-done.5.refs_1_.refs_3_, f32[256,8]{1,0:T(8,128)S(1)} %get-tuple-element.72.refs_2_.refs_1_, f32[8,128]{1,0:T(8,128)S(1)} %get-tuple-element.83.refs_3_), custom_call_target="tpu_custom_call" | custom-call | flops 1 | bytes 1 | tf_op jit(solution)/shard_map/pair_drive/pallas_call | solution.py:71
  26.0 0.1 carry_on.12
  26.1 0.2 collective-permute-start.8
  26.3 0.8 %collective-permute-done.4.refs_1_.refs_3_ = bf16[4,256,128]{2,1,0:T(8,128)(2,1)S(1)} collective-permute-done((bf16[4,256,128]{2,1,0:T(8,128)(2,1)S(1)}, bf16[4,256,128]{2,1,0:T(8,128)(2,1)S(1)}, u32[]{:S(2)}, u32[]{:S(2)}) %collective-permute-start.4) | collective-permute-done | bytes 262176 | tf_op jit(solution)/shard_map/ppermute | solution.py:372
  27.1 0.3 pair_drive.6
  27.5 0.1 collective-permute-start.6
  27.6 0.1 carry_on.14
  27.7 3.6 %collective-permute-start.11 = (bf16[4,256,128]{2,1,0:T(8,128)(2,1)S(1)}, bf16[4,256,128]{2,1,0:T(8,128)(2,1)S(1)}, u32[]{:S(2)}, u32[]{:S(2)}) collective-permute-start(bf16[4,256,128]{2,1,0:T(8,128)(2,1)S(1)} %get-tuple-element.100), channel_id=1, source_target_pairs={{0,8},{4,12},{8,0},{12,4},{16,24},{20,28},{24,16},{28,20},{1,9},{5... | collective-permute-start | bytes 786440 | tf_op jit(solution)/shard_map/ppermute | solution.py:387
  31.3 0.9 %collective-permute-done.7.refs_1_.refs_3_ = bf16[4,256,128]{2,1,0:T(8,128)(2,1)S(1)} collective-permute-done((bf16[4,256,128]{2,1,0:T(8,128)(2,1)S(1)}, bf16[4,256,128]{2,1,0:T(8,128)(2,1)S(1)}, u32[]{:S(2)}, u32[]{:S(2)}) %collective-permute-start.7) | collective-permute-done | bytes 262176 | tf_op jit(solution)/shard_map/ppermute | solution.py:372
  32.2 0.3 pair_drive.7
  32.5 2.7 %collective-permute-done.8.refs_3_.refs_4_ = bf16[4,256,128]{2,1,0:T(8,128)(2,1)S(1)} collective-permute-done((bf16[4,256,128]{2,1,0:T(8,128)(2,1)S(1)}, bf16[4,256,128]{2,1,0:T(8,128)(2,1)S(1)}, u32[]{:S(2)}, u32[]{:S(2)}) %collective-permute-start.8) | collective-permute-done | bytes 262176 | tf_op jit(solution)/shard_map/ppermute | solution.py:387
  35.3 0.1 collective-permute-start.10
  35.4 0.0 collective-permute-done.6.refs_4_.refs_5_
  35.4 0.1 carry_on.16
  35.4 3.2 %collective-permute-start.9 = (bf16[4,256,128]{2,1,0:T(8,128)(2,1)S(1)}, bf16[4,256,128]{2,1,0:T(8,128)(2,1)S(1)}, u32[]{:S(2)}, u32[]{:S(2)}) collective-permute-start(bf16[4,256,128]{2,1,0:T(8,128)(2,1)S(1)} %get-tuple-element.98), channel_id=1, source_target_pairs={{0,8},{4,12},{8,0},{12,4},{16,24},{20,28},{24,16},{28,20},{1,9},{5... | collective-permute-start | bytes 786440 | tf_op jit(solution)/shard_map/ppermute | solution.py:387
  38.6 2.2 %collective-permute-done.11.refs_3_.refs_4_ = bf16[4,256,128]{2,1,0:T(8,128)(2,1)S(1)} collective-permute-done((bf16[4,256,128]{2,1,0:T(8,128)(2,1)S(1)}, bf16[4,256,128]{2,1,0:T(8,128)(2,1)S(1)}, u32[]{:S(2)}, u32[]{:S(2)}) %collective-permute-start.11) | collective-permute-done | bytes 262176 | tf_op jit(solution)/shard_map/ppermute | solution.py:387
  40.9 0.1 collective-permute-start.14
  41.0 0.0 collective-permute-done.10.refs_3_.refs_5_
  41.0 3.2 %collective-permute-start.13 = (bf16[4,256,128]{2,1,0:T(8,128)(2,1)S(1)}, bf16[4,256,128]{2,1,0:T(8,128)(2,1)S(1)}, u32[]{:S(2)}, u32[]{:S(2)}) collective-permute-start(bf16[4,256,128]{2,1,0:T(8,128)(2,1)S(1)} %get-tuple-element.105), channel_id=1, source_target_pairs={{0,8},{4,12},{8,0},{12,4},{16,24},{20,28},{24,16},{28,20},{1,9},{5... | collective-permute-start | bytes 786440 | tf_op jit(solution)/shard_map/ppermute | solution.py:387
  44.3 2.2 %collective-permute-done.9.refs_6_.refs_3_.refs_4_ = bf16[4,256,128]{2,1,0:T(8,128)(2,1)S(1)} collective-permute-done((bf16[4,256,128]{2,1,0:T(8,128)(2,1)S(1)}, bf16[4,256,128]{2,1,0:T(8,128)(2,1)S(1)}, u32[]{:S(2)}, u32[]{:S(2)}) %collective-permute-start.9) | collective-permute-done | bytes 262176 | tf_op jit(solution)/shard_map/ppermute | solution.py:387
  46.5 0.4 states_of.4
  46.9 0.1 collective-permute-start.17
  47.0 1.1 %collective-permute-start.12 = (bf16[4,256,128]{2,1,0:T(8,128)(2,1)S(1)}, bf16[4,256,128]{2,1,0:T(8,128)(2,1)S(1)}, u32[]{:S(2)}, u32[]{:S(2)}) collective-permute-start(bf16[4,256,128]{2,1,0:T(8,128)(2,1)S(1)} %get-tuple-element.104), channel_id=1, source_target_pairs={{0,4},{4,0},{8,12},{12,8},{16,20},{20,16},{24,28},{28,24},{1,5},{5... | collective-permute-start | bytes 786440 | tf_op jit(solution)/shard_map/ppermute | solution.py:403
  48.1 0.0 collective-permute-done.14.refs_3_.refs_5_
  48.1 4.1 %collective-permute-start.16 = (bf16[4,256,128]{2,1,0:T(8,128)(2,1)S(1)}, bf16[4,256,128]{2,1,0:T(8,128)(2,1)S(1)}, u32[]{:S(2)}, u32[]{:S(2)}) collective-permute-start(bf16[4,256,128]{2,1,0:T(8,128)(2,1)S(1)} %get-tuple-element.111), channel_id=1, source_target_pairs={{0,8},{4,12},{8,0},{12,4},{16,24},{20,28},{24,16},{28,20},{1,9},{5... | collective-permute-start | bytes 786440 | tf_op jit(solution)/shard_map/ppermute | solution.py:387
  52.2 0.0 collective-permute-done.13.refs_6_
  52.2 1.3 %states_of.5 = (bf16[4,256,128]{2,1,0:T(8,128)(2,1)S(1)}, bf16[4,256,128]{2,1,0:T(8,128)(2,1)S(1)}, f32[8,128]{1,0:T(8,128)S(1)}) custom-call(s32[1]{0:T(128)} %bitcast.4.refs_0_, f32[256,8]{1,0:T(8,128)S(1)} %get-tuple-element.72.refs_2_.refs_1_, f32[4,256,128]{2,1,0:T(8,128)S(1)} %get-tuple-element.81.refs_0_.refs_2_, ...), custom_call_target="tpu_custom_call" | custom-call | flops 1 | bytes 1 | tf_op jit(solution)/shard_map/states_of/pallas_call | solution.py:71
  53.5 0.4 collective-permute-start.15
  53.9 0.0 collective-permute-done.17.refs_3_.refs_5_
  54.0 0.0 copy-start.3
  54.0 0.0 copy-start.5
  54.0 2.2 %collective-permute-start.19 = (bf16[4,256,128]{2,1,0:T(8,128)(2,1)S(1)}, bf16[4,256,128]{2,1,0:T(8,128)(2,1)S(1)}, u32[]{:S(2)}, u32[]{:S(2)}) collective-permute-start(bf16[4,256,128]{2,1,0:T(8,128)(2,1)S(1)} %get-tuple-element.116), channel_id=1, source_target_pairs={{0,8},{4,12},{8,0},{12,4},{16,24},{20,28},{24,16},{28,20},{1,9},{5... | collective-permute-start | bytes 786440 | tf_op jit(solution)/shard_map/ppermute | solution.py:387
  56.2 0.0 collective-permute-done.12.refs_8_.refs_4_
  56.2 2.7 %collective-permute-done.16.refs_6_ = bf16[4,256,128]{2,1,0:T(8,128)(2,1)S(1)} collective-permute-done((bf16[4,256,128]{2,1,0:T(8,128)(2,1)S(1)}, bf16[4,256,128]{2,1,0:T(8,128)(2,1)S(1)}, u32[]{:S(2)}, u32[]{:S(2)}) %collective-permute-start.16) | collective-permute-done | bytes 262176 | tf_op jit(solution)/shard_map/ppermute | solution.py:387
  58.9 0.4 states_of.6
  59.3 0.1 collective-permute-start.18
  59.3 3.4 %collective-permute-done.15.refs_8_.refs_5_ = bf16[4,256,128]{2,1,0:T(8,128)(2,1)S(1)} collective-permute-done((bf16[4,256,128]{2,1,0:T(8,128)(2,1)S(1)}, bf16[4,256,128]{2,1,0:T(8,128)(2,1)S(1)}, u32[]{:S(2)}, u32[]{:S(2)}) %collective-permute-start.15) | collective-permute-done | bytes 262176 | tf_op jit(solution)/shard_map/ppermute | solution.py:403
  62.8 0.1 collective-permute-done.19.refs_6_
  62.9 0.4 states_of.7
  63.3 0.6 collective-permute-start.20
  63.8 3.0 %output_half.2 = (bf16[256,32,128]{2,1,0:T(8,128)(2,1)}, f32[8,128]{1,0:T(8,128)S(1)}) custom-call(s32[1]{0:T(128)} %bitcast.5.refs_0_, bf16[32,256,128]{2,1,0:T(8,128)(2,1)S(1)} %bitcast.16, bf16[256,256]{1,0:T(8,128)(2,1)S(1)} %copy-done.3, f32[1,256]{1,0:T(1,128)S(1)} %bitcast.18, bf16[4,256,128]{2,1,0:T(8,128)(2,1)S(1)} %get-tuple-element.119.refs_4_, ...), custom_call_target="tpu_custom_call" | custom-call | flops 1 | bytes 1 | tf_op jit(solution)/shard_map/output_half/pallas_call | solution.py:71
  66.9 1.7 %collective-permute-done.18.refs_6_ = bf16[4,256,128]{2,1,0:T(8,128)(2,1)S(1)} collective-permute-done((bf16[4,256,128]{2,1,0:T(8,128)(2,1)S(1)}, bf16[4,256,128]{2,1,0:T(8,128)(2,1)S(1)}, u32[]{:S(2)}, u32[]{:S(2)}) %collective-permute-start.18) | collective-permute-done | bytes 262176 | tf_op jit(solution)/shard_map/ppermute | solution.py:403
  68.6 4.0 %collective-permute-done.20.refs_7_ = bf16[4,256,128]{2,1,0:T(8,128)(2,1)S(1)} collective-permute-done((bf16[4,256,128]{2,1,0:T(8,128)(2,1)S(1)}, bf16[4,256,128]{2,1,0:T(8,128)(2,1)S(1)}, u32[]{:S(2)}, u32[]{:S(2)}) %collective-permute-start.20) | collective-permute-done | bytes 262176 | tf_op jit(solution)/shard_map/ppermute | solution.py:403
  72.6 3.7 %output_half.3 = (bf16[256,32,128]{2,1,0:T(8,128)(2,1)}, f32[8,128]{1,0:T(8,128)}) custom-call(s32[1]{0:T(128)} %bitcast.refs_0_, bf16[32,256,128]{2,1,0:T(8,128)(2,1)S(1)} %bitcast.17, bf16[256,256]{1,0:T(8,128)(2,1)S(1)} %copy-done.3, f32[1,256]{1,0:T(1,128)S(1)} %bitcast.19, ...), custom_call_target="tpu_custom_call", output_to_operand_aliasing={{0}: (8, {})} | custom-call | flops 1 | bytes 1 | tf_op jit(solution)/shard_map/output_half/pallas_call | solution.py:71
  (17 shorter events, 0.3 us)
Async XLA Ops:
  0.0 2.5 %copy-start = (bf16[3,3,256,256]{3,2,1,0:T(8,128)(2,1)S(1)}, bf16[3,3,256,256]{3,2,1,0:T(8,128)(2,1)}, u32[]{:S(2)}) copy-start(bf16[3,3,256,256]{3,2,1,0:T(8,128)(2,1)} %refs_3_.7) | copy-start | bytes 3538948
  0.0 2.5 %copy-start.4 = (f32[1,256]{1,0:T(1,128)S(1)}, f32[1,256]{1,0:T(1,128)}, u32[]{:S(2)}) copy-start(f32[1,256]{1,0:T(1,128)} %refs_4_.7) | copy-start | bytes 3076
  5.7 12.3 %collective-permute-start = (bf16[1040,128]{1,0:T(8,128)(2,1)}, bf16[1040,128]{1,0:T(8,128)(2,1)S(1)}, u32[]{:S(2)}, u32[]{:S(2)}) collective-permute-start(bf16[1040,128]{1,0:T(8,128)(2,1)} %get-tuple-element.66), channel_id=1, source_target_pairs={{0,4},{4,0},{8,12},{12,8},{16,20},{20,16},{24,28},{28,24},{1,5},{5... | collective-permute-start | bytes 798728 | tf_op jit(solution)/shard_map/ppermute | solution.py:368
  8.7 4.0 %collective-permute-start.1 = (bf16[256,128]{1,0:T(8,128)(2,1)}, bf16[256,128]{1,0:T(8,128)(2,1)}, u32[]{:S(2)}, u32[]{:S(2)}) collective-permute-start(bf16[256,128]{1,0:T(8,128)(2,1)} %get-tuple-element.67), channel_id=1, source_target_pairs={{0,1},{1,2},{2,3},{3,0},{4,5},{5,6},{6,7},{7,4},{8,9},{9,10},{10,1... | collective-permute-start | bytes 196616 | tf_op jit(solution)/shard_map/ppermute | solution.py:369
  8.7 4.0 %collective-permute-start.2 = (bf16[256,128]{1,0:T(8,128)(2,1)}, bf16[256,128]{1,0:T(8,128)(2,1)}, u32[]{:S(2)}, u32[]{:S(2)}) collective-permute-start(bf16[256,128]{1,0:T(8,128)(2,1)} %get-tuple-element.68), channel_id=1, source_target_pairs={{0,3},{1,0},{2,1},{3,2},{4,7},{5,4},{6,5},{7,6},{8,11},{9,8},{10,9... | collective-permute-start | bytes 196616 | tf_op jit(solution)/shard_map/ppermute | solution.py:369
  10.5 14.2 %collective-permute-start.5 = (bf16[4,256,128]{2,1,0:T(8,128)(2,1)}, bf16[4,256,128]{2,1,0:T(8,128)(2,1)}, u32[]{:S(2)}, u32[]{:S(2)}) collective-permute-start(bf16[4,256,128]{2,1,0:T(8,128)(2,1)} %get-tuple-element.82), channel_id=1, source_target_pairs={{0,4},{4,0},{8,12},{12,8},{16,20},{20,16},{24,28},{28,24},{1,5},{5... | collective-permute-start | bytes 786440 | tf_op jit(solution)/shard_map/ppermute | solution.py:368
  11.9 0.8 %copy-start.1 = (f32[4,256,128]{2,1,0:T(8,128)}, f32[4,256,128]{2,1,0:T(8,128)S(1)}, u32[]{:S(2)}) copy-start(f32[4,256,128]{2,1,0:T(8,128)S(1)} %get-tuple-element.73.refs_0_.refs_2_) | copy-start | bytes 1572868
  12.7 5.4 %copy-start.2 = (f32[4,256,128]{2,1,0:T(8,128)S(1)}, f32[4,256,128]{2,1,0:T(8,128)}, u32[]{:S(2)}) copy-start(f32[4,256,128]{2,1,0:T(8,128)} %copy-done.1) | copy-start | bytes 1572868
  15.9 11.2 %collective-permute-start.4 = (bf16[4,256,128]{2,1,0:T(8,128)(2,1)S(1)}, bf16[4,256,128]{2,1,0:T(8,128)(2,1)S(1)}, u32[]{:S(2)}, u32[]{:S(2)}) collective-permute-start(bf16[4,256,128]{2,1,0:T(8,128)(2,1)S(1)} %get-tuple-element.80), channel_id=1, source_target_pairs={{0,4},{4,0},{8,12},{12,8},{16,20},{20,16},{24,28},{28,24},{1,5},{5... | collective-permute-start | bytes 786440 | tf_op jit(solution)/shard_map/ppermute | solution.py:372
  18.5 8.9 %collective-permute-start.3 = (bf16[4,256,128]{2,1,0:T(8,128)(2,1)S(1)}, bf16[4,256,128]{2,1,0:T(8,128)(2,1)S(1)}, u32[]{:S(2)}, u32[]{:S(2)}) collective-permute-start(bf16[4,256,128]{2,1,0:T(8,128)(2,1)S(1)} %get-tuple-element.77), channel_id=1, source_target_pairs={{0,8},{4,12},{8,0},{12,4},{16,24},{20,28},{24,16},{28,20},{1,9},{5... | collective-permute-start | bytes 786440 | tf_op jit(solution)/shard_map/ppermute | solution.py:387
  20.2 12.0 %collective-permute-start.7 = (bf16[4,256,128]{2,1,0:T(8,128)(2,1)S(1)}, bf16[4,256,128]{2,1,0:T(8,128)(2,1)S(1)}, u32[]{:S(2)}, u32[]{:S(2)}) collective-permute-start(bf16[4,256,128]{2,1,0:T(8,128)(2,1)S(1)} %get-tuple-element.90), channel_id=1, source_target_pairs={{0,4},{4,0},{8,12},{12,8},{16,20},{20,16},{24,28},{28,24},{1,5},{5... | collective-permute-start | bytes 786440 | tf_op jit(solution)/shard_map/ppermute | solution.py:372
  26.1 9.2 %collective-permute-start.8 = (bf16[4,256,128]{2,1,0:T(8,128)(2,1)S(1)}, bf16[4,256,128]{2,1,0:T(8,128)(2,1)S(1)}, u32[]{:S(2)}, u32[]{:S(2)}) collective-permute-start(bf16[4,256,128]{2,1,0:T(8,128)(2,1)S(1)} %get-tuple-element.95), channel_id=1, source_target_pairs={{0,8},{4,12},{8,0},{12,4},{16,24},{20,28},{24,16},{28,20},{1,9},{5... | collective-permute-start | bytes 786440 | tf_op jit(solution)/shard_map/ppermute | solution.py:387
  27.5 7.8 %collective-permute-start.6 = (bf16[4,256,128]{2,1,0:T(8,128)(2,1)S(1)}, bf16[4,256,128]{2,1,0:T(8,128)(2,1)S(1)}, u32[]{:S(2)}, u32[]{:S(2)}) collective-permute-start(bf16[4,256,128]{2,1,0:T(8,128)(2,1)S(1)} %get-tuple-element.88), channel_id=1, source_target_pairs={{0,1},{1,0},{2,3},{3,2},{4,5},{5,4},{6,7},{7,6},{8,16},{9,17},{10,... | collective-permute-start | bytes 786440 | tf_op jit(solution)/shard_map/ppermute | solution.py:411
  27.7 13.2 %collective-permute-start.11 = (bf16[4,256,128]{2,1,0:T(8,128)(2,1)S(1)}, bf16[4,256,128]{2,1,0:T(8,128)(2,1)S(1)}, u32[]{:S(2)}, u32[]{:S(2)}) collective-permute-start(bf16[4,256,128]{2,1,0:T(8,128)(2,1)S(1)} %get-tuple-element.100), channel_id=1, source_target_pairs={{0,8},{4,12},{8,0},{12,4},{16,24},{20,28},{24,16},{28,20},{1,9},{5... | collective-permute-start | bytes 786440 | tf_op jit(solution)/shard_map/ppermute | solution.py:387
  35.3 5.7 %collective-permute-start.10 = (bf16[4,256,128]{2,1,0:T(8,128)(2,1)S(1)}, bf16[4,256,128]{2,1,0:T(8,128)(2,1)S(1)}, u32[]{:S(2)}, u32[]{:S(2)}) collective-permute-start(bf16[4,256,128]{2,1,0:T(8,128)(2,1)S(1)} %get-tuple-element.99), channel_id=1, source_target_pairs={{0,1},{1,0},{2,3},{3,2},{4,5},{5,4},{6,7},{7,6},{8,16},{9,17},{10,... | collective-permute-start | bytes 786440 | tf_op jit(solution)/shard_map/ppermute | solution.py:411
  35.4 11.0 %collective-permute-start.9 = (bf16[4,256,128]{2,1,0:T(8,128)(2,1)S(1)}, bf16[4,256,128]{2,1,0:T(8,128)(2,1)S(1)}, u32[]{:S(2)}, u32[]{:S(2)}) collective-permute-start(bf16[4,256,128]{2,1,0:T(8,128)(2,1)S(1)} %get-tuple-element.98), channel_id=1, source_target_pairs={{0,8},{4,12},{8,0},{12,4},{16,24},{20,28},{24,16},{28,20},{1,9},{5... | collective-permute-start | bytes 786440 | tf_op jit(solution)/shard_map/ppermute | solution.py:387
  40.9 7.2 %collective-permute-start.14 = (bf16[4,256,128]{2,1,0:T(8,128)(2,1)S(1)}, bf16[4,256,128]{2,1,0:T(8,128)(2,1)S(1)}, u32[]{:S(2)}, u32[]{:S(2)}) collective-permute-start(bf16[4,256,128]{2,1,0:T(8,128)(2,1)S(1)} %get-tuple-element.106), channel_id=1, source_target_pairs={{0,1},{1,0},{2,3},{3,2},{4,5},{5,4},{6,7},{7,6},{8,16},{9,17},{10,... | collective-permute-start | bytes 786440 | tf_op jit(solution)/shard_map/ppermute | solution.py:411
  41.0 11.1 %collective-permute-start.13 = (bf16[4,256,128]{2,1,0:T(8,128)(2,1)S(1)}, bf16[4,256,128]{2,1,0:T(8,128)(2,1)S(1)}, u32[]{:S(2)}, u32[]{:S(2)}) collective-permute-start(bf16[4,256,128]{2,1,0:T(8,128)(2,1)S(1)} %get-tuple-element.105), channel_id=1, source_target_pairs={{0,8},{4,12},{8,0},{12,4},{16,24},{20,28},{24,16},{28,20},{1,9},{5... | collective-permute-start | bytes 786440 | tf_op jit(solution)/shard_map/ppermute | solution.py:387
  46.9 7.0 %collective-permute-start.17 = (bf16[4,256,128]{2,1,0:T(8,128)(2,1)S(1)}, bf16[4,256,128]{2,1,0:T(8,128)(2,1)S(1)}, u32[]{:S(2)}, u32[]{:S(2)}) collective-permute-start(bf16[4,256,128]{2,1,0:T(8,128)(2,1)S(1)} %get-tuple-element.112), channel_id=1, source_target_pairs={{0,1},{1,0},{2,3},{3,2},{4,5},{5,4},{6,7},{7,6},{8,16},{9,17},{10,... | collective-permute-start | bytes 786440 | tf_op jit(solution)/shard_map/ppermute | solution.py:411
  47.0 9.2 %collective-permute-start.12 = (bf16[4,256,128]{2,1,0:T(8,128)(2,1)S(1)}, bf16[4,256,128]{2,1,0:T(8,128)(2,1)S(1)}, u32[]{:S(2)}, u32[]{:S(2)}) collective-permute-start(bf16[4,256,128]{2,1,0:T(8,128)(2,1)S(1)} %get-tuple-element.104), channel_id=1, source_target_pairs={{0,4},{4,0},{8,12},{12,8},{16,20},{20,16},{24,28},{28,24},{1,5},{5... | collective-permute-start | bytes 786440 | tf_op jit(solution)/shard_map/ppermute | solution.py:403
  48.1 10.8 %collective-permute-start.16 = (bf16[4,256,128]{2,1,0:T(8,128)(2,1)S(1)}, bf16[4,256,128]{2,1,0:T(8,128)(2,1)S(1)}, u32[]{:S(2)}, u32[]{:S(2)}) collective-permute-start(bf16[4,256,128]{2,1,0:T(8,128)(2,1)S(1)} %get-tuple-element.111), channel_id=1, source_target_pairs={{0,8},{4,12},{8,0},{12,4},{16,24},{20,28},{24,16},{28,20},{1,9},{5... | collective-permute-start | bytes 786440 | tf_op jit(solution)/shard_map/ppermute | solution.py:387
  53.5 9.3 %collective-permute-start.15 = (bf16[4,256,128]{2,1,0:T(8,128)(2,1)S(1)}, bf16[4,256,128]{2,1,0:T(8,128)(2,1)S(1)}, u32[]{:S(2)}, u32[]{:S(2)}) collective-permute-start(bf16[4,256,128]{2,1,0:T(8,128)(2,1)S(1)} %get-tuple-element.110), channel_id=1, source_target_pairs={{0,4},{4,0},{8,12},{12,8},{16,20},{20,16},{24,28},{28,24},{1,5},{5... | collective-permute-start | bytes 786440 | tf_op jit(solution)/shard_map/ppermute | solution.py:403
  54.0 9.9 %copy-start.3 = (bf16[256,256]{1,0:T(8,128)(2,1)S(1)}, bf16[256,256]{1,0:T(8,128)(2,1)}, u32[]{:S(2)}) copy-start(bf16[256,256]{1,0:T(8,128)(2,1)} %refs_2_.3) | copy-start | bytes 393220
  54.0 9.8 %copy-start.5 = (f32[256]{0:T(256)S(1)}, f32[256]{0:T(256)}, u32[]{:S(2)}) copy-start(f32[256]{0:T(256)} %param.8) | copy-start | bytes 3076
  54.0 8.9 %collective-permute-start.19 = (bf16[4,256,128]{2,1,0:T(8,128)(2,1)S(1)}, bf16[4,256,128]{2,1,0:T(8,128)(2,1)S(1)}, u32[]{:S(2)}, u32[]{:S(2)}) collective-permute-start(bf16[4,256,128]{2,1,0:T(8,128)(2,1)S(1)} %get-tuple-element.116), channel_id=1, source_target_pairs={{0,8},{4,12},{8,0},{12,4},{16,24},{20,28},{24,16},{28,20},{1,9},{5... | collective-permute-start | bytes 786440 | tf_op jit(solution)/shard_map/ppermute | solution.py:387
  59.3 9.3 %collective-permute-start.18 = (bf16[4,256,128]{2,1,0:T(8,128)(2,1)S(1)}, bf16[4,256,128]{2,1,0:T(8,128)(2,1)S(1)}, u32[]{:S(2)}, u32[]{:S(2)}) collective-permute-start(bf16[4,256,128]{2,1,0:T(8,128)(2,1)S(1)} %get-tuple-element.115), channel_id=1, source_target_pairs={{0,4},{4,0},{8,12},{12,8},{16,20},{20,16},{24,28},{28,24},{1,5},{5... | collective-permute-start | bytes 786440 | tf_op jit(solution)/shard_map/ppermute | solution.py:403
  63.3 9.3 %collective-permute-start.20 = (bf16[4,256,128]{2,1,0:T(8,128)(2,1)S(1)}, bf16[4,256,128]{2,1,0:T(8,128)(2,1)S(1)}, u32[]{:S(2)}, u32[]{:S(2)}) collective-permute-start(bf16[4,256,128]{2,1,0:T(8,128)(2,1)S(1)} %get-tuple-element.118), channel_id=1, source_target_pairs={{0,4},{4,0},{8,12},{12,8},{16,20},{20,16},{24,28},{28,24},{1,5},{5... | collective-permute-start | bytes 786440 | tf_op jit(solution)/shard_map/ppermute | solution.py:403

commit v4 on v3

--- a/solution.py
+++ b/solution.py
@@ -19,8 +19,9 @@
 
 
 def sizes_of(half):
-    rows = 4 if half % 4 == 0 else 2
-    return [rows] * (half // rows)
+    if half % 4 or half < 8:
+        return [2] * (half // 2)
+    return [2] + [4] * (half // 4 - 1) + [2]
 
 
 def row(ref, q, channels):
@@ -81,7 +82,7 @@
     )(*scalars, *operands, *after)
 
 
-def conv(rows_in, halos, weight, decays, lower, edge, sizes, start, count, dtype, after, edges=False):
+def conv(rows_in, halos, weight, decays, lower, edge, sizes, start, count, dtype, after, edges=False, pair=None):
     tile_rows, channels, width = rows_in.shape
     states = weight.shape[2]
     half = tile_rows // 2
@@ -90,6 +91,8 @@
     whole = start + count == len(sizes)
     assert whole == bool(halos)
     out_shape = [jax.ShapeDtypeStruct((n, states, width), dtype) for n in mine]
+    if pair:
+        out_shape += [jax.ShapeDtypeStruct((n, states, width), dtype) for n in mine]
     if edges:
         out_shape += [jax.ShapeDtypeStruct((channels, width), rows_in.dtype)] * 2
         out_shape[0] = jax.ShapeDtypeStruct((mine[0] * states + PAD, width), dtype)
@@ -97,48 +100,40 @@
     def kernel(lower_ref, edge_ref, rows_ref, weight_ref, decays_ref, *refs):
         refs = list(refs)
         above, below = (refs.pop(0), refs.pop(0)) if whole else (None, None)
-        outs, (rows, shifted, sems) = refs[:-3], refs[-3:]
+        other_ref, coefs_ref = (refs.pop(0), refs.pop(0)) if pair else (None, None)
+        shifted, outs = refs.pop(), refs
         low = lower_ref[0]
-        copied = total + 1 if whole else total + 2
-        first_low = half + before - 1
-        first_up = 0 if whole else half - before - total - 1
-        main = pltpu.make_async_copy(
-            rows_ref.at[pl.ds(first_up + low * (first_low - first_up), copied)],
-            rows.at[pl.ds((1 - low) if whole else 0, copied)],
-            sems.at[0],
-        )
-        main.start()
+        first_low, first_up = half + before - 1, half - before - total - 1
+        first = first_up + low * (first_low - first_up)
         if edges:
-            top = pltpu.make_async_copy(rows_ref.at[0], outs[count], sems.at[1])
-            bottom = pltpu.make_async_copy(rows_ref.at[tile_rows - 1], outs[count + 1], sems.at[2])
-            top.start()
-            bottom.start()
+            outs[count][...] = rows_ref[0]
+            outs[count + 1][...] = rows_ref[tile_rows - 1]
             outs[0][mine[0] * states :] = split_decays(decays_ref[...])
-        main.wait()
-        if whole:
-            slot = low * (total + 1)
-            halo = jnp.where(low == 1, below[...].astype(F32), above[...].astype(F32))
-            rows[slot] = jnp.where(edge_ref[0] == 1, 0.0, halo).astype(rows.dtype)
         lane = lax.broadcasted_iota(jnp.int32, (channels, width), 1)
 
-        def shift(r, carry):
-            row = rows[r].astype(F32)
-            left = jnp.where(lane == 0, 0.0, pltpu.roll(row, 1, 1))
-            right = jnp.where(lane == width - 1, 0.0, pltpu.roll(row, width - 1, 1))
-            shifted[r, :channels] = left.astype(rows.dtype)
-            shifted[r, channels : 2 * channels] = rows[r]
-            shifted[r, 2 * channels :] = right.astype(rows.dtype)
-            return carry
-
-        lax.fori_loop(0, total + 2, shift, 0, unroll=2)
+        def shift(n):
+            slot = (total + 1 - n) + low * (2 * n - total - 1)
+            if whole and n == total + 1:
+                value = jnp.where(low == 1, below[...].astype(F32), above[...].astype(F32))
+                value = jnp.where(edge_ref[0] == 1, 0.0, value)
+            else:
+                value = rows_ref[first + slot].astype(F32)
+            left = jnp.where(lane == 0, 0.0, pltpu.roll(value, 1, 1))
+            right = jnp.where(lane == width - 1, 0.0, pltpu.roll(value, width - 1, 1))
+            shifted[slot, :channels] = left.astype(BF16)
+            shifted[slot, channels : 2 * channels] = value.astype(BF16)
+            shifted[slot, 2 * channels :] = right.astype(BF16)
+
         decay = decays_ref[...]
         gain = columns(jnp.sqrt(1.0 - decay * decay))[:, 0:1]
         taps = jnp.concatenate([weight_ref[i, j] for i in range(3) for j in range(3)], axis=1)
+        for n in range(4):
+            shift(n)
         done = 0
         for n, size in enumerate(mine):
-            at_low, at_up = done, total - done - size
             for q in range(0, size, 2):
-                r = at_up + q + low * (at_low - at_up)
+                at = done + q
+                r = (total - 2 - at) + low * (2 * at - total + 2)
                 window = jnp.concatenate(
                     [
                         jnp.concatenate([shifted[r + i], shifted[r + i + 1]], axis=1)
@@ -147,28 +142,31 @@
                     axis=0,
                 )
                 drive = gain * jnp.dot(taps, window, preferred_element_type=F32)
+                place = (size - 2 - q) + low * (2 * q - size + 2)
                 for i in range(2):
                     value = drive[:, i * width : (i + 1) * width].astype(dtype)
                     if len(outs[n].shape) == 2:
-                        outs[n][(q + i) * states : (q + i + 1) * states] = value
+                        begin = pl.multiple_of((place + i) * states, states)
+                        outs[n][pl.ds(begin, states)] = value
                     else:
-                        outs[n][q + i] = value
+                        outs[n][place + i] = value
+                    if pair:
+                        if len(other_ref.shape) == 2:
+                            begin = pl.multiple_of((place + i) * states, states)
+                            other = other_ref[pl.ds(begin, states)]
+                        else:
+                            other = other_ref[place + i]
+                        outs[1][place + i] = (
+                            coefs_ref[:, 1:2] * value + coefs_ref[:, 2:3] * other.astype(F32)
+                        )
+                for i in range(at + 4, min(at + 6, total + 2)):
+                    shift(i)
             done += size
-        if edges:
-            top.wait()
-            bottom.wait()
-
-    out_specs = [VMEM] * count + ([ANY, ANY] if edges else [])
+
     return call(
         kernel, out_shape, [lower, edge],
-        [rows_in, weight, decays] + list(halos), after, "conv_chunks", 14,
-        scratch=[
-            pltpu.VMEM((total + 2, channels, width), rows_in.dtype),
-            pltpu.VMEM((total + 2, 3 * channels, width), rows_in.dtype),
-            pltpu.SemaphoreType.DMA((3,)),
-        ],
-        specs=[ANY, VMEM, VMEM] + [VMEM] * len(halos),
-        out_specs=out_specs,
+        [rows_in, weight, decays] + list(halos) + list(pair or []), after, "conv_chunks", 14,
+        scratch=[pltpu.VMEM((total + 2, 3 * channels, width), rows_in.dtype)],
     )
 
 
@@ -193,17 +191,6 @@
     return call(kernel, [shape], [odd], [own_decay, first], after, "coefficients")
 
 
-def pair_drive(keep, other, coefs, after):
-    def kernel(keep_ref, other_ref, coefs_ref, out):
-        for q in range(keep.shape[0]):
-            out[q] = coefs_ref[:, 1:2] * keep_ref[q] + coefs_ref[:, 2:3] * row(
-                other_ref, q, keep.shape[1]
-            ).astype(F32)
-
-    shape = jax.ShapeDtypeStruct(keep.shape, F32)
-    return call(kernel, [shape], [], [keep, other, coefs], after, "pair_drive")
-
-
 def carry_on(group, coefs, drives, carry, after):
     groups = sorted(drives)
     most = max(drives[g].shape[0] for g in groups)
@@ -261,41 +248,25 @@
 
     def kernel(lower_ref, rows_ref, weight_ref, skip_ref, *refs):
         chunks = refs[:count]
-        out, rows, held, total, tile, sems = refs[-6:]
+        out, total, tile, sem = refs[-4:]
         low = lower_ref[0]
         begin = pl.multiple_of(low * half, half)
-        main = pltpu.make_async_copy(rows_ref.at[pl.ds(begin, half)], rows, sems.at[0])
-        main.start()
-        copies = []
+        gain = columns(skip_ref[...])[:, 0:1]
         done = 0
         for n, chunk in enumerate(chunks):
             at_up = half - done - sizes[n]
             r = at_up + low * (done - at_up)
-            copies.append(
-                pltpu.make_async_copy(chunk, held.at[pl.ds(r, sizes[n])], sems.at[n + 1])
-            )
+            for q in range(0, sizes[n], 2):
+                value = jnp.dot(
+                    weight_ref[...],
+                    jnp.concatenate([chunk[q], chunk[q + 1]], axis=1),
+                    preferred_element_type=F32,
+                )
+                for i in range(2):
+                    total[pl.ds((r + q + i) * pitch, channels), :] = value[
+                        :, i * width : (i + 1) * width
+                    ] + gain * rows_ref[begin + r + q + i].astype(F32)
             done += sizes[n]
-        for copy in copies:
-            copy.start()
-        gain = columns(skip_ref[...])[:, 0:1]
-        main.wait()
-        for copy in copies:
-            copy.wait()
-
-        def one(p, carry):
-            r = 2 * p
-            value = jnp.dot(
-                weight_ref[...],
-                jnp.concatenate([held[r], held[r + 1]], axis=1),
-                preferred_element_type=F32,
-            )
-            for q in range(2):
-                total[pl.ds((r + q) * pitch, channels), :] = value[
-                    :, q * width : (q + 1) * width
-                ] + gain * rows[r + q].astype(F32)
-            return carry
-
-        lax.fori_loop(0, half // 2, one, 0)
 
         def settle(n, carry):
             for i in range(8):
@@ -303,7 +274,7 @@
             return carry
 
         lax.fori_loop(0, channels // 8, settle, 0, unroll=2)
-        last = pltpu.make_async_copy(tile, out.at[:, pl.ds(begin, half), :], sems.at[count + 1])
+        last = pltpu.make_async_copy(tile, out.at[:, pl.ds(begin, half), :], sem)
         last.start()
         last.wait()
 
@@ -317,13 +288,11 @@
         [jax.ShapeDtypeStruct((channels, tile_rows, width), dtype)],
         [lower], operands, after, "output_half", 10,
         scratch=[
-            pltpu.VMEM((half, channels, width), rows_in.dtype),
-            pltpu.VMEM((half, channels, width), BF16),
             pltpu.VMEM((half * pitch + 8, width), F32),
             pltpu.VMEM((channels, half, width), dtype),
-            pltpu.SemaphoreType.DMA((count + 2,)),
+            pltpu.SemaphoreType.DMA,
         ],
-        specs=[ANY, VMEM, VMEM] + [ANY] * (len(operands) - 3),
+        specs=[VMEM] * (3 + count) + [ANY] * (len(operands) - 3 - count),
         out_specs=[ANY],
         **more,
     )
@@ -367,15 +336,27 @@
     *mine, top, bottom, token = sent(halos=[], start=0, count=early, after=[], edges=True)
     others = [lax.ppermute(value, "tm", swap) for value in mine]
     halos = [lax.ppermute(bottom, "space", down), lax.ppermute(top, "space", up)]
-    *held, token = kept(halos=[], start=0, count=1, after=[token])
-    *rest, token = sent(halos=halos, start=early, count=chunks - early, after=[token])
-    others += [lax.ppermute(value, "tm", swap) for value in rest]
     coefs, token = coefficients(odd, decays, others[0], [token])
-
+    held, drives = [], []
+
+    def pair_drive(k, token):
+        keep, drive, token = kept(
+            halos=halos if k == chunks - 1 else [], start=k, count=1, after=[token],
+            pair=[others[k], coefs],
+        )
+        held.append(keep)
+        drives.append(drive)
+        return token
+
+    token = pair_drive(0, token)
     lag = 3 * ((groups - 2) // 2) + 1
-    drives, evens, odds, own, back = [], {}, {}, [], []
-    drive, token = pair_drive(held[0], others[0], coefs, [token])
-    drives.append(drive)
+    evens, odds, own, back = {}, {}, [], []
+    early_pairs = [chunks - 1]
+    waits = {("S", lag + 2): [0], ("E", lag + 3): [1], ("S", lag + chunks - 1): [chunks - 3]}
+
+    def held_up(kind, step):
+        return [back[n] for n in waits.get((kind, step), []) if 0 <= n < len(back)]
+
     for step in range(chunks + lag):
         ready = {
             g: drives[step - 3 * (g // 2)]
@@ -383,32 +364,34 @@
             if 0 <= step - 3 * (g // 2) < chunks
         }
         if ready:
-            value, token = carry_on(group, coefs, ready, odds.get(step - 2), [token])
+            after = [token] + ([evens[0]] if step == 1 else []) + held_up('E', step)
+            value, token = carry_on(group, coefs, ready, odds.get(step - 2), after)
             evens[step] = lax.ppermute(value, "tm", even_hop)
         if step == 0:
-            *more, token = kept(halos=halos, start=1, count=chunks - 1, after=[token])
-            held += more
-        if step + 1 < chunks:
-            drive, token = pair_drive(held[step + 1], others[step + 1], coefs, [token])
-            drives.append(drive)
+            *rest, token = sent(halos=halos, start=early, count=chunks - early, after=[token])
+            others += [lax.ppermute(value, "tm", swap) for value in rest]
         k = step - lag
         if k >= 0:
             carries = [
                 evens[k + 3 * ((g - 1) // 2)] if g % 2 else odds[k + 1 + 3 * ((g - 2) // 2)]
                 for g in range(1, groups)
             ]
-            after = [token] + ([back[k - 2]] if k >= 2 else [])
+            after = [token] + held_up('S', step)
             mine, theirs, token = states_of(group, coefs, held[k], others[k], carries, after)
             own.append(mine)
             back.append(lax.ppermute(theirs, "tm", swap))
+        if step + 1 in early_pairs:
+            token = pair_drive(step + 1, token)
         ready = {
             g: drives[step - 1 - 3 * ((g - 1) // 2)]
             for g in range(1, groups - 1, 2)
             if 0 <= step - 1 - 3 * ((g - 1) // 2) < chunks
         }
         if ready:
-            value, token = carry_on(group, coefs, ready, evens[step - 1], [token])
+            value, token = carry_on(group, coefs, ready, evens[step - 1], [token] + held_up('O', step))
             odds[step] = lax.ppermute(value, ("tm", "space"), odd_hop)
+        if step + 1 < chunks and step + 1 not in early_pairs:
+            token = pair_drive(step + 1, token)
 
     skip = skip_gain[None]
     dtype = frames_in.dtype

time: 76.6 us -> 72.5 us (0.946)
  Pallas kernels: 23.8 us -> 18 us
  starting transfers between devices: 27.9 us -> 32.2 us
  waiting for transfers between devices: 20.8 us -> 19.1 us
  local copies, waits for them, and re-layouts: 3.31 us -> 2.52 us
    pallas_call x26 -> x28, Pallas kernels: 23.8 us -> 18 us  [call(): pl.pallas_call(body, out_shape=list(out_shape) + [TOKEN], in_specs=[SMEM]...]
    ppermute x7 -> x8, waiting for transfers between devices: 9.99 us -> 5.05 us  [on_device(): evens[step] = lax.ppermute(value, 'tm', even_hop)]
    ppermute x4 -> x5, starting transfers between devices: 2.14 us -> 6.48 us  [on_device(): back.append(lax.ppermute(theirs, 'tm', swap))]
    ppermute x2, waiting for transfers between devices: 0.01 us -> 2.85 us  [on_device(): others = [lax.ppermute(value, 'tm', swap) for value in mine]]
    ppermute x2 -> x3, starting transfers between devices: 2.53 us -> 4.34 us  [on_device(): others += [lax.ppermute(value, 'tm', swap) for value in rest]]
    ppermute x7 -> x8, starting transfers between devices: 18.1 us -> 16.3 us  [on_device(): evens[step] = lax.ppermute(value, 'tm', even_hop)]
    ppermute x2 -> x3, waiting for transfers between devices: 1.68 us -> 3.44 us  [on_device(): others += [lax.ppermute(value, 'tm', swap) for value in rest]]
    ppermute x4 -> x5, waiting for transfers between devices: 9.13 us -> 7.79 us  [on_device(): back.append(lax.ppermute(theirs, 'tm', swap))]
  transfers between devices with their start and end apart: 21 -> 25, of which waited for: 10 -> 10; matrix products, arithmetic and copies ran while one was open for 0% -> 0% of each run, Pallas kernels for 22% -> 19%
where the time goes in v4:
time: 72.5 us; the launch traced here: 72.3 us
  starting transfers between devices  32.2 us (44%)
  waiting for transfers between devices  19.1 us (26%)
  Pallas kernels  18 us (25%)
  local copies, waits for them, and re-layouts  2.52 us (3%)
    pallas_call x28, Pallas kernels, call(): pl.pallas_call(body, out_shape=list(out_shape) + [TOKEN], in_specs=[SMEM]...  18 us
    ppermute x8, starting transfers between devices, on_device(): evens[step] = lax.ppermute(value, 'tm', even_hop)  16.3 us
    ppermute x5, waiting for transfers between devices, on_device(): back.append(lax.ppermute(theirs, 'tm', swap))  7.79 us
    ppermute x5, starting transfers between devices, on_device(): back.append(lax.ppermute(theirs, 'tm', swap))  6.48 us
    ppermute x8, waiting for transfers between devices, on_device(): evens[step] = lax.ppermute(value, 'tm', even_hop)  5.05 us
    ppermute x3, starting transfers between devices, on_device(): others += [lax.ppermute(value, 'tm', swap) for value in rest]  4.34 us
    ppermute x3, waiting for transfers between devices, on_device(): others += [lax.ppermute(value, 'tm', swap) for value in rest]  3.44 us
    ppermute x2, starting transfers between devices, on_device(): others = [lax.ppermute(value, 'tm', swap) for value in mine]  3 us
  transfers between devices with their start and end apart: 25, of which 10 were waited for; matrix products, arithmetic and copies ran while one was open for 0% of the time, Pallas kernels for 19%

profile of v4, /device:TPU:0, one launch (start us, length us, event | category | flops | bytes accessed | tf_op | source)
XLA Modules:
  0.0 72.3 jit_solution(16422265421767310754)
XLA Ops:
  0.0 2.5 %copy.9 = bf16[1,256,32,128]{3,1,2,0:T(8,128)(2,1)S(1)} copy(bf16[1,256,32,128]{3,2,1,0:T(8,128)(2,1)} %param.5) | data formatting | bytes 4194304 | tf_op args[0]
  2.5 2.2 %conv_chunks.7 = (bf16[528,128]{1,0:T(8,128)(2,1)}, bf16[4,256,128]{2,1,0:T(8,128)(2,1)}, bf16[256,128]{1,0:T(8,128)(2,1)}, bf16[256,128]{1,0:T(8,128)(2,1)}, f32[8,128]{1,0:T(8,128)S(1)}) custom-call(s32[1]{0:T(128)} %bitcast.refs_0_, s32[1]{0:T(128)} %bitcast.6.refs_1_, bf16[32,256,128]{2,1,0:T(8,128)(2,1)S(1)} %bitcast.12, ...), custom_call_target="tpu_custom_call" | custom-call | flops 1 | bytes 1 | tf_op jit(solution)/shard_map/conv_chunks/pallas_call | solution.py:72
  4.7 3.0 %collective-permute-start = (bf16[528,128]{1,0:T(8,128)(2,1)}, bf16[528,128]{1,0:T(8,128)(2,1)S(1)}, u32[]{:S(2)}, u32[]{:S(2)}) collective-permute-start(bf16[528,128]{1,0:T(8,128)(2,1)} %get-tuple-element.75), channel_id=1, source_target_pairs={{0,4},{4,0},{8,12},{12,8},{16,20},{20,16},{24,28},{28,24},{1,5},{5... | collective-permute-start | bytes 405512 | tf_op jit(solution)/shard_map/ppermute | solution.py:337
  7.7 0.0 collective-permute-start.2
  7.7 1.7 %collective-permute-start.4 = (bf16[256,128]{1,0:T(8,128)(2,1)}, bf16[256,128]{1,0:T(8,128)(2,1)S(1)}, u32[]{:S(2)}, u32[]{:S(2)}) collective-permute-start(bf16[256,128]{1,0:T(8,128)(2,1)} %get-tuple-element.85), channel_id=1, source_target_pairs={{0,3},{1,0},{2,1},{3,2},{4,7},{5,4},{6,5},{7,6},{8,11},{9,8},{10,9... | collective-permute-start | bytes 196616 | tf_op jit(solution)/shard_map/ppermute | solution.py:338
  9.5 2.8 %collective-permute-done.refs_2_.refs_5_.refs_3_ = bf16[528,128]{1,0:T(8,128)(2,1)S(1)} collective-permute-done((bf16[528,128]{1,0:T(8,128)(2,1)}, bf16[528,128]{1,0:T(8,128)(2,1)S(1)}, u32[]{:S(2)}, u32[]{:S(2)}) %collective-permute-start) | collective-permute-done | bytes 135200 | tf_op jit(solution)/shard_map/ppermute | solution.py:337
  12.3 0.1 coefficients.1
  12.4 0.8 %conv_chunks.8 = (f32[2,256,128]{2,1,0:T(8,128)S(1)}, f32[2,256,128]{2,1,0:T(8,128)S(1)}, f32[8,128]{1,0:T(8,128)S(1)}) custom-call(s32[1]{0:T(128)} %bitcast.5.refs_0_, s32[1]{0:T(128)} %bitcast.8.refs_1_, bf16[32,256,128]{2,1,0:T(8,128)(2,1)S(1)} %bitcast.13, bf16[3,3,256,256]{3,2,1,0:T(8,128)(2,1)S(1)} %copy-done, f32[1,256]{1,0:T(1,128)S(1)} %copy-done.2, ...), custom_call_target="tpu_custom_call" | custom-call | flops 1 | bytes 1 | tf_op jit(solution)/shard_map/conv_chunks/pallas_call | solution.py:72
  13.2 2.2 %collective-permute-start.1 = (bf16[2,256,128]{2,1,0:T(8,128)(2,1)S(1)}, bf16[2,256,128]{2,1,0:T(8,128)(2,1)S(1)}, u32[]{:S(2)}, u32[]{:S(2)}) collective-permute-start(bf16[2,256,128]{2,1,0:T(8,128)(2,1)S(1)} %get-tuple-element.82), channel_id=1, source_target_pairs={{0,8},{4,12},{8,0},{12,4},{16,24},{20,28},{24,16},{28,20},{1,9},{5... | collective-permute-start | bytes 393224 | tf_op jit(solution)/shard_map/ppermute | solution.py:369
  15.4 0.0 collective-permute-done.3.refs_5_
  15.4 0.0 collective-permute-done.4.refs_6_
  15.4 2.3 %conv_chunks.9 = (bf16[4,256,128]{2,1,0:T(8,128)(2,1)S(1)}, bf16[4,256,128]{2,1,0:T(8,128)(2,1)S(1)}, bf16[2,256,128]{2,1,0:T(8,128)(2,1)S(1)}, f32[8,128]{1,0:T(8,128)S(1)}) custom-call(s32[1]{0:T(128)} %bitcast.refs_0_, s32[1]{0:T(128)} %bitcast.6.refs_1_, bf16[32,256,128]{2,1,0:T(8,128)(2,1)S(1)} %bitcast.14, bf16[3,3,256,256]{3,2,1,0:T(8,128)(2,1)S(1)} %copy-done, ...), custom_call_target="tpu_custom_call" | custom-call | flops 1 | bytes 1 | tf_op jit(solution)/shard_map/conv_chunks/pallas_call | solution.py:72
  17.7 1.6 %collective-permute-start.8 = (bf16[4,256,128]{2,1,0:T(8,128)(2,1)S(1)}, bf16[4,256,128]{2,1,0:T(8,128)(2,1)S(1)}, u32[]{:S(2)}, u32[]{:S(2)}) collective-permute-start(bf16[4,256,128]{2,1,0:T(8,128)(2,1)S(1)} %get-tuple-element.94), channel_id=1, source_target_pairs={{0,4},{4,0},{8,12},{12,8},{16,20},{20,16},{24,28},{28,24},{1,5},{5... | collective-permute-start | bytes 786440 | tf_op jit(solution)/shard_map/ppermute | solution.py:372
  19.3 2.1 %conv_chunks.10 = (f32[4,256,128]{2,1,0:T(8,128)S(1)}, f32[4,256,128]{2,1,0:T(8,128)S(1)}, f32[8,128]{1,0:T(8,128)S(1)}) custom-call(s32[1]{0:T(128)} %bitcast.5.refs_0_, s32[1]{0:T(128)} %bitcast.8.refs_1_, bf16[32,256,128]{2,1,0:T(8,128)(2,1)S(1)} %bitcast.15, bf16[3,3,256,256]{3,2,1,0:T(8,128)(2,1)S(1)} %copy-done, f32[1,256]{1,0:T(1,128)S(1)} %copy-done.2, ...), custom_call_target="tpu_custom_call" | custom-call | flops 1 | bytes 1 | tf_op jit(solution)/shard_map/conv_chunks/pallas_call | solution.py:72
  21.4 0.0 collective-permute-done.1.refs_4_.refs_3_
  21.4 0.1 carry_on.14
  21.5 0.5 collective-permute-start.7
  22.0 0.8 %collective-permute-start.6 = (bf16[4,256,128]{2,1,0:T(8,128)(2,1)S(1)}, bf16[4,256,128]{2,1,0:T(8,128)(2,1)S(1)}, u32[]{:S(2)}, u32[]{:S(2)}) collective-permute-start(bf16[4,256,128]{2,1,0:T(8,128)(2,1)S(1)} %get-tuple-element.92), channel_id=1, source_target_pairs={{0,4},{4,0},{8,12},{12,8},{16,20},{20,16},{24,28},{28,24},{1,5},{5... | collective-permute-start | bytes 786440 | tf_op jit(solution)/shard_map/ppermute | solution.py:372
  22.8 0.1 collective-permute-start.5
  22.9 2.5 %collective-permute-done.8.refs_5_.refs_3_ = bf16[4,256,128]{2,1,0:T(8,128)(2,1)S(1)} collective-permute-done((bf16[4,256,128]{2,1,0:T(8,128)(2,1)S(1)}, bf16[4,256,128]{2,1,0:T(8,128)(2,1)S(1)}, u32[]{:S(2)}, u32[]{:S(2)}) %collective-permute-start.8) | collective-permute-done | bytes 262176 | tf_op jit(solution)/shard_map/ppermute | solution.py:372
  25.4 1.2 %conv_chunks.11 = (f32[4,256,128]{2,1,0:T(8,128)S(1)}, f32[4,256,128]{2,1,0:T(8,128)S(1)}, f32[8,128]{1,0:T(8,128)S(1)}) custom-call(s32[1]{0:T(128)} %bitcast.5.refs_0_, s32[1]{0:T(128)} %bitcast.8.refs_1_, bf16[32,256,128]{2,1,0:T(8,128)(2,1)S(1)} %bitcast.16, bf16[3,3,256,256]{3,2,1,0:T(8,128)(2,1)S(1)} %copy-done, f32[1,256]{1,0:T(1,128)S(1)} %copy-done.2, ...), custom_call_target="tpu_custom_call" | custom-call | flops 1 | bytes 1 | tf_op jit(solution)/shard_map/conv_chunks/pallas_call | solution.py:72
  26.6 0.1 carry_on.16
  26.7 1.6 %collective-permute-start.12 = (bf16[4,256,128]{2,1,0:T(8,128)(2,1)S(1)}, bf16[4,256,128]{2,1,0:T(8,128)(2,1)S(1)}, u32[]{:S(2)}, u32[]{:S(2)}) collective-permute-start(bf16[4,256,128]{2,1,0:T(8,128)(2,1)S(1)} %get-tuple-element.107), channel_id=1, source_target_pairs={{0,8},{4,12},{8,0},{12,4},{16,24},{20,28},{24,16},{28,20},{1,9},{5... | collective-permute-start | bytes 786440 | tf_op jit(solution)/shard_map/ppermute | solution.py:369
  28.3 2.0 %collective-permute-start.10 = (bf16[2,256,128]{2,1,0:T(8,128)(2,1)S(1)}, bf16[2,256,128]{2,1,0:T(8,128)(2,1)S(1)}, u32[]{:S(2)}, u32[]{:S(2)}) collective-permute-start(bf16[2,256,128]{2,1,0:T(8,128)(2,1)S(1)} %get-tuple-element.103), channel_id=1, source_target_pairs={{0,4},{4,0},{8,12},{12,8},{16,20},{20,16},{24,28},{28,24},{1,5},{5... | collective-permute-start | bytes 393224 | tf_op jit(solution)/shard_map/ppermute | solution.py:372
  30.3 0.0 collective-permute-done.7.refs_3_.refs_4_
  30.3 0.1 collective-permute-start.11
  30.4 0.9 %collective-permute-done.6.refs_5_.refs_3_ = bf16[4,256,128]{2,1,0:T(8,128)(2,1)S(1)} collective-permute-done((bf16[4,256,128]{2,1,0:T(8,128)(2,1)S(1)}, bf16[4,256,128]{2,1,0:T(8,128)(2,1)S(1)}, u32[]{:S(2)}, u32[]{:S(2)}) %collective-permute-start.6) | collective-permute-done | bytes 262176 | tf_op jit(solution)/shard_map/ppermute | solution.py:372
  31.3 1.2 %conv_chunks.12 = (f32[4,256,128]{2,1,0:T(8,128)S(1)}, f32[4,256,128]{2,1,0:T(8,128)S(1)}, f32[8,128]{1,0:T(8,128)S(1)}) custom-call(s32[1]{0:T(128)} %bitcast.5.refs_0_, s32[1]{0:T(128)} %bitcast.8.refs_1_, bf16[32,256,128]{2,1,0:T(8,128)(2,1)S(1)} %bitcast.17, bf16[3,3,256,256]{3,2,1,0:T(8,128)(2,1)S(1)} %copy-done, f32[1,256]{1,0:T(1,128)S(1)} %copy-done.2, ...), custom_call_target="tpu_custom_call" | custom-call | flops 1 | bytes 1 | tf_op jit(solution)/shard_map/conv_chunks/pallas_call | solution.py:72
  32.5 0.0 collective-permute-done.5.refs_4_.refs_5_
  32.5 0.1 carry_on.18
  32.5 2.3 %collective-permute-start.9 = (bf16[4,256,128]{2,1,0:T(8,128)(2,1)S(1)}, bf16[4,256,128]{2,1,0:T(8,128)(2,1)S(1)}, u32[]{:S(2)}, u32[]{:S(2)}) collective-permute-start(bf16[4,256,128]{2,1,0:T(8,128)(2,1)S(1)} %get-tuple-element.102), channel_id=1, source_target_pairs={{0,8},{4,12},{8,0},{12,4},{16,24},{20,28},{24,16},{28,20},{1,9},{5... | collective-permute-start | bytes 786440 | tf_op jit(solution)/shard_map/ppermute | solution.py:369
  34.8 0.0 collective-permute-done.10.refs_7_.refs_3_
  34.8 0.8 %conv_chunks.13 = (f32[2,256,128]{2,1,0:T(8,128)S(1)}, f32[2,256,128]{2,1,0:T(8,128)S(1)}, f32[8,128]{1,0:T(8,128)S(1)}) custom-call(s32[1]{0:T(128)} %bitcast.5.refs_0_, s32[1]{0:T(128)} %bitcast.8.refs_1_, bf16[32,256,128]{2,1,0:T(8,128)(2,1)S(1)} %bitcast.18, bf16[3,3,256,256]{3,2,1,0:T(8,128)(2,1)S(1)} %copy-done, f32[1,256]{1,0:T(1,128)S(1)} %copy-done.2, ...), custom_call_target="tpu_custom_call" | custom-call | flops 1 | bytes 1 | tf_op jit(solution)/shard_map/conv_chunks/pallas_call | solution.py:72
  35.7 0.1 collective-permute-start.15
  35.7 0.0 collective-permute-done.11.refs_4_.refs_5_
  35.7 0.1 carry_on.20
  35.8 2.7 %collective-permute-start.14 = (bf16[4,256,128]{2,1,0:T(8,128)(2,1)S(1)}, bf16[4,256,128]{2,1,0:T(8,128)(2,1)S(1)}, u32[]{:S(2)}, u32[]{:S(2)}) collective-permute-start(bf16[4,256,128]{2,1,0:T(8,128)(2,1)S(1)} %get-tuple-element.113), channel_id=1, source_target_pairs={{0,8},{4,12},{8,0},{12,4},{16,24},{20,28},{24,16},{28,20},{1,9},{5... | collective-permute-start | bytes 786440 | tf_op jit(solution)/shard_map/ppermute | solution.py:369
  38.5 3.3 %collective-permute-done.9.refs_6_.refs_3_.refs_4_ = bf16[4,256,128]{2,1,0:T(8,128)(2,1)S(1)} collective-permute-done((bf16[4,256,128]{2,1,0:T(8,128)(2,1)S(1)}, bf16[4,256,128]{2,1,0:T(8,128)(2,1)S(1)}, u32[]{:S(2)}, u32[]{:S(2)}) %collective-permute-start.9) | collective-permute-done | bytes 262176 | tf_op jit(solution)/shard_map/ppermute | solution.py:369
  41.8 0.2 states_of.5
  42.1 0.2 carry_on.21
  42.3 0.1 collective-permute-start.18
  42.4 3.4 %collective-permute-start.17 = (bf16[4,256,128]{2,1,0:T(8,128)(2,1)S(1)}, bf16[4,256,128]{2,1,0:T(8,128)(2,1)S(1)}, u32[]{:S(2)}, u32[]{:S(2)}) collective-permute-start(bf16[4,256,128]{2,1,0:T(8,128)(2,1)S(1)} %get-tuple-element.120), channel_id=1, source_target_pairs={{0,8},{4,12},{8,0},{12,4},{16,24},{20,28},{24,16},{28,20},{1,9},{5... | collective-permute-start | bytes 786440 | tf_op jit(solution)/shard_map/ppermute | solution.py:369
  45.9 1.4 %collective-permute-start.13 = (bf16[2,256,128]{2,1,0:T(8,128)(2,1)S(1)}, bf16[2,256,128]{2,1,0:T(8,128)(2,1)S(1)}, u32[]{:S(2)}, u32[]{:S(2)}) collective-permute-start(bf16[2,256,128]{2,1,0:T(8,128)(2,1)S(1)} %get-tuple-element.111), channel_id=1, source_target_pairs={{0,4},{4,0},{8,12},{12,8},{16,20},{20,16},{24,28},{28,24},{1,5},{5... | collective-permute-start | bytes 393224 | tf_op jit(solution)/shard_map/ppermute | solution.py:382
  47.3 1.3 %states_of.6 = (bf16[4,256,128]{2,1,0:T(8,128)(2,1)S(1)}, bf16[4,256,128]{2,1,0:T(8,128)(2,1)S(1)}, f32[8,128]{1,0:T(8,128)S(1)}) custom-call(s32[1]{0:T(128)} %bitcast.4.refs_0_, f32[256,8]{1,0:T(8,128)S(1)} %get-tuple-element.77.refs_6_.refs_1_.refs_8_, f32[4,256,128]{2,1,0:T(8,128)S(1)} %get-tuple-element.112.refs_2_, ...), custom_call_target="tpu_custom_call" | custom-call | flops 1 | bytes 1 | tf_op jit(solution)/shard_map/states_of/pallas_call | solution.py:72
  48.6 0.7 collective-permute-start.16
  49.4 1.9 %collective-permute-start.20 = (bf16[4,256,128]{2,1,0:T(8,128)(2,1)S(1)}, bf16[4,256,128]{2,1,0:T(8,128)(2,1)S(1)}, u32[]{:S(2)}, u32[]{:S(2)}) collective-permute-start(bf16[4,256,128]{2,1,0:T(8,128)(2,1)S(1)} %get-tuple-element.127), channel_id=1, source_target_pairs={{0,8},{4,12},{8,0},{12,4},{16,24},{20,28},{24,16},{28,20},{1,9},{5... | collective-permute-start | bytes 786440 | tf_op jit(solution)/shard_map/ppermute | solution.py:369
  51.3 0.0 collective-permute-start.21
  51.3 0.9 %collective-permute-done.13.refs_8_.refs_4_ = bf16[2,256,128]{2,1,0:T(8,128)(2,1)S(1)} collective-permute-done((bf16[2,256,128]{2,1,0:T(8,128)(2,1)S(1)}, bf16[2,256,128]{2,1,0:T(8,128)(2,1)S(1)}, u32[]{:S(2)}, u32[]{:S(2)}) %collective-permute-start.13) | collective-permute-done | bytes 131104 | tf_op jit(solution)/shard_map/ppermute | solution.py:382
  52.2 0.9 %collective-permute-done.17.refs_6_ = bf16[4,256,128]{2,1,0:T(8,128)(2,1)S(1)} collective-permute-done((bf16[4,256,128]{2,1,0:T(8,128)(2,1)S(1)}, bf16[4,256,128]{2,1,0:T(8,128)(2,1)S(1)}, u32[]{:S(2)}, u32[]{:S(2)}) %collective-permute-start.17) | collective-permute-done | bytes 262176 | tf_op jit(solution)/shard_map/ppermute | solution.py:369
  53.1 0.4 states_of.7
  53.5 0.0 copy-start.1
  53.5 0.0 copy-start.3
  53.5 1.2 %collective-permute-start.19 = (bf16[4,256,128]{2,1,0:T(8,128)(2,1)S(1)}, bf16[4,256,128]{2,1,0:T(8,128)(2,1)S(1)}, u32[]{:S(2)}, u32[]{:S(2)}) collective-permute-start(bf16[4,256,128]{2,1,0:T(8,128)(2,1)S(1)} %get-tuple-element.125), channel_id=1, source_target_pairs={{0,4},{4,0},{8,12},{12,8},{16,20},{20,16},{24,28},{28,24},{1,5},{5... | collective-permute-start | bytes 786440 | tf_op jit(solution)/shard_map/ppermute | solution.py:382
  54.7 1.9 %collective-permute-done.16.refs_5_ = bf16[4,256,128]{2,1,0:T(8,128)(2,1)S(1)} collective-permute-done((bf16[4,256,128]{2,1,0:T(8,128)(2,1)S(1)}, bf16[4,256,128]{2,1,0:T(8,128)(2,1)S(1)}, u32[]{:S(2)}, u32[]{:S(2)}) %collective-permute-start.16) | collective-permute-done | bytes 262176 | tf_op jit(solution)/shard_map/ppermute | solution.py:382
  56.6 1.7 %collective-permute-start.23 = (bf16[2,256,128]{2,1,0:T(8,128)(2,1)S(1)}, bf16[2,256,128]{2,1,0:T(8,128)(2,1)S(1)}, u32[]{:S(2)}, u32[]{:S(2)}) collective-permute-start(bf16[2,256,128]{2,1,0:T(8,128)(2,1)S(1)} %get-tuple-element.133), channel_id=1, source_target_pairs={{0,8},{4,12},{8,0},{12,4},{16,24},{20,28},{24,16},{28,20},{1,9},{5... | collective-permute-start | bytes 393224 | tf_op jit(solution)/shard_map/ppermute | solution.py:369
  58.3 0.4 states_of.8
  58.7 2.1 %collective-permute-start.22 = (bf16[4,256,128]{2,1,0:T(8,128)(2,1)S(1)}, bf16[4,256,128]{2,1,0:T(8,128)(2,1)S(1)}, u32[]{:S(2)}, u32[]{:S(2)}) collective-permute-start(bf16[4,256,128]{2,1,0:T(8,128)(2,1)S(1)} %get-tuple-element.131), channel_id=1, source_target_pairs={{0,4},{4,0},{8,12},{12,8},{16,20},{20,16},{24,28},{28,24},{1,5},{5... | collective-permute-start | bytes 786440 | tf_op jit(solution)/shard_map/ppermute | solution.py:382
  60.8 0.8 %collective-permute-done.23.refs_6_ = bf16[2,256,128]{2,1,0:T(8,128)(2,1)S(1)} collective-permute-done((bf16[2,256,128]{2,1,0:T(8,128)(2,1)S(1)}, bf16[2,256,128]{2,1,0:T(8,128)(2,1)S(1)}, u32[]{:S(2)}, u32[]{:S(2)}) %collective-permute-start.23) | collective-permute-done | bytes 131104 | tf_op jit(solution)/shard_map/ppermute | solution.py:369
  61.6 1.2 %collective-permute-done.19.refs_8_.refs_6_ = bf16[4,256,128]{2,1,0:T(8,128)(2,1)S(1)} collective-permute-done((bf16[4,256,128]{2,1,0:T(8,128)(2,1)S(1)}, bf16[4,256,128]{2,1,0:T(8,128)(2,1)S(1)}, u32[]{:S(2)}, u32[]{:S(2)}) %collective-permute-start.19) | collective-permute-done | bytes 262176 | tf_op jit(solution)/shard_map/ppermute | solution.py:382
  62.8 0.2 states_of.9
  63.1 1.2 %collective-permute-start.24 = (bf16[2,256,128]{2,1,0:T(8,128)(2,1)S(1)}, bf16[2,256,128]{2,1,0:T(8,128)(2,1)S(1)}, u32[]{:S(2)}, u32[]{:S(2)}) collective-permute-start(bf16[2,256,128]{2,1,0:T(8,128)(2,1)S(1)} %get-tuple-element.135), channel_id=1, source_target_pairs={{0,4},{4,0},{8,12},{12,8},{16,20},{20,16},{24,28},{28,24},{1,5},{5... | collective-permute-start | bytes 393224 | tf_op jit(solution)/shard_map/ppermute | solution.py:382
  64.2 1.8 %output_half.2 = (bf16[256,32,128]{2,1,0:T(8,128)(2,1)}, f32[8,128]{1,0:T(8,128)S(1)}) custom-call(s32[1]{0:T(128)} %bitcast.5.refs_0_, bf16[32,256,128]{2,1,0:T(8,128)(2,1)S(1)} %bitcast.19, bf16[256,256]{1,0:T(8,128)(2,1)S(1)} %copy-done.1, f32[1,256]{1,0:T(1,128)S(1)} %bitcast.21, bf16[2,256,128]{2,1,0:T(8,128)(2,1)S(1)} %get-tuple-element.136.refs_4_, ...), custom_call_target="tpu_custom_call" | custom-call | flops 1 | bytes 1 | tf_op jit(solution)/shard_map/output_half/pallas_call | solution.py:72
  66.0 3.8 %collective-permute-done.24.refs_8_ = bf16[2,256,128]{2,1,0:T(8,128)(2,1)S(1)} collective-permute-done((bf16[2,256,128]{2,1,0:T(8,128)(2,1)S(1)}, bf16[2,256,128]{2,1,0:T(8,128)(2,1)S(1)}, u32[]{:S(2)}, u32[]{:S(2)}) %collective-permute-start.24) | collective-permute-done | bytes 131104 | tf_op jit(solution)/shard_map/ppermute | solution.py:382
  69.8 2.4 %output_half.3 = (bf16[256,32,128]{2,1,0:T(8,128)(2,1)}, f32[8,128]{1,0:T(8,128)}) custom-call(s32[1]{0:T(128)} %bitcast.refs_0_, bf16[32,256,128]{2,1,0:T(8,128)(2,1)S(1)} %bitcast.20, bf16[256,256]{1,0:T(8,128)(2,1)S(1)} %copy-done.1, f32[1,256]{1,0:T(1,128)S(1)} %bitcast.22, ...), custom_call_target="tpu_custom_call", output_to_operand_aliasing={{0}: (9, {})} | custom-call | flops 1 | bytes 1 | tf_op jit(solution)/shard_map/output_half/pallas_call | solution.py:72
  (23 shorter events, 0.3 us)
Async XLA Ops:
  0.0 2.5 %copy-start = (bf16[3,3,256,256]{3,2,1,0:T(8,128)(2,1)S(1)}, bf16[3,3,256,256]{3,2,1,0:T(8,128)(2,1)}, u32[]{:S(2)}) copy-start(bf16[3,3,256,256]{3,2,1,0:T(8,128)(2,1)} %refs_3_.13) | copy-start | bytes 3538948
  0.0 2.5 %copy-start.2 = (f32[1,256]{1,0:T(1,128)S(1)}, f32[1,256]{1,0:T(1,128)}, u32[]{:S(2)}) copy-start(f32[1,256]{1,0:T(1,128)} %refs_4_.13) | copy-start | bytes 3076
  4.7 7.6 %collective-permute-start = (bf16[528,128]{1,0:T(8,128)(2,1)}, bf16[528,128]{1,0:T(8,128)(2,1)S(1)}, u32[]{:S(2)}, u32[]{:S(2)}) collective-permute-start(bf16[528,128]{1,0:T(8,128)(2,1)} %get-tuple-element.75), channel_id=1, source_target_pairs={{0,4},{4,0},{8,12},{12,8},{16,20},{20,16},{24,28},{28,24},{1,5},{5... | collective-permute-start | bytes 405512 | tf_op jit(solution)/shard_map/ppermute | solution.py:337
  7.7 11.6 %collective-permute-start.2 = (bf16[4,256,128]{2,1,0:T(8,128)(2,1)}, bf16[4,256,128]{2,1,0:T(8,128)(2,1)}, u32[]{:S(2)}, u32[]{:S(2)}) collective-permute-start(bf16[4,256,128]{2,1,0:T(8,128)(2,1)} %get-tuple-element.83), channel_id=1, source_target_pairs={{0,4},{4,0},{8,12},{12,8},{16,20},{20,16},{24,28},{28,24},{1,5},{5... | collective-permute-start | bytes 786440 | tf_op jit(solution)/shard_map/ppermute | solution.py:337
  7.7 7.7 %collective-permute-start.3 = (bf16[256,128]{1,0:T(8,128)(2,1)}, bf16[256,128]{1,0:T(8,128)(2,1)S(1)}, u32[]{:S(2)}, u32[]{:S(2)}) collective-permute-start(bf16[256,128]{1,0:T(8,128)(2,1)} %get-tuple-element.84), channel_id=1, source_target_pairs={{0,1},{1,2},{2,3},{3,0},{4,5},{5,6},{6,7},{7,4},{8,9},{9,10},{10,1... | collective-permute-start | bytes 196616 | tf_op jit(solution)/shard_map/ppermute | solution.py:338
  7.7 7.7 %collective-permute-start.4 = (bf16[256,128]{1,0:T(8,128)(2,1)}, bf16[256,128]{1,0:T(8,128)(2,1)S(1)}, u32[]{:S(2)}, u32[]{:S(2)}) collective-permute-start(bf16[256,128]{1,0:T(8,128)(2,1)} %get-tuple-element.85), channel_id=1, source_target_pairs={{0,3},{1,0},{2,1},{3,2},{4,7},{5,4},{6,5},{7,6},{8,11},{9,8},{10,9... | collective-permute-start | bytes 196616 | tf_op jit(solution)/shard_map/ppermute | solution.py:338
  13.2 8.2 %collective-permute-start.1 = (bf16[2,256,128]{2,1,0:T(8,128)(2,1)S(1)}, bf16[2,256,128]{2,1,0:T(8,128)(2,1)S(1)}, u32[]{:S(2)}, u32[]{:S(2)}) collective-permute-start(bf16[2,256,128]{2,1,0:T(8,128)(2,1)S(1)} %get-tuple-element.82), channel_id=1, source_target_pairs={{0,8},{4,12},{8,0},{12,4},{16,24},{20,28},{24,16},{28,20},{1,9},{5... | collective-permute-start | bytes 393224 | tf_op jit(solution)/shard_map/ppermute | solution.py:369
  17.7 7.7 %collective-permute-start.8 = (bf16[4,256,128]{2,1,0:T(8,128)(2,1)S(1)}, bf16[4,256,128]{2,1,0:T(8,128)(2,1)S(1)}, u32[]{:S(2)}, u32[]{:S(2)}) collective-permute-start(bf16[4,256,128]{2,1,0:T(8,128)(2,1)S(1)} %get-tuple-element.94), channel_id=1, source_target_pairs={{0,4},{4,0},{8,12},{12,8},{16,20},{20,16},{24,28},{28,24},{1,5},{5... | collective-permute-start | bytes 786440 | tf_op jit(solution)/shard_map/ppermute | solution.py:372
  21.5 8.7 %collective-permute-start.7 = (bf16[4,256,128]{2,1,0:T(8,128)(2,1)S(1)}, bf16[4,256,128]{2,1,0:T(8,128)(2,1)S(1)}, u32[]{:S(2)}, u32[]{:S(2)}) collective-permute-start(bf16[4,256,128]{2,1,0:T(8,128)(2,1)S(1)} %get-tuple-element.93), channel_id=1, source_target_pairs={{0,8},{4,12},{8,0},{12,4},{16,24},{20,28},{24,16},{28,20},{1,9},{5... | collective-permute-start | bytes 786440 | tf_op jit(solution)/shard_map/ppermute | solution.py:369
  22.0 9.2 %collective-permute-start.6 = (bf16[4,256,128]{2,1,0:T(8,128)(2,1)S(1)}, bf16[4,256,128]{2,1,0:T(8,128)(2,1)S(1)}, u32[]{:S(2)}, u32[]{:S(2)}) collective-permute-start(bf16[4,256,128]{2,1,0:T(8,128)(2,1)S(1)} %get-tuple-element.92), channel_id=1, source_target_pairs={{0,4},{4,0},{8,12},{12,8},{16,20},{20,16},{24,28},{28,24},{1,5},{5... | collective-permute-start | bytes 786440 | tf_op jit(solution)/shard_map/ppermute | solution.py:372
  22.8 9.7 %collective-permute-start.5 = (bf16[2,256,128]{2,1,0:T(8,128)(2,1)S(1)}, bf16[2,256,128]{2,1,0:T(8,128)(2,1)S(1)}, u32[]{:S(2)}, u32[]{:S(2)}) collective-permute-start(bf16[2,256,128]{2,1,0:T(8,128)(2,1)S(1)} %get-tuple-element.91), channel_id=1, source_target_pairs={{0,1},{1,0},{2,3},{3,2},{4,5},{5,4},{6,7},{7,6},{8,16},{9,17},{10,... | collective-permute-start | bytes 393224 | tf_op jit(solution)/shard_map/ppermute | solution.py:392
  26.7 8.9 %collective-permute-start.12 = (bf16[4,256,128]{2,1,0:T(8,128)(2,1)S(1)}, bf16[4,256,128]{2,1,0:T(8,128)(2,1)S(1)}, u32[]{:S(2)}, u32[]{:S(2)}) collective-permute-start(bf16[4,256,128]{2,1,0:T(8,128)(2,1)S(1)} %get-tuple-element.107), channel_id=1, source_target_pairs={{0,8},{4,12},{8,0},{12,4},{16,24},{20,28},{24,16},{28,20},{1,9},{5... | collective-permute-start | bytes 786440 | tf_op jit(solution)/shard_map/ppermute | solution.py:369
  28.3 6.6 %collective-permute-start.10 = (bf16[2,256,128]{2,1,0:T(8,128)(2,1)S(1)}, bf16[2,256,128]{2,1,0:T(8,128)(2,1)S(1)}, u32[]{:S(2)}, u32[]{:S(2)}) collective-permute-start(bf16[2,256,128]{2,1,0:T(8,128)(2,1)S(1)} %get-tuple-element.103), channel_id=1, source_target_pairs={{0,4},{4,0},{8,12},{12,8},{16,20},{20,16},{24,28},{28,24},{1,5},{5... | collective-permute-start | bytes 393224 | tf_op jit(solution)/shard_map/ppermute | solution.py:372
  30.3 5.4 %collective-permute-start.11 = (bf16[4,256,128]{2,1,0:T(8,128)(2,1)S(1)}, bf16[4,256,128]{2,1,0:T(8,128)(2,1)S(1)}, u32[]{:S(2)}, u32[]{:S(2)}) collective-permute-start(bf16[4,256,128]{2,1,0:T(8,128)(2,1)S(1)} %get-tuple-element.106), channel_id=1, source_target_pairs={{0,1},{1,0},{2,3},{3,2},{4,5},{5,4},{6,7},{7,6},{8,16},{9,17},{10,... | collective-permute-start | bytes 786440 | tf_op jit(solution)/shard_map/ppermute | solution.py:392
  32.5 9.3 %collective-permute-start.9 = (bf16[4,256,128]{2,1,0:T(8,128)(2,1)S(1)}, bf16[4,256,128]{2,1,0:T(8,128)(2,1)S(1)}, u32[]{:S(2)}, u32[]{:S(2)}) collective-permute-start(bf16[4,256,128]{2,1,0:T(8,128)(2,1)S(1)} %get-tuple-element.102), channel_id=1, source_target_pairs={{0,8},{4,12},{8,0},{12,4},{16,24},{20,28},{24,16},{28,20},{1,9},{5... | collective-permute-start | bytes 786440 | tf_op jit(solution)/shard_map/ppermute | solution.py:369
  35.7 6.7 %collective-permute-start.15 = (bf16[4,256,128]{2,1,0:T(8,128)(2,1)S(1)}, bf16[4,256,128]{2,1,0:T(8,128)(2,1)S(1)}, u32[]{:S(2)}, u32[]{:S(2)}) collective-permute-start(bf16[4,256,128]{2,1,0:T(8,128)(2,1)S(1)} %get-tuple-element.114), channel_id=1, source_target_pairs={{0,1},{1,0},{2,3},{3,2},{4,5},{5,4},{6,7},{7,6},{8,16},{9,17},{10,... | collective-permute-start | bytes 786440 | tf_op jit(solution)/shard_map/ppermute | solution.py:392
  35.8 11.5 %collective-permute-start.14 = (bf16[4,256,128]{2,1,0:T(8,128)(2,1)S(1)}, bf16[4,256,128]{2,1,0:T(8,128)(2,1)S(1)}, u32[]{:S(2)}, u32[]{:S(2)}) collective-permute-start(bf16[4,256,128]{2,1,0:T(8,128)(2,1)S(1)} %get-tuple-element.113), channel_id=1, source_target_pairs={{0,8},{4,12},{8,0},{12,4},{16,24},{20,28},{24,16},{28,20},{1,9},{5... | collective-permute-start | bytes 786440 | tf_op jit(solution)/shard_map/ppermute | solution.py:369
  42.3 7.0 %collective-permute-start.18 = (bf16[4,256,128]{2,1,0:T(8,128)(2,1)S(1)}, bf16[4,256,128]{2,1,0:T(8,128)(2,1)S(1)}, u32[]{:S(2)}, u32[]{:S(2)}) collective-permute-start(bf16[4,256,128]{2,1,0:T(8,128)(2,1)S(1)} %get-tuple-element.121), channel_id=1, source_target_pairs={{0,1},{1,0},{2,3},{3,2},{4,5},{5,4},{6,7},{7,6},{8,16},{9,17},{10,... | collective-permute-start | bytes 786440 | tf_op jit(solution)/shard_map/ppermute | solution.py:392
  42.4 10.7 %collective-permute-start.17 = (bf16[4,256,128]{2,1,0:T(8,128)(2,1)S(1)}, bf16[4,256,128]{2,1,0:T(8,128)(2,1)S(1)}, u32[]{:S(2)}, u32[]{:S(2)}) collective-permute-start(bf16[4,256,128]{2,1,0:T(8,128)(2,1)S(1)} %get-tuple-element.120), channel_id=1, source_target_pairs={{0,8},{4,12},{8,0},{12,4},{16,24},{20,28},{24,16},{28,20},{1,9},{5... | collective-permute-start | bytes 786440 | tf_op jit(solution)/shard_map/ppermute | solution.py:369
  45.9 6.3 %collective-permute-start.13 = (bf16[2,256,128]{2,1,0:T(8,128)(2,1)S(1)}, bf16[2,256,128]{2,1,0:T(8,128)(2,1)S(1)}, u32[]{:S(2)}, u32[]{:S(2)}) collective-permute-start(bf16[2,256,128]{2,1,0:T(8,128)(2,1)S(1)} %get-tuple-element.111), channel_id=1, source_target_pairs={{0,4},{4,0},{8,12},{12,8},{16,20},{20,16},{24,28},{28,24},{1,5},{5... | collective-permute-start | bytes 393224 | tf_op jit(solution)/shard_map/ppermute | solution.py:382
  48.6 8.0 %collective-permute-start.16 = (bf16[4,256,128]{2,1,0:T(8,128)(2,1)S(1)}, bf16[4,256,128]{2,1,0:T(8,128)(2,1)S(1)}, u32[]{:S(2)}, u32[]{:S(2)}) collective-permute-start(bf16[4,256,128]{2,1,0:T(8,128)(2,1)S(1)} %get-tuple-element.118), channel_id=1, source_target_pairs={{0,4},{4,0},{8,12},{12,8},{16,20},{20,16},{24,28},{28,24},{1,5},{5... | collective-permute-start | bytes 786440 | tf_op jit(solution)/shard_map/ppermute | solution.py:382
  49.4 9.0 %collective-permute-start.20 = (bf16[4,256,128]{2,1,0:T(8,128)(2,1)S(1)}, bf16[4,256,128]{2,1,0:T(8,128)(2,1)S(1)}, u32[]{:S(2)}, u32[]{:S(2)}) collective-permute-start(bf16[4,256,128]{2,1,0:T(8,128)(2,1)S(1)} %get-tuple-element.127), channel_id=1, source_target_pairs={{0,8},{4,12},{8,0},{12,4},{16,24},{20,28},{24,16},{28,20},{1,9},{5... | collective-permute-start | bytes 786440 | tf_op jit(solution)/shard_map/ppermute | solution.py:369
  51.3 3.4 %collective-permute-start.21 = (bf16[2,256,128]{2,1,0:T(8,128)(2,1)S(1)}, bf16[2,256,128]{2,1,0:T(8,128)(2,1)S(1)}, u32[]{:S(2)}, u32[]{:S(2)}) collective-permute-start(bf16[2,256,128]{2,1,0:T(8,128)(2,1)S(1)} %get-tuple-element.128), channel_id=1, source_target_pairs={{0,1},{1,0},{2,3},{3,2},{4,5},{5,4},{6,7},{7,6},{8,16},{9,17},{10,... | collective-permute-start | bytes 393224 | tf_op jit(solution)/shard_map/ppermute | solution.py:392
  53.5 10.7 %copy-start.1 = (bf16[256,256]{1,0:T(8,128)(2,1)S(1)}, bf16[256,256]{1,0:T(8,128)(2,1)}, u32[]{:S(2)}) copy-start(bf16[256,256]{1,0:T(8,128)(2,1)} %refs_2_.3) | copy-start | bytes 393220
  53.5 10.7 %copy-start.3 = (f32[256]{0:T(256)S(1)}, f32[256]{0:T(256)}, u32[]{:S(2)}) copy-start(f32[256]{0:T(256)} %param.8) | copy-start | bytes 3076
  53.5 9.3 %collective-permute-start.19 = (bf16[4,256,128]{2,1,0:T(8,128)(2,1)S(1)}, bf16[4,256,128]{2,1,0:T(8,128)(2,1)S(1)}, u32[]{:S(2)}, u32[]{:S(2)}) collective-permute-start(bf16[4,256,128]{2,1,0:T(8,128)(2,1)S(1)} %get-tuple-element.125), channel_id=1, source_target_pairs={{0,4},{4,0},{8,12},{12,8},{16,20},{20,16},{24,28},{28,24},{1,5},{5... | collective-permute-start | bytes 786440 | tf_op jit(solution)/shard_map/ppermute | solution.py:382
  56.6 5.0 %collective-permute-start.23 = (bf16[2,256,128]{2,1,0:T(8,128)(2,1)S(1)}, bf16[2,256,128]{2,1,0:T(8,128)(2,1)S(1)}, u32[]{:S(2)}, u32[]{:S(2)}) collective-permute-start(bf16[2,256,128]{2,1,0:T(8,128)(2,1)S(1)} %get-tuple-element.133), channel_id=1, source_target_pairs={{0,8},{4,12},{8,0},{12,4},{16,24},{20,28},{24,16},{28,20},{1,9},{5... | collective-permute-start | bytes 393224 | tf_op jit(solution)/shard_map/ppermute | solution.py:369
  58.7 11.1 %collective-permute-start.22 = (bf16[4,256,128]{2,1,0:T(8,128)(2,1)S(1)}, bf16[4,256,128]{2,1,0:T(8,128)(2,1)S(1)}, u32[]{:S(2)}, u32[]{:S(2)}) collective-permute-start(bf16[4,256,128]{2,1,0:T(8,128)(2,1)S(1)} %get-tuple-element.131), channel_id=1, source_target_pairs={{0,4},{4,0},{8,12},{12,8},{16,20},{20,16},{24,28},{28,24},{1,5},{5... | collective-permute-start | bytes 786440 | tf_op jit(solution)/shard_map/ppermute | solution.py:382
  63.1 6.7 %collective-permute-start.24 = (bf16[2,256,128]{2,1,0:T(8,128)(2,1)S(1)}, bf16[2,256,128]{2,1,0:T(8,128)(2,1)S(1)}, u32[]{:S(2)}, u32[]{:S(2)}) collective-permute-start(bf16[2,256,128]{2,1,0:T(8,128)(2,1)S(1)} %get-tuple-element.135), channel_id=1, source_target_pairs={{0,4},{4,0},{8,12},{12,8},{16,20},{20,16},{24,28},{28,24},{1,5},{5... | collective-permute-start | bytes 393224 | tf_op jit(solution)/shard_map/ppermute | solution.py:382

commit v5 on v4

--- a/solution.py
+++ b/solution.py
@@ -22,10 +22,6 @@
     if half % 4 or half < 8:
         return [2] * (half // 2)
     return [2] + [4] * (half // 4 - 1) + [2]
-
-
-def row(ref, q, channels):
-    return ref[q * channels : (q + 1) * channels] if len(ref.shape) == 2 else ref[q]
 
 
 PAD = 16
@@ -145,20 +141,18 @@
                 place = (size - 2 - q) + low * (2 * q - size + 2)
                 for i in range(2):
                     value = drive[:, i * width : (i + 1) * width].astype(dtype)
-                    if len(outs[n].shape) == 2:
-                        begin = pl.multiple_of((place + i) * states, states)
+                    begin = pl.multiple_of((place + i) * states, states)
+                    if pair:
+                        flat = len(other_ref.shape) == 2
+                        other = other_ref[pl.ds(begin, states) if flat else place + i].astype(F32)
+                        outs[0][place + i] = jnp.where(low == 1, other, value)
+                        outs[1][place + i] = (
+                            coefs_ref[:, 1:2] * value + coefs_ref[:, 2:3] * other
+                        )
+                    elif len(outs[n].shape) == 2:
                         outs[n][pl.ds(begin, states)] = value
                     else:
                         outs[n][place + i] = value
-                    if pair:
-                        if len(other_ref.shape) == 2:
-                            begin = pl.multiple_of((place + i) * states, states)
-                            other = other_ref[pl.ds(begin, states)]
-                        else:
-                            other = other_ref[place + i]
-                        outs[1][place + i] = (
-                            coefs_ref[:, 1:2] * value + coefs_ref[:, 2:3] * other.astype(F32)
-                        )
                 for i in range(at + 4, min(at + 6, total + 2)):
                     shift(i)
             done += size
@@ -176,15 +170,12 @@
         own = own_ref[...]
         other = join_decays(first_ref[first.shape[0] - PAD :], own.shape[1])
         both = own * other
-        one, zero = jnp.ones_like(own), jnp.zeros_like(own)
+        one = jnp.ones_like(own)
         out[...] = columns(
             both,
             jnp.where(is_odd, one, other),
             jnp.where(is_odd, own, one),
-            jnp.where(is_odd, both, own),
-            jnp.where(is_odd, other, both),
-            jnp.where(is_odd, own, zero),
-            jnp.where(is_odd, zero, other),
+            jnp.where(is_odd, other, own),
         )
 
     shape = jax.ShapeDtypeStruct((own_decay.shape[1], 8), F32)
@@ -213,30 +204,30 @@
     return call(kernel, [shape], [group], operands, after, "carry_on")
 
 
-def states_of(group, coefs, keep, other, carries, after):
-    shape = jax.ShapeDtypeStruct(keep.shape, BF16)
-
-    def kernel(group_ref, coefs_ref, keep_ref, other_ref, *refs):
+def states_of(group, odd, coefs, first, pair, carries, after):
+    shape = jax.ShapeDtypeStruct(first.shape, BF16)
+
+    def kernel(group_ref, odd_ref, coefs_ref, first_ref, pair_ref, *refs):
         own, back = refs[-2:]
 
-        def settle(carry_ref):
-            for q in range(keep.shape[0]):
-                held, sent = keep_ref[q], row(other_ref, q, keep.shape[1]).astype(F32)
-                mine = held + coefs_ref[:, 5:6] * sent
-                theirs = coefs_ref[:, 6:7] * held + sent
+        def settle(carry_ref, of_even, of_odd):
+            for q in range(first.shape[0]):
+                even_state, odd_state = first_ref[q], pair_ref[q]
                 if carry_ref is not None:
                     carry = carry_ref[q].astype(F32)
-                    mine = mine + coefs_ref[:, 3:4] * carry
-                    theirs = theirs + coefs_ref[:, 4:5] * carry
-                own[q] = mine.astype(BF16)
-                back[q] = theirs.astype(BF16)
+                    even_state = even_state + coefs_ref[:, 3:4] * carry
+                    odd_state = odd_state + coefs_ref[:, 0:1] * carry
+                of_even[q] = even_state.astype(BF16)
+                of_odd[q] = odd_state.astype(BF16)
 
         for g in range(len(carries) + 1):
-            pl.when(group_ref[0] == g)(functools.partial(settle, refs[g - 1] if g else None))
-
-    return call(
-        kernel, [shape, shape], [group], [coefs, keep, other] + list(carries), after, "states_of"
-    )
+            carry_ref = refs[g - 1] if g else None
+            here = group_ref[0] == g
+            pl.when(here & (odd_ref[0] == 0))(functools.partial(settle, carry_ref, own, back))
+            pl.when(here & (odd_ref[0] == 1))(functools.partial(settle, carry_ref, back, own))
+
+    operands = [coefs, first, pair] + list(carries)
+    return call(kernel, [shape, shape], [group, odd], operands, after, "states_of")
 
 
 def output_half(lower, rows_in, weight, skip, states, earlier, after, dtype):
@@ -245,10 +236,11 @@
     pitch = channels + 1
     count = len(states)
     sizes = [value.shape[0] for value in states]
+    blocks = 4 if channels % 64 == 0 else 1
 
     def kernel(lower_ref, rows_ref, weight_ref, skip_ref, *refs):
         chunks = refs[:count]
-        out, total, tile, sem = refs[-4:]
+        out, total, tile, sems = refs[-4:]
         low = lower_ref[0]
         begin = pl.multiple_of(low * half, half)
         gain = columns(skip_ref[...])[:, 0:1]
@@ -273,10 +265,19 @@
                 tile[n * 8 + i] = total[pl.ds(n * 8 + i, half, stride=pitch), :].astype(dtype)
             return carry
 
-        lax.fori_loop(0, channels // 8, settle, 0, unroll=2)
-        last = pltpu.make_async_copy(tile, out.at[:, pl.ds(begin, half), :], sem)
-        last.start()
-        last.wait()
+        copies = []
+        size = channels // blocks
+        for n in range(blocks):
+            lax.fori_loop(n * size // 8, (n + 1) * size // 8, settle, 0, unroll=2)
+            part = pl.ds(n * size, size)
+            copies.append(
+                pltpu.make_async_copy(
+                    tile.at[part], out.at[part, pl.ds(begin, half), :], sems.at[n]
+                )
+            )
+            copies[-1].start()
+        for copy in copies:
+            copy.wait()
 
     operands = [rows_in, weight, skip] + list(states)
     more = {}
@@ -288,9 +289,9 @@
         [jax.ShapeDtypeStruct((channels, tile_rows, width), dtype)],
         [lower], operands, after, "output_half", 10,
         scratch=[
-            pltpu.VMEM((half * pitch + 8, width), F32),
+            pltpu.VMEM(((half + 1) * pitch + 7, width), F32),
             pltpu.VMEM((channels, half, width), dtype),
-            pltpu.SemaphoreType.DMA,
+            pltpu.SemaphoreType.DMA((blocks,)),
         ],
         specs=[VMEM] * (3 + count) + [ANY] * (len(operands) - 3 - count),
         out_specs=[ANY],
@@ -339,9 +340,9 @@
     coefs, token = coefficients(odd, decays, others[0], [token])
     held, drives = [], []
 
-    def pair_drive(k, token):
+    def pair_drive(k, token, after=[]):
         keep, drive, token = kept(
-            halos=halos if k == chunks - 1 else [], start=k, count=1, after=[token],
+            halos=halos if k == chunks - 1 else [], start=k, count=1, after=[token] + after,
             pair=[others[k], coefs],
         )
         held.append(keep)
@@ -351,8 +352,7 @@
     token = pair_drive(0, token)
     lag = 3 * ((groups - 2) // 2) + 1
     evens, odds, own, back = {}, {}, [], []
-    early_pairs = [chunks - 1]
-    waits = {("S", lag + 2): [0], ("E", lag + 3): [1], ("S", lag + chunks - 1): [chunks - 3]}
+    waits = {('O', lag + 1): [0], ('E', lag + 3): [1], ('S', lag + chunks - 1): [chunks - 3]}
 
     def held_up(kind, step):
         return [back[n] for n in waits.get((kind, step), []) if 0 <= n < len(back)]
@@ -364,7 +364,7 @@
             if 0 <= step - 3 * (g // 2) < chunks
         }
         if ready:
-            after = [token] + ([evens[0]] if step == 1 else []) + held_up('E', step)
+            after = [token] + [] + held_up('E', step)
             value, token = carry_on(group, coefs, ready, odds.get(step - 2), after)
             evens[step] = lax.ppermute(value, "tm", even_hop)
         if step == 0:
@@ -377,11 +377,9 @@
                 for g in range(1, groups)
             ]
             after = [token] + held_up('S', step)
-            mine, theirs, token = states_of(group, coefs, held[k], others[k], carries, after)
+            mine, theirs, token = states_of(group, odd, coefs, held[k], drives[k], carries, after)
             own.append(mine)
             back.append(lax.ppermute(theirs, "tm", swap))
-        if step + 1 in early_pairs:
-            token = pair_drive(step + 1, token)
         ready = {
             g: drives[step - 1 - 3 * ((g - 1) // 2)]
             for g in range(1, groups - 1, 2)
@@ -390,8 +388,8 @@
         if ready:
             value, token = carry_on(group, coefs, ready, evens[step - 1], [token] + held_up('O', step))
             odds[step] = lax.ppermute(value, ("tm", "space"), odd_hop)
-        if step + 1 < chunks and step + 1 not in early_pairs:
-            token = pair_drive(step + 1, token)
+        if step + 1 < chunks:
+            token = pair_drive(step + 1, token, [evens[0]] if step == 0 else [])
 
     skip = skip_gain[None]
     dtype = frames_in.dtype

time: 72.5 us -> 70.1 us (0.967)
  Pallas kernels: 18 us -> 15.6 us
    ppermute x5, waiting for transfers between devices: 7.79 us -> 4.19 us  [on_device(): back.append(lax.ppermute(theirs, 'tm', swap))]
    ppermute x8, starting transfers between devices: 16.3 us -> 13.5 us  [on_device(): evens[step] = lax.ppermute(value, 'tm', even_hop)]
    ppermute x5, starting transfers between devices: 6.48 us -> 9.02 us  [on_device(): back.append(lax.ppermute(theirs, 'tm', swap))]
    pallas_call x28, Pallas kernels: 18 us -> 15.6 us  [call(): pl.pallas_call(body, out_shape=list(out_shape) + [TOKEN], in_specs=[SMEM]...]
    ppermute x3, waiting for transfers between devices: 3.44 us -> 5.55 us  [on_device(): others += [lax.ppermute(value, 'tm', swap) for value in rest]]
    ppermute x8, waiting for transfers between devices: 5.05 us -> 6.67 us  [on_device(): evens[step] = lax.ppermute(value, 'tm', even_hop)]
  transfers between devices with their start and end apart: 25 -> 25, of which waited for: 10 -> 10; matrix products, arithmetic and copies ran while one was open for 0% -> 0% of each run, Pallas kernels for 19% -> 16%
where the time goes in v5:
time: 70.1 us; the launch traced here: 69.9 us
  starting transfers between devices  32.1 us (46%)
  waiting for transfers between devices  19.3 us (28%)
  Pallas kernels  15.6 us (22%)
  local copies, waits for them, and re-layouts  2.52 us (4%)
    pallas_call x28, Pallas kernels, call(): pl.pallas_call(body, out_shape=list(out_shape) + [TOKEN], in_specs=[SMEM]...  15.6 us
    ppermute x8, starting transfers between devices, on_device(): evens[step] = lax.ppermute(value, 'tm', even_hop)  13.5 us
    ppermute x5, starting transfers between devices, on_device(): back.append(lax.ppermute(theirs, 'tm', swap))  9.02 us
    ppermute x8, waiting for transfers between devices, on_device(): evens[step] = lax.ppermute(value, 'tm', even_hop)  6.67 us
    ppermute x3, waiting for transfers between devices, on_device(): others += [lax.ppermute(value, 'tm', swap) for value in rest]  5.55 us
    ppermute x3, starting transfers between devices, on_device(): others += [lax.ppermute(value, 'tm', swap) for value in rest]  4.54 us
    ppermute x5, waiting for transfers between devices, on_device(): back.append(lax.ppermute(theirs, 'tm', swap))  4.19 us
    ppermute x2, starting transfers between devices, on_device(): others = [lax.ppermute(value, 'tm', swap) for value in mine]  3 us
  transfers between devices with their start and end apart: 25, of which 10 were waited for; matrix products, arithmetic and copies ran while one was open for 0% of the time, Pallas kernels for 16%

profile of v5, /device:TPU:0, one launch (start us, length us, event | category | flops | bytes accessed | tf_op | source)
XLA Modules:
  0.0 69.9 jit_solution(9787709861111237355)
XLA Ops:
  0.0 2.5 %copy.9 = bf16[1,256,32,128]{3,1,2,0:T(8,128)(2,1)S(1)} copy(bf16[1,256,32,128]{3,2,1,0:T(8,128)(2,1)} %param.5) | data formatting | bytes 4194304 | tf_op args[0]
  2.5 2.2 %conv_chunks.7 = (bf16[528,128]{1,0:T(8,128)(2,1)}, bf16[4,256,128]{2,1,0:T(8,128)(2,1)}, bf16[256,128]{1,0:T(8,128)(2,1)}, bf16[256,128]{1,0:T(8,128)(2,1)}, f32[8,128]{1,0:T(8,128)S(1)}) custom-call(s32[1]{0:T(128)} %bitcast.refs_0_, s32[1]{0:T(128)} %bitcast.6.refs_1_, bf16[32,256,128]{2,1,0:T(8,128)(2,1)S(1)} %bitcast.12, ...), custom_call_target="tpu_custom_call" | custom-call | flops 1 | bytes 1 | tf_op jit(solution)/shard_map/conv_chunks/pallas_call | solution.py:68
  4.7 3.0 %collective-permute-start = (bf16[528,128]{1,0:T(8,128)(2,1)}, bf16[528,128]{1,0:T(8,128)(2,1)S(1)}, u32[]{:S(2)}, u32[]{:S(2)}) collective-permute-start(bf16[528,128]{1,0:T(8,128)(2,1)} %get-tuple-element.75), channel_id=1, source_target_pairs={{0,4},{4,0},{8,12},{12,8},{16,20},{20,16},{24,28},{28,24},{1,5},{5... | collective-permute-start | bytes 405512 | tf_op jit(solution)/shard_map/ppermute | solution.py:338
  7.7 0.0 collective-permute-start.2
  7.7 0.0 collective-permute-start.3
  7.7 1.7 %collective-permute-start.4 = (bf16[256,128]{1,0:T(8,128)(2,1)}, bf16[256,128]{1,0:T(8,128)(2,1)S(1)}, u32[]{:S(2)}, u32[]{:S(2)}) collective-permute-start(bf16[256,128]{1,0:T(8,128)(2,1)} %get-tuple-element.85), channel_id=1, source_target_pairs={{0,3},{1,0},{2,1},{3,2},{4,7},{5,4},{6,5},{7,6},{8,11},{9,8},{10,9... | collective-permute-start | bytes 196616 | tf_op jit(solution)/shard_map/ppermute | solution.py:339
  9.5 2.8 %collective-permute-done.refs_2_.refs_5_ = bf16[528,128]{1,0:T(8,128)(2,1)S(1)} collective-permute-done((bf16[528,128]{1,0:T(8,128)(2,1)}, bf16[528,128]{1,0:T(8,128)(2,1)S(1)}, u32[]{:S(2)}, u32[]{:S(2)}) %collective-permute-start) | collective-permute-done | bytes 135200 | tf_op jit(solution)/shard_map/ppermute | solution.py:338
  12.3 0.1 coefficients.1
  12.4 0.8 %conv_chunks.8 = (f32[2,256,128]{2,1,0:T(8,128)S(1)}, f32[2,256,128]{2,1,0:T(8,128)S(1)}, f32[8,128]{1,0:T(8,128)S(1)}) custom-call(s32[1]{0:T(128)} %bitcast.5.refs_0_.refs_1_, s32[1]{0:T(128)} %bitcast.8.refs_1_, bf16[32,256,128]{2,1,0:T(8,128)(2,1)S(1)} %bitcast.13, bf16[3,3,256,256]{3,2,1,0:T(8,128)(2,1)S(1)} %copy-done, f32[1,256]{1,0:T(1,128)S(1)} %copy-done.2, ...), custom_call_target="tpu_custom_call" | custom-call | flops 1 | bytes 1 | tf_op jit(solution)/shard_map/conv_chunks/pallas_call | solution.py:68
  13.2 2.2 %collective-permute-start.1 = (bf16[2,256,128]{2,1,0:T(8,128)(2,1)S(1)}, bf16[2,256,128]{2,1,0:T(8,128)(2,1)S(1)}, u32[]{:S(2)}, u32[]{:S(2)}) collective-permute-start(bf16[2,256,128]{2,1,0:T(8,128)(2,1)S(1)} %get-tuple-element.82), channel_id=1, source_target_pairs={{0,8},{4,12},{8,0},{12,4},{16,24},{20,28},{24,16},{28,20},{1,9},{5... | collective-permute-start | bytes 393224 | tf_op jit(solution)/shard_map/ppermute | solution.py:369
  15.4 0.0 collective-permute-done.3.refs_5_
  15.4 0.0 collective-permute-done.4.refs_6_
  15.4 2.3 %conv_chunks.9 = (bf16[4,256,128]{2,1,0:T(8,128)(2,1)S(1)}, bf16[4,256,128]{2,1,0:T(8,128)(2,1)S(1)}, bf16[2,256,128]{2,1,0:T(8,128)(2,1)S(1)}, f32[8,128]{1,0:T(8,128)S(1)}) custom-call(s32[1]{0:T(128)} %bitcast.refs_0_, s32[1]{0:T(128)} %bitcast.6.refs_1_, bf16[32,256,128]{2,1,0:T(8,128)(2,1)S(1)} %bitcast.14, bf16[3,3,256,256]{3,2,1,0:T(8,128)(2,1)S(1)} %copy-done, ...), custom_call_target="tpu_custom_call" | custom-call | flops 1 | bytes 1 | tf_op jit(solution)/shard_map/conv_chunks/pallas_call | solution.py:68
  17.7 1.6 %collective-permute-start.8 = (bf16[4,256,128]{2,1,0:T(8,128)(2,1)S(1)}, bf16[4,256,128]{2,1,0:T(8,128)(2,1)S(1)}, u32[]{:S(2)}, u32[]{:S(2)}) collective-permute-start(bf16[4,256,128]{2,1,0:T(8,128)(2,1)S(1)} %get-tuple-element.94), channel_id=1, source_target_pairs={{0,4},{4,0},{8,12},{12,8},{16,20},{20,16},{24,28},{28,24},{1,5},{5... | collective-permute-start | bytes 786440 | tf_op jit(solution)/shard_map/ppermute | solution.py:372
  19.3 0.0 collective-permute-done.2.refs_5_
  19.3 0.0 collective-permute-done.1.refs_8_.refs_3_.refs_5_
  19.3 2.1 %conv_chunks.10 = (f32[4,256,128]{2,1,0:T(8,128)S(1)}, f32[4,256,128]{2,1,0:T(8,128)S(1)}, f32[8,128]{1,0:T(8,128)S(1)}) custom-call(s32[1]{0:T(128)} %bitcast.5.refs_0_.refs_1_, s32[1]{0:T(128)} %bitcast.8.refs_1_, bf16[32,256,128]{2,1,0:T(8,128)(2,1)S(1)} %bitcast.15, bf16[3,3,256,256]{3,2,1,0:T(8,128)(2,1)S(1)} %copy-done, f32[1,256]{1,0:T(1,128)S(1)} %copy-done.2, ...), custom_call_target="tpu_custom_call" | custom-call | flops 1 | bytes 1 | tf_op jit(solution)/shard_map/conv_chunks/pallas_call | solution.py:68
  21.4 0.1 carry_on.14
  21.5 1.1 %collective-permute-start.7 = (bf16[4,256,128]{2,1,0:T(8,128)(2,1)S(1)}, bf16[4,256,128]{2,1,0:T(8,128)(2,1)S(1)}, u32[]{:S(2)}, u32[]{:S(2)}) collective-permute-start(bf16[4,256,128]{2,1,0:T(8,128)(2,1)S(1)} %get-tuple-element.93), channel_id=1, source_target_pairs={{0,8},{4,12},{8,0},{12,4},{16,24},{20,28},{24,16},{28,20},{1,9},{5... | collective-permute-start | bytes 786440 | tf_op jit(solution)/shard_map/ppermute | solution.py:369
  22.6 1.5 %collective-permute-start.6 = (bf16[4,256,128]{2,1,0:T(8,128)(2,1)S(1)}, bf16[4,256,128]{2,1,0:T(8,128)(2,1)S(1)}, u32[]{:S(2)}, u32[]{:S(2)}) collective-permute-start(bf16[4,256,128]{2,1,0:T(8,128)(2,1)S(1)} %get-tuple-element.92), channel_id=1, source_target_pairs={{0,4},{4,0},{8,12},{12,8},{16,20},{20,16},{24,28},{28,24},{1,5},{5... | collective-permute-start | bytes 786440 | tf_op jit(solution)/shard_map/ppermute | solution.py:372
  24.2 0.1 collective-permute-start.5
  24.3 1.2 %collective-permute-done.8.refs_5_ = bf16[4,256,128]{2,1,0:T(8,128)(2,1)S(1)} collective-permute-done((bf16[4,256,128]{2,1,0:T(8,128)(2,1)S(1)}, bf16[4,256,128]{2,1,0:T(8,128)(2,1)S(1)}, u32[]{:S(2)}, u32[]{:S(2)}) %collective-permute-start.8) | collective-permute-done | bytes 262176 | tf_op jit(solution)/shard_map/ppermute | solution.py:372
  25.4 1.2 %conv_chunks.11 = (f32[4,256,128]{2,1,0:T(8,128)S(1)}, f32[4,256,128]{2,1,0:T(8,128)S(1)}, f32[8,128]{1,0:T(8,128)S(1)}) custom-call(s32[1]{0:T(128)} %bitcast.5.refs_0_.refs_1_, s32[1]{0:T(128)} %bitcast.8.refs_1_, bf16[32,256,128]{2,1,0:T(8,128)(2,1)S(1)} %bitcast.16, bf16[3,3,256,256]{3,2,1,0:T(8,128)(2,1)S(1)} %copy-done, f32[1,256]{1,0:T(1,128)S(1)} %copy-done.2, ...), custom_call_target="tpu_custom_call" | custom-call | flops 1 | bytes 1 | tf_op jit(solution)/shard_map/conv_chunks/pallas_call | solution.py:68
  26.6 0.1 carry_on.16
  26.7 2.0 %collective-permute-start.11 = (bf16[4,256,128]{2,1,0:T(8,128)(2,1)S(1)}, bf16[4,256,128]{2,1,0:T(8,128)(2,1)S(1)}, u32[]{:S(2)}, u32[]{:S(2)}) collective-permute-start(bf16[4,256,128]{2,1,0:T(8,128)(2,1)S(1)} %get-tuple-element.104), channel_id=1, source_target_pairs={{0,8},{4,12},{8,0},{12,4},{16,24},{20,28},{24,16},{28,20},{1,9},{5... | collective-permute-start | bytes 786440 | tf_op jit(solution)/shard_map/ppermute | solution.py:369
  28.7 0.0 collective-permute-done.7.refs_3_.refs_5_
  28.8 0.1 collective-permute-start.12
  28.8 1.4 %collective-permute-done.6.refs_5_ = bf16[4,256,128]{2,1,0:T(8,128)(2,1)S(1)} collective-permute-done((bf16[4,256,128]{2,1,0:T(8,128)(2,1)S(1)}, bf16[4,256,128]{2,1,0:T(8,128)(2,1)S(1)}, u32[]{:S(2)}, u32[]{:S(2)}) %collective-permute-start.6) | collective-permute-done | bytes 262176 | tf_op jit(solution)/shard_map/ppermute | solution.py:372
  30.2 1.2 %conv_chunks.12 = (f32[4,256,128]{2,1,0:T(8,128)S(1)}, f32[4,256,128]{2,1,0:T(8,128)S(1)}, f32[8,128]{1,0:T(8,128)S(1)}) custom-call(s32[1]{0:T(128)} %bitcast.5.refs_0_.refs_1_, s32[1]{0:T(128)} %bitcast.8.refs_1_, bf16[32,256,128]{2,1,0:T(8,128)(2,1)S(1)} %bitcast.17, bf16[3,3,256,256]{3,2,1,0:T(8,128)(2,1)S(1)} %copy-done, f32[1,256]{1,0:T(1,128)S(1)} %copy-done.2, ...), custom_call_target="tpu_custom_call" | custom-call | flops 1 | bytes 1 | tf_op jit(solution)/shard_map/conv_chunks/pallas_call | solution.py:68
  31.4 0.1 carry_on.18
  31.5 1.9 %collective-permute-start.9 = (bf16[4,256,128]{2,1,0:T(8,128)(2,1)S(1)}, bf16[4,256,128]{2,1,0:T(8,128)(2,1)S(1)}, u32[]{:S(2)}, u32[]{:S(2)}) collective-permute-start(bf16[4,256,128]{2,1,0:T(8,128)(2,1)S(1)} %get-tuple-element.102), channel_id=1, source_target_pairs={{0,8},{4,12},{8,0},{12,4},{16,24},{20,28},{24,16},{28,20},{1,9},{5... | collective-permute-start | bytes 786440 | tf_op jit(solution)/shard_map/ppermute | solution.py:369
  33.4 1.4 %collective-permute-start.10 = (bf16[2,256,128]{2,1,0:T(8,128)(2,1)S(1)}, bf16[2,256,128]{2,1,0:T(8,128)(2,1)S(1)}, u32[]{:S(2)}, u32[]{:S(2)}) collective-permute-start(bf16[2,256,128]{2,1,0:T(8,128)(2,1)S(1)} %get-tuple-element.103), channel_id=1, source_target_pairs={{0,4},{4,0},{8,12},{12,8},{16,20},{20,16},{24,28},{28,24},{1,5},{5... | collective-permute-start | bytes 393224 | tf_op jit(solution)/shard_map/ppermute | solution.py:372
  34.8 0.4 collective-permute-done.11.refs_3_.refs_5_
  35.3 0.1 collective-permute-start.15
  35.4 3.0 %collective-permute-done.10.refs_7_ = bf16[2,256,128]{2,1,0:T(8,128)(2,1)S(1)} collective-permute-done((bf16[2,256,128]{2,1,0:T(8,128)(2,1)S(1)}, bf16[2,256,128]{2,1,0:T(8,128)(2,1)S(1)}, u32[]{:S(2)}, u32[]{:S(2)}) %collective-permute-start.10) | collective-permute-done | bytes 131104 | tf_op jit(solution)/shard_map/ppermute | solution.py:372
  38.3 0.8 %conv_chunks.13 = (f32[2,256,128]{2,1,0:T(8,128)S(1)}, f32[2,256,128]{2,1,0:T(8,128)S(1)}, f32[8,128]{1,0:T(8,128)S(1)}) custom-call(s32[1]{0:T(128)} %bitcast.5.refs_0_.refs_1_, s32[1]{0:T(128)} %bitcast.8.refs_1_, bf16[32,256,128]{2,1,0:T(8,128)(2,1)S(1)} %bitcast.18, bf16[3,3,256,256]{3,2,1,0:T(8,128)(2,1)S(1)} %copy-done, f32[1,256]{1,0:T(1,128)S(1)} %copy-done.2, ...), custom_call_target="tpu_custom_call" | custom-call | flops 1 | bytes 1 | tf_op jit(solution)/shard_map/conv_chunks/pallas_call | solution.py:68
  39.1 0.0 collective-permute-done.12.refs_4_.refs_6_
  39.1 0.1 carry_on.20
  39.2 0.3 collective-permute-start.14
  39.5 0.7 %collective-permute-done.9.refs_7_.refs_3_.refs_5_ = bf16[4,256,128]{2,1,0:T(8,128)(2,1)S(1)} collective-permute-done((bf16[4,256,128]{2,1,0:T(8,128)(2,1)S(1)}, bf16[4,256,128]{2,1,0:T(8,128)(2,1)S(1)}, u32[]{:S(2)}, u32[]{:S(2)}) %collective-permute-start.9) | collective-permute-done | bytes 262176 | tf_op jit(solution)/shard_map/ppermute | solution.py:369
  40.2 0.1 states_of.5
  40.3 0.2 carry_on.21
  40.5 0.1 collective-permute-start.18
  40.6 1.3 %collective-permute-start.13 = (bf16[2,256,128]{2,1,0:T(8,128)(2,1)S(1)}, bf16[2,256,128]{2,1,0:T(8,128)(2,1)S(1)}, u32[]{:S(2)}, u32[]{:S(2)}) collective-permute-start(bf16[2,256,128]{2,1,0:T(8,128)(2,1)S(1)} %get-tuple-element.111), channel_id=1, source_target_pairs={{0,4},{4,0},{8,12},{12,8},{16,20},{20,16},{24,28},{28,24},{1,5},{5... | collective-permute-start | bytes 393224 | tf_op jit(solution)/shard_map/ppermute | solution.py:382
  41.9 0.0 collective-permute-done.15.refs_3_.refs_6_
  42.0 3.0 %collective-permute-start.17 = (bf16[4,256,128]{2,1,0:T(8,128)(2,1)S(1)}, bf16[4,256,128]{2,1,0:T(8,128)(2,1)S(1)}, u32[]{:S(2)}, u32[]{:S(2)}) collective-permute-start(bf16[4,256,128]{2,1,0:T(8,128)(2,1)S(1)} %get-tuple-element.120), channel_id=1, source_target_pairs={{0,8},{4,12},{8,0},{12,4},{16,24},{20,28},{24,16},{28,20},{1,9},{5... | collective-permute-start | bytes 786440 | tf_op jit(solution)/shard_map/ppermute | solution.py:369
  44.9 1.4 %collective-permute-done.14.refs_7_.refs_3_.refs_5_ = bf16[4,256,128]{2,1,0:T(8,128)(2,1)S(1)} collective-permute-done((bf16[4,256,128]{2,1,0:T(8,128)(2,1)S(1)}, bf16[4,256,128]{2,1,0:T(8,128)(2,1)S(1)}, u32[]{:S(2)}, u32[]{:S(2)}) %collective-permute-start.14) | collective-permute-done | bytes 262176 | tf_op jit(solution)/shard_map/ppermute | solution.py:369
  46.4 0.1 states_of.6
  46.5 2.2 %collective-permute-start.16 = (bf16[4,256,128]{2,1,0:T(8,128)(2,1)S(1)}, bf16[4,256,128]{2,1,0:T(8,128)(2,1)S(1)}, u32[]{:S(2)}, u32[]{:S(2)}) collective-permute-start(bf16[4,256,128]{2,1,0:T(8,128)(2,1)S(1)} %get-tuple-element.118), channel_id=1, source_target_pairs={{0,4},{4,0},{8,12},{12,8},{16,20},{20,16},{24,28},{28,24},{1,5},{5... | collective-permute-start | bytes 786440 | tf_op jit(solution)/shard_map/ppermute | solution.py:382
  48.7 0.0 collective-permute-done.13.refs_5_.refs_4_
  48.8 1.4 %collective-permute-start.20 = (bf16[4,256,128]{2,1,0:T(8,128)(2,1)S(1)}, bf16[4,256,128]{2,1,0:T(8,128)(2,1)S(1)}, u32[]{:S(2)}, u32[]{:S(2)}) collective-permute-start(bf16[4,256,128]{2,1,0:T(8,128)(2,1)S(1)} %get-tuple-element.127), channel_id=1, source_target_pairs={{0,8},{4,12},{8,0},{12,4},{16,24},{20,28},{24,16},{28,20},{1,9},{5... | collective-permute-start | bytes 786440 | tf_op jit(solution)/shard_map/ppermute | solution.py:369
  50.2 1.9 %collective-permute-done.17.refs_7_ = bf16[4,256,128]{2,1,0:T(8,128)(2,1)S(1)} collective-permute-done((bf16[4,256,128]{2,1,0:T(8,128)(2,1)S(1)}, bf16[4,256,128]{2,1,0:T(8,128)(2,1)S(1)}, u32[]{:S(2)}, u32[]{:S(2)}) %collective-permute-start.17) | collective-permute-done | bytes 262176 | tf_op jit(solution)/shard_map/ppermute | solution.py:369
  52.2 0.1 states_of.7
  52.3 2.0 %collective-permute-start.19 = (bf16[4,256,128]{2,1,0:T(8,128)(2,1)S(1)}, bf16[4,256,128]{2,1,0:T(8,128)(2,1)S(1)}, u32[]{:S(2)}, u32[]{:S(2)}) collective-permute-start(bf16[4,256,128]{2,1,0:T(8,128)(2,1)S(1)} %get-tuple-element.125), channel_id=1, source_target_pairs={{0,4},{4,0},{8,12},{12,8},{16,20},{20,16},{24,28},{28,24},{1,5},{5... | collective-permute-start | bytes 786440 | tf_op jit(solution)/shard_map/ppermute | solution.py:382
  54.3 0.0 copy-start.3
  54.4 1.6 %collective-permute-start.23 = (bf16[2,256,128]{2,1,0:T(8,128)(2,1)S(1)}, bf16[2,256,128]{2,1,0:T(8,128)(2,1)S(1)}, u32[]{:S(2)}, u32[]{:S(2)}) collective-permute-start(bf16[2,256,128]{2,1,0:T(8,128)(2,1)S(1)} %get-tuple-element.133), channel_id=1, source_target_pairs={{0,8},{4,12},{8,0},{12,4},{16,24},{20,28},{24,16},{28,20},{1,9},{5... | collective-permute-start | bytes 393224 | tf_op jit(solution)/shard_map/ppermute | solution.py:369
  55.9 2.1 %collective-permute-done.20.refs_7_ = bf16[4,256,128]{2,1,0:T(8,128)(2,1)S(1)} collective-permute-done((bf16[4,256,128]{2,1,0:T(8,128)(2,1)S(1)}, bf16[4,256,128]{2,1,0:T(8,128)(2,1)S(1)}, u32[]{:S(2)}, u32[]{:S(2)}) %collective-permute-start.20) | collective-permute-done | bytes 262176 | tf_op jit(solution)/shard_map/ppermute | solution.py:369
  58.1 0.1 states_of.8
  58.2 1.7 %collective-permute-start.22 = (bf16[4,256,128]{2,1,0:T(8,128)(2,1)S(1)}, bf16[4,256,128]{2,1,0:T(8,128)(2,1)S(1)}, u32[]{:S(2)}, u32[]{:S(2)}) collective-permute-start(bf16[4,256,128]{2,1,0:T(8,128)(2,1)S(1)} %get-tuple-element.131), channel_id=1, source_target_pairs={{0,4},{4,0},{8,12},{12,8},{16,20},{20,16},{24,28},{28,24},{1,5},{5... | collective-permute-start | bytes 786440 | tf_op jit(solution)/shard_map/ppermute | solution.py:382
  59.9 0.1 states_of.9
  60.0 1.8 %collective-permute-start.24 = (bf16[2,256,128]{2,1,0:T(8,128)(2,1)S(1)}, bf16[2,256,128]{2,1,0:T(8,128)(2,1)S(1)}, u32[]{:S(2)}, u32[]{:S(2)}) collective-permute-start(bf16[2,256,128]{2,1,0:T(8,128)(2,1)S(1)} %get-tuple-element.135), channel_id=1, source_target_pairs={{0,4},{4,0},{8,12},{12,8},{16,20},{20,16},{24,28},{28,24},{1,5},{5... | collective-permute-start | bytes 393224 | tf_op jit(solution)/shard_map/ppermute | solution.py:382
  61.7 1.6 %output_half.2 = (bf16[256,32,128]{2,1,0:T(8,128)(2,1)}, f32[8,128]{1,0:T(8,128)S(1)}) custom-call(s32[1]{0:T(128)} %bitcast.5.refs_0_.refs_1_, bf16[32,256,128]{2,1,0:T(8,128)(2,1)S(1)} %bitcast.19, bf16[256,256]{1,0:T(8,128)(2,1)S(1)} %copy-done.1, f32[1,256]{1,0:T(1,128)S(1)} %bitcast.21, bf16[2,256,128]{2,1,0:T(8,128)(2,1)S(1)} %get-tuple-element.136.refs_4_, ...), custom_call_target="tpu_custom_call" | custom-call | flops 1 | bytes 1 | tf_op jit(solution)/shard_map/output_half/pallas_call | solution.py:68
  63.4 4.2 %collective-permute-done.24.refs_8_ = bf16[2,256,128]{2,1,0:T(8,128)(2,1)S(1)} collective-permute-done((bf16[2,256,128]{2,1,0:T(8,128)(2,1)S(1)}, bf16[2,256,128]{2,1,0:T(8,128)(2,1)S(1)}, u32[]{:S(2)}, u32[]{:S(2)}) %collective-permute-start.24) | collective-permute-done | bytes 131104 | tf_op jit(solution)/shard_map/ppermute | solution.py:382
  67.6 2.2 %output_half.3 = (bf16[256,32,128]{2,1,0:T(8,128)(2,1)}, f32[8,128]{1,0:T(8,128)}) custom-call(s32[1]{0:T(128)} %bitcast.refs_0_, bf16[32,256,128]{2,1,0:T(8,128)(2,1)S(1)} %bitcast.20, bf16[256,256]{1,0:T(8,128)(2,1)S(1)} %copy-done.1, f32[1,256]{1,0:T(1,128)S(1)} %bitcast.22, ...), custom_call_target="tpu_custom_call", output_to_operand_aliasing={{0}: (9, {})} | custom-call | flops 1 | bytes 1 | tf_op jit(solution)/shard_map/output_half/pallas_call | solution.py:68
  (23 shorter events, 0.3 us)
Async XLA Ops:
  0.0 2.5 %copy-start = (bf16[3,3,256,256]{3,2,1,0:T(8,128)(2,1)S(1)}, bf16[3,3,256,256]{3,2,1,0:T(8,128)(2,1)}, u32[]{:S(2)}) copy-start(bf16[3,3,256,256]{3,2,1,0:T(8,128)(2,1)} %refs_3_.13) | copy-start | bytes 3538948
  0.0 2.5 %copy-start.2 = (f32[1,256]{1,0:T(1,128)S(1)}, f32[1,256]{1,0:T(1,128)}, u32[]{:S(2)}) copy-start(f32[1,256]{1,0:T(1,128)} %refs_4_.13) | copy-start | bytes 3076
  4.7 7.6 %collective-permute-start = (bf16[528,128]{1,0:T(8,128)(2,1)}, bf16[528,128]{1,0:T(8,128)(2,1)S(1)}, u32[]{:S(2)}, u32[]{:S(2)}) collective-permute-start(bf16[528,128]{1,0:T(8,128)(2,1)} %get-tuple-element.75), channel_id=1, source_target_pairs={{0,4},{4,0},{8,12},{12,8},{16,20},{20,16},{24,28},{28,24},{1,5},{5... | collective-permute-start | bytes 405512 | tf_op jit(solution)/shard_map/ppermute | solution.py:338
  7.7 11.6 %collective-permute-start.2 = (bf16[4,256,128]{2,1,0:T(8,128)(2,1)}, bf16[4,256,128]{2,1,0:T(8,128)(2,1)}, u32[]{:S(2)}, u32[]{:S(2)}) collective-permute-start(bf16[4,256,128]{2,1,0:T(8,128)(2,1)} %get-tuple-element.83), channel_id=1, source_target_pairs={{0,4},{4,0},{8,12},{12,8},{16,20},{20,16},{24,28},{28,24},{1,5},{5... | collective-permute-start | bytes 786440 | tf_op jit(solution)/shard_map/ppermute | solution.py:338
  7.7 7.7 %collective-permute-start.3 = (bf16[256,128]{1,0:T(8,128)(2,1)}, bf16[256,128]{1,0:T(8,128)(2,1)S(1)}, u32[]{:S(2)}, u32[]{:S(2)}) collective-permute-start(bf16[256,128]{1,0:T(8,128)(2,1)} %get-tuple-element.84), channel_id=1, source_target_pairs={{0,1},{1,2},{2,3},{3,0},{4,5},{5,6},{6,7},{7,4},{8,9},{9,10},{10,1... | collective-permute-start | bytes 196616 | tf_op jit(solution)/shard_map/ppermute | solution.py:339
  7.7 7.7 %collective-permute-start.4 = (bf16[256,128]{1,0:T(8,128)(2,1)}, bf16[256,128]{1,0:T(8,128)(2,1)S(1)}, u32[]{:S(2)}, u32[]{:S(2)}) collective-permute-start(bf16[256,128]{1,0:T(8,128)(2,1)} %get-tuple-element.85), channel_id=1, source_target_pairs={{0,3},{1,0},{2,1},{3,2},{4,7},{5,4},{6,5},{7,6},{8,11},{9,8},{10,9... | collective-permute-start | bytes 196616 | tf_op jit(solution)/shard_map/ppermute | solution.py:339
  13.2 6.0 %collective-permute-start.1 = (bf16[2,256,128]{2,1,0:T(8,128)(2,1)S(1)}, bf16[2,256,128]{2,1,0:T(8,128)(2,1)S(1)}, u32[]{:S(2)}, u32[]{:S(2)}) collective-permute-start(bf16[2,256,128]{2,1,0:T(8,128)(2,1)S(1)} %get-tuple-element.82), channel_id=1, source_target_pairs={{0,8},{4,12},{8,0},{12,4},{16,24},{20,28},{24,16},{28,20},{1,9},{5... | collective-permute-start | bytes 393224 | tf_op jit(solution)/shard_map/ppermute | solution.py:369
  17.7 7.7 %collective-permute-start.8 = (bf16[4,256,128]{2,1,0:T(8,128)(2,1)S(1)}, bf16[4,256,128]{2,1,0:T(8,128)(2,1)S(1)}, u32[]{:S(2)}, u32[]{:S(2)}) collective-permute-start(bf16[4,256,128]{2,1,0:T(8,128)(2,1)S(1)} %get-tuple-element.94), channel_id=1, source_target_pairs={{0,4},{4,0},{8,12},{12,8},{16,20},{20,16},{24,28},{28,24},{1,5},{5... | collective-permute-start | bytes 786440 | tf_op jit(solution)/shard_map/ppermute | solution.py:372
  21.5 7.2 %collective-permute-start.7 = (bf16[4,256,128]{2,1,0:T(8,128)(2,1)S(1)}, bf16[4,256,128]{2,1,0:T(8,128)(2,1)S(1)}, u32[]{:S(2)}, u32[]{:S(2)}) collective-permute-start(bf16[4,256,128]{2,1,0:T(8,128)(2,1)S(1)} %get-tuple-element.93), channel_id=1, source_target_pairs={{0,8},{4,12},{8,0},{12,4},{16,24},{20,28},{24,16},{28,20},{1,9},{5... | collective-permute-start | bytes 786440 | tf_op jit(solution)/shard_map/ppermute | solution.py:369
  22.6 7.6 %collective-permute-start.6 = (bf16[4,256,128]{2,1,0:T(8,128)(2,1)S(1)}, bf16[4,256,128]{2,1,0:T(8,128)(2,1)S(1)}, u32[]{:S(2)}, u32[]{:S(2)}) collective-permute-start(bf16[4,256,128]{2,1,0:T(8,128)(2,1)S(1)} %get-tuple-element.92), channel_id=1, source_target_pairs={{0,4},{4,0},{8,12},{12,8},{16,20},{20,16},{24,28},{28,24},{1,5},{5... | collective-permute-start | bytes 786440 | tf_op jit(solution)/shard_map/ppermute | solution.py:372
  24.2 7.2 %collective-permute-start.5 = (bf16[2,256,128]{2,1,0:T(8,128)(2,1)S(1)}, bf16[2,256,128]{2,1,0:T(8,128)(2,1)S(1)}, u32[]{:S(2)}, u32[]{:S(2)}) collective-permute-start(bf16[2,256,128]{2,1,0:T(8,128)(2,1)S(1)} %get-tuple-element.91), channel_id=1, source_target_pairs={{0,1},{1,0},{2,3},{3,2},{4,5},{5,4},{6,7},{7,6},{8,16},{9,17},{10,... | collective-permute-start | bytes 393224 | tf_op jit(solution)/shard_map/ppermute | solution.py:390
  26.7 8.6 %collective-permute-start.11 = (bf16[4,256,128]{2,1,0:T(8,128)(2,1)S(1)}, bf16[4,256,128]{2,1,0:T(8,128)(2,1)S(1)}, u32[]{:S(2)}, u32[]{:S(2)}) collective-permute-start(bf16[4,256,128]{2,1,0:T(8,128)(2,1)S(1)} %get-tuple-element.104), channel_id=1, source_target_pairs={{0,8},{4,12},{8,0},{12,4},{16,24},{20,28},{24,16},{28,20},{1,9},{5... | collective-permute-start | bytes 786440 | tf_op jit(solution)/shard_map/ppermute | solution.py:369
  28.8 10.4 %collective-permute-start.12 = (bf16[4,256,128]{2,1,0:T(8,128)(2,1)S(1)}, bf16[4,256,128]{2,1,0:T(8,128)(2,1)S(1)}, u32[]{:S(2)}, u32[]{:S(2)}) collective-permute-start(bf16[4,256,128]{2,1,0:T(8,128)(2,1)S(1)} %get-tuple-element.108), channel_id=1, source_target_pairs={{0,1},{1,0},{2,3},{3,2},{4,5},{5,4},{6,7},{7,6},{8,16},{9,17},{10,... | collective-permute-start | bytes 786440 | tf_op jit(solution)/shard_map/ppermute | solution.py:390
  31.5 8.7 %collective-permute-start.9 = (bf16[4,256,128]{2,1,0:T(8,128)(2,1)S(1)}, bf16[4,256,128]{2,1,0:T(8,128)(2,1)S(1)}, u32[]{:S(2)}, u32[]{:S(2)}) collective-permute-start(bf16[4,256,128]{2,1,0:T(8,128)(2,1)S(1)} %get-tuple-element.102), channel_id=1, source_target_pairs={{0,8},{4,12},{8,0},{12,4},{16,24},{20,28},{24,16},{28,20},{1,9},{5... | collective-permute-start | bytes 786440 | tf_op jit(solution)/shard_map/ppermute | solution.py:369
  33.4 5.0 %collective-permute-start.10 = (bf16[2,256,128]{2,1,0:T(8,128)(2,1)S(1)}, bf16[2,256,128]{2,1,0:T(8,128)(2,1)S(1)}, u32[]{:S(2)}, u32[]{:S(2)}) collective-permute-start(bf16[2,256,128]{2,1,0:T(8,128)(2,1)S(1)} %get-tuple-element.103), channel_id=1, source_target_pairs={{0,4},{4,0},{8,12},{12,8},{16,20},{20,16},{24,28},{28,24},{1,5},{5... | collective-permute-start | bytes 393224 | tf_op jit(solution)/shard_map/ppermute | solution.py:372
  35.3 6.7 %collective-permute-start.15 = (bf16[4,256,128]{2,1,0:T(8,128)(2,1)S(1)}, bf16[4,256,128]{2,1,0:T(8,128)(2,1)S(1)}, u32[]{:S(2)}, u32[]{:S(2)}) collective-permute-start(bf16[4,256,128]{2,1,0:T(8,128)(2,1)S(1)} %get-tuple-element.114), channel_id=1, source_target_pairs={{0,1},{1,0},{2,3},{3,2},{4,5},{5,4},{6,7},{7,6},{8,16},{9,17},{10,... | collective-permute-start | bytes 786440 | tf_op jit(solution)/shard_map/ppermute | solution.py:390
  39.2 7.2 %collective-permute-start.14 = (bf16[4,256,128]{2,1,0:T(8,128)(2,1)S(1)}, bf16[4,256,128]{2,1,0:T(8,128)(2,1)S(1)}, u32[]{:S(2)}, u32[]{:S(2)}) collective-permute-start(bf16[4,256,128]{2,1,0:T(8,128)(2,1)S(1)} %get-tuple-element.113), channel_id=1, source_target_pairs={{0,8},{4,12},{8,0},{12,4},{16,24},{20,28},{24,16},{28,20},{1,9},{5... | collective-permute-start | bytes 786440 | tf_op jit(solution)/shard_map/ppermute | solution.py:369
  40.5 8.2 %collective-permute-start.18 = (bf16[4,256,128]{2,1,0:T(8,128)(2,1)S(1)}, bf16[4,256,128]{2,1,0:T(8,128)(2,1)S(1)}, u32[]{:S(2)}, u32[]{:S(2)}) collective-permute-start(bf16[4,256,128]{2,1,0:T(8,128)(2,1)S(1)} %get-tuple-element.121), channel_id=1, source_target_pairs={{0,1},{1,0},{2,3},{3,2},{4,5},{5,4},{6,7},{7,6},{8,16},{9,17},{10,... | collective-permute-start | bytes 786440 | tf_op jit(solution)/shard_map/ppermute | solution.py:390
  40.6 8.1 %collective-permute-start.13 = (bf16[2,256,128]{2,1,0:T(8,128)(2,1)S(1)}, bf16[2,256,128]{2,1,0:T(8,128)(2,1)S(1)}, u32[]{:S(2)}, u32[]{:S(2)}) collective-permute-start(bf16[2,256,128]{2,1,0:T(8,128)(2,1)S(1)} %get-tuple-element.111), channel_id=1, source_target_pairs={{0,4},{4,0},{8,12},{12,8},{16,20},{20,16},{24,28},{28,24},{1,5},{5... | collective-permute-start | bytes 393224 | tf_op jit(solution)/shard_map/ppermute | solution.py:382
  42.0 10.2 %collective-permute-start.17 = (bf16[4,256,128]{2,1,0:T(8,128)(2,1)S(1)}, bf16[4,256,128]{2,1,0:T(8,128)(2,1)S(1)}, u32[]{:S(2)}, u32[]{:S(2)}) collective-permute-start(bf16[4,256,128]{2,1,0:T(8,128)(2,1)S(1)} %get-tuple-element.120), channel_id=1, source_target_pairs={{0,8},{4,12},{8,0},{12,4},{16,24},{20,28},{24,16},{28,20},{1,9},{5... | collective-permute-start | bytes 786440 | tf_op jit(solution)/shard_map/ppermute | solution.py:369
  46.5 7.8 %collective-permute-start.16 = (bf16[4,256,128]{2,1,0:T(8,128)(2,1)S(1)}, bf16[4,256,128]{2,1,0:T(8,128)(2,1)S(1)}, u32[]{:S(2)}, u32[]{:S(2)}) collective-permute-start(bf16[4,256,128]{2,1,0:T(8,128)(2,1)S(1)} %get-tuple-element.118), channel_id=1, source_target_pairs={{0,4},{4,0},{8,12},{12,8},{16,20},{20,16},{24,28},{28,24},{1,5},{5... | collective-permute-start | bytes 786440 | tf_op jit(solution)/shard_map/ppermute | solution.py:382
  48.8 9.3 %collective-permute-start.20 = (bf16[4,256,128]{2,1,0:T(8,128)(2,1)S(1)}, bf16[4,256,128]{2,1,0:T(8,128)(2,1)S(1)}, u32[]{:S(2)}, u32[]{:S(2)}) collective-permute-start(bf16[4,256,128]{2,1,0:T(8,128)(2,1)S(1)} %get-tuple-element.127), channel_id=1, source_target_pairs={{0,8},{4,12},{8,0},{12,4},{16,24},{20,28},{24,16},{28,20},{1,9},{5... | collective-permute-start | bytes 786440 | tf_op jit(solution)/shard_map/ppermute | solution.py:369
  50.2 4.1 %collective-permute-start.21 = (bf16[2,256,128]{2,1,0:T(8,128)(2,1)S(1)}, bf16[2,256,128]{2,1,0:T(8,128)(2,1)S(1)}, u32[]{:S(2)}, u32[]{:S(2)}) collective-permute-start(bf16[2,256,128]{2,1,0:T(8,128)(2,1)S(1)} %get-tuple-element.128), channel_id=1, source_target_pairs={{0,1},{1,0},{2,3},{3,2},{4,5},{5,4},{6,7},{7,6},{8,16},{9,17},{10,... | collective-permute-start | bytes 393224 | tf_op jit(solution)/shard_map/ppermute | solution.py:390
  52.3 7.6 %collective-permute-start.19 = (bf16[4,256,128]{2,1,0:T(8,128)(2,1)S(1)}, bf16[4,256,128]{2,1,0:T(8,128)(2,1)S(1)}, u32[]{:S(2)}, u32[]{:S(2)}) collective-permute-start(bf16[4,256,128]{2,1,0:T(8,128)(2,1)S(1)} %get-tuple-element.125), channel_id=1, source_target_pairs={{0,4},{4,0},{8,12},{12,8},{16,20},{20,16},{24,28},{28,24},{1,5},{5... | collective-permute-start | bytes 786440 | tf_op jit(solution)/shard_map/ppermute | solution.py:382
  54.3 7.4 %copy-start.1 = (bf16[256,256]{1,0:T(8,128)(2,1)S(1)}, bf16[256,256]{1,0:T(8,128)(2,1)}, u32[]{:S(2)}) copy-start(bf16[256,256]{1,0:T(8,128)(2,1)} %refs_2_.3) | copy-start | bytes 393220
  54.3 7.4 %copy-start.3 = (f32[256]{0:T(256)S(1)}, f32[256]{0:T(256)}, u32[]{:S(2)}) copy-start(f32[256]{0:T(256)} %param.8) | copy-start | bytes 3076
  54.4 5.5 %collective-permute-start.23 = (bf16[2,256,128]{2,1,0:T(8,128)(2,1)S(1)}, bf16[2,256,128]{2,1,0:T(8,128)(2,1)S(1)}, u32[]{:S(2)}, u32[]{:S(2)}) collective-permute-start(bf16[2,256,128]{2,1,0:T(8,128)(2,1)S(1)} %get-tuple-element.133), channel_id=1, source_target_pairs={{0,8},{4,12},{8,0},{12,4},{16,24},{20,28},{24,16},{28,20},{1,9},{5... | collective-permute-start | bytes 393224 | tf_op jit(solution)/shard_map/ppermute | solution.py:369
  58.2 9.4 %collective-permute-start.22 = (bf16[4,256,128]{2,1,0:T(8,128)(2,1)S(1)}, bf16[4,256,128]{2,1,0:T(8,128)(2,1)S(1)}, u32[]{:S(2)}, u32[]{:S(2)}) collective-permute-start(bf16[4,256,128]{2,1,0:T(8,128)(2,1)S(1)} %get-tuple-element.131), channel_id=1, source_target_pairs={{0,4},{4,0},{8,12},{12,8},{16,20},{20,16},{24,28},{28,24},{1,5},{5... | collective-permute-start | bytes 786440 | tf_op jit(solution)/shard_map/ppermute | solution.py:382
  60.0 7.6 %collective-permute-start.24 = (bf16[2,256,128]{2,1,0:T(8,128)(2,1)S(1)}, bf16[2,256,128]{2,1,0:T(8,128)(2,1)S(1)}, u32[]{:S(2)}, u32[]{:S(2)}) collective-permute-start(bf16[2,256,128]{2,1,0:T(8,128)(2,1)S(1)} %get-tuple-element.135), channel_id=1, source_target_pairs={{0,4},{4,0},{8,12},{12,8},{16,20},{20,16},{24,28},{28,24},{1,5},{5... | collective-permute-start | bytes 393224 | tf_op jit(solution)/shard_map/ppermute | solution.py:382

commit v6 on v5

--- a/solution.py
+++ b/solution.py
@@ -230,22 +230,28 @@
     return call(kernel, [shape, shape], [group, odd], operands, after, "states_of")
 
 
-def output_half(lower, rows_in, weight, skip, states, earlier, after, dtype):
+def output_half(lower, rows_in, weight, skip, states, begun, earlier, after, dtype, finish=True):
     tile_rows, channels, width = rows_in.shape
     half = tile_rows // 2
     pitch = channels + 1
-    count = len(states)
-    sizes = [value.shape[0] for value in states]
+    sizes = sizes_of(half)
+    here = [n for n, value in enumerate(states) if value is not None]
+    count = len(here)
     blocks = 4 if channels % 64 == 0 else 1
+    held_rows = (half + 1) * pitch + 7
 
     def kernel(lower_ref, rows_ref, weight_ref, skip_ref, *refs):
-        chunks = refs[:count]
-        out, total, tile, sems = refs[-4:]
+        chunks = dict(zip(here, refs[:count]))
+        if finish:
+            total, tile, sems = refs[-3:]
+            out = refs[-4]
+        else:
+            total = refs[-1]
         low = lower_ref[0]
         begin = pl.multiple_of(low * half, half)
         gain = columns(skip_ref[...])[:, 0:1]
-        done = 0
-        for n, chunk in enumerate(chunks):
+        for n, chunk in chunks.items():
+            done = sum(sizes[:n])
             at_up = half - done - sizes[n]
             r = at_up + low * (done - at_up)
             for q in range(0, sizes[n], 2):
@@ -258,11 +264,24 @@
                     total[pl.ds((r + q + i) * pitch, channels), :] = value[
                         :, i * width : (i + 1) * width
                     ] + gain * rows_ref[begin + r + q + i].astype(F32)
-            done += sizes[n]
+        if not finish:
+            return
+        if begun is not None:
+            begun_ref = refs[count]
+            now = [sum(sizes[: here[0]]), sum(sizes[: here[-1] + 1])]
+            low_at = [half - now[1], half - now[0]]
+            first = low_at[0] + low * (now[0] - low_at[0])
+            last_row = low_at[1] + low * (now[1] - low_at[1])
+            at = lax.broadcasted_iota(jnp.int32, (half, width), 0)
+            fresh = (at >= first) & (at < last_row)
 
         def settle(n, carry):
             for i in range(8):
-                tile[n * 8 + i] = total[pl.ds(n * 8 + i, half, stride=pitch), :].astype(dtype)
+                value = total[pl.ds(n * 8 + i, half, stride=pitch), :]
+                if begun is not None:
+                    old = begun_ref[pl.ds(n * 8 + i, half, stride=pitch), :]
+                    value = jnp.where(fresh, value, old)
+                tile[n * 8 + i] = value.astype(dtype)
             return carry
 
         copies = []
@@ -279,21 +298,28 @@
         for copy in copies:
             copy.wait()
 
-    operands = [rows_in, weight, skip] + list(states)
+    operands = [rows_in, weight, skip] + [states[n] for n in here]
+    if begun is not None:
+        operands.append(begun)
+    in_place = len(operands)
     more = {}
     if earlier is not None:
         operands.append(earlier)
         more["input_output_aliases"] = {len(operands): 0}
+    specs = [VMEM] * in_place + [ANY] * (len(operands) - in_place)
+    if not finish:
+        shape = jax.ShapeDtypeStruct((held_rows, width), F32)
+        return call(kernel, [shape], [lower], operands, after, "output_begun", 10, specs=specs)
     return call(
         kernel,
         [jax.ShapeDtypeStruct((channels, tile_rows, width), dtype)],
         [lower], operands, after, "output_half", 10,
         scratch=[
-            pltpu.VMEM(((half + 1) * pitch + 7, width), F32),
+            pltpu.VMEM((held_rows, width), F32),
             pltpu.VMEM((channels, half, width), dtype),
             pltpu.SemaphoreType.DMA((blocks,)),
         ],
-        specs=[VMEM] * (3 + count) + [ANY] * (len(operands) - 3 - count),
+        specs=specs,
         out_specs=[ANY],
         **more,
     )
@@ -393,8 +419,16 @@
 
     skip = skip_gain[None]
     dtype = frames_in.dtype
-    half_done, token = output_half(odd, rows, out_weight, skip, own, None, [token], dtype)
-    result, token = output_half(even, rows, out_weight, skip, back, half_done, [token], dtype)
+    half_done, token = output_half(
+        odd, rows, out_weight, skip, own, None, None, [token], dtype
+    )
+    begun, token = output_half(
+        even, rows, out_weight, skip, back[:-2] + [None] * 2, None, None, [token], dtype, finish=False
+    )
+    result, token = output_half(
+        even, rows, out_weight, skip, [None] * (chunks - 2) + back[-2:], begun, half_done,
+        [token], dtype,
+    )
     return result[None]
 
 

time: 70.1 us -> 69.8 us (level)
    pallas_call x28 -> x29, Pallas kernels: 15.6 us -> 15.8 us  [call(): pl.pallas_call(body, out_shape=list(out_shape) + [TOKEN], in_specs=[SMEM]...]
  transfers between devices with their start and end apart: 25 -> 25, of which waited for: 10 -> 10; matrix products, arithmetic and copies ran while one was open for 0% -> 0% of each run, Pallas kernels for 16% -> 17%
where the time goes in v6:
time: 69.8 us; the launch traced here: 69.6 us
  starting transfers between devices  32 us (46%)
  waiting for transfers between devices  18.9 us (27%)
  Pallas kernels  15.8 us (23%)
  local copies, waits for them, and re-layouts  2.52 us (4%)
    pallas_call x29, Pallas kernels, call(): pl.pallas_call(body, out_shape=list(out_shape) + [TOKEN], in_specs=[SMEM]...  15.8 us
    ppermute x8, starting transfers between devices, on_device(): evens[step] = lax.ppermute(value, 'tm', even_hop)  13.5 us
    ppermute x5, starting transfers between devices, on_device(): back.append(lax.ppermute(theirs, 'tm', swap))  9.05 us
    ppermute x8, waiting for transfers between devices, on_device(): evens[step] = lax.ppermute(value, 'tm', even_hop)  6.75 us
    ppermute x3, waiting for transfers between devices, on_device(): others += [lax.ppermute(value, 'tm', swap) for value in rest]  5.64 us
    ppermute x3, starting transfers between devices, on_device(): others += [lax.ppermute(value, 'tm', swap) for value in rest]  4.49 us
    ppermute x5, waiting for transfers between devices, on_device(): back.append(lax.ppermute(theirs, 'tm', swap))  3.6 us
    ppermute x2, starting transfers between devices, on_device(): others = [lax.ppermute(value, 'tm', swap) for value in mine]  3 us
  transfers between devices with their start and end apart: 25, of which 10 were waited for; matrix products, arithmetic and copies ran while one was open for 0% of the time, Pallas kernels for 17%

profile of v6, /device:TPU:0, one launch (start us, length us, event | category | flops | bytes accessed | tf_op | source)
XLA Modules:
  0.0 69.6 jit_solution(17846642009863069911)
XLA Ops:
  0.0 2.5 %copy.9 = bf16[1,256,32,128]{3,1,2,0:T(8,128)(2,1)S(1)} copy(bf16[1,256,32,128]{3,2,1,0:T(8,128)(2,1)} %param.5) | data formatting | bytes 4194304 | tf_op args[0]
  2.5 2.2 %conv_chunks.7 = (bf16[528,128]{1,0:T(8,128)(2,1)}, bf16[4,256,128]{2,1,0:T(8,128)(2,1)}, bf16[256,128]{1,0:T(8,128)(2,1)}, bf16[256,128]{1,0:T(8,128)(2,1)}, f32[8,128]{1,0:T(8,128)S(1)}) custom-call(s32[1]{0:T(128)} %bitcast.refs_0_, s32[1]{0:T(128)} %bitcast.6.refs_1_, bf16[32,256,128]{2,1,0:T(8,128)(2,1)S(1)} %bitcast.12, ...), custom_call_target="tpu_custom_call" | custom-call | flops 1 | bytes 1 | tf_op jit(solution)/shard_map/conv_chunks/pallas_call | solution.py:68
  4.7 3.0 %collective-permute-start = (bf16[528,128]{1,0:T(8,128)(2,1)}, bf16[528,128]{1,0:T(8,128)(2,1)S(1)}, u32[]{:S(2)}, u32[]{:S(2)}) collective-permute-start(bf16[528,128]{1,0:T(8,128)(2,1)} %get-tuple-element.77), channel_id=1, source_target_pairs={{0,4},{4,0},{8,12},{12,8},{16,20},{20,16},{24,28},{28,24},{1,5},{5... | collective-permute-start | bytes 405512 | tf_op jit(solution)/shard_map/ppermute | solution.py:364
  7.7 0.0 collective-permute-start.4
  7.7 1.7 %collective-permute-start.2 = (bf16[256,128]{1,0:T(8,128)(2,1)}, bf16[256,128]{1,0:T(8,128)(2,1)S(1)}, u32[]{:S(2)}, u32[]{:S(2)}) collective-permute-start(bf16[256,128]{1,0:T(8,128)(2,1)} %get-tuple-element.81), channel_id=1, source_target_pairs={{0,3},{1,0},{2,1},{3,2},{4,7},{5,4},{6,5},{7,6},{8,11},{9,8},{10,9... | collective-permute-start | bytes 196616 | tf_op jit(solution)/shard_map/ppermute | solution.py:365
  9.5 2.8 %collective-permute-done.refs_2_.refs_5_ = bf16[528,128]{1,0:T(8,128)(2,1)S(1)} collective-permute-done((bf16[528,128]{1,0:T(8,128)(2,1)}, bf16[528,128]{1,0:T(8,128)(2,1)S(1)}, u32[]{:S(2)}, u32[]{:S(2)}) %collective-permute-start) | collective-permute-done | bytes 135200 | tf_op jit(solution)/shard_map/ppermute | solution.py:364
  12.3 0.1 coefficients.1
  12.5 0.8 %conv_chunks.8 = (f32[2,256,128]{2,1,0:T(8,128)S(1)}, f32[2,256,128]{2,1,0:T(8,128)S(1)}, f32[8,128]{1,0:T(8,128)S(1)}) custom-call(s32[1]{0:T(128)} %bitcast.5.refs_0_.refs_1_, s32[1]{0:T(128)} %bitcast.8.refs_1_, bf16[32,256,128]{2,1,0:T(8,128)(2,1)S(1)} %bitcast.13, bf16[3,3,256,256]{3,2,1,0:T(8,128)(2,1)S(1)} %copy-done, f32[1,256]{1,0:T(1,128)S(1)} %copy-done.2, ...), custom_call_target="tpu_custom_call" | custom-call | flops 1 | bytes 1 | tf_op jit(solution)/shard_map/conv_chunks/pallas_call | solution.py:68
  13.3 2.2 %collective-permute-start.5 = (bf16[2,256,128]{2,1,0:T(8,128)(2,1)S(1)}, bf16[2,256,128]{2,1,0:T(8,128)(2,1)S(1)}, u32[]{:S(2)}, u32[]{:S(2)}) collective-permute-start(bf16[2,256,128]{2,1,0:T(8,128)(2,1)S(1)} %get-tuple-element.89), channel_id=1, source_target_pairs={{0,8},{4,12},{8,0},{12,4},{16,24},{20,28},{24,16},{28,20},{1,9},{5... | collective-permute-start | bytes 393224 | tf_op jit(solution)/shard_map/ppermute | solution.py:395
  15.4 0.0 collective-permute-done.1.refs_5_
  15.4 0.0 collective-permute-done.2.refs_6_
  15.4 2.3 %conv_chunks.9 = (bf16[4,256,128]{2,1,0:T(8,128)(2,1)S(1)}, bf16[4,256,128]{2,1,0:T(8,128)(2,1)S(1)}, bf16[2,256,128]{2,1,0:T(8,128)(2,1)S(1)}, f32[8,128]{1,0:T(8,128)S(1)}) custom-call(s32[1]{0:T(128)} %bitcast.refs_0_, s32[1]{0:T(128)} %bitcast.6.refs_1_, bf16[32,256,128]{2,1,0:T(8,128)(2,1)S(1)} %bitcast.14, bf16[3,3,256,256]{3,2,1,0:T(8,128)(2,1)S(1)} %copy-done, ...), custom_call_target="tpu_custom_call" | custom-call | flops 1 | bytes 1 | tf_op jit(solution)/shard_map/conv_chunks/pallas_call | solution.py:68
  17.7 1.6 %collective-permute-start.7 = (bf16[4,256,128]{2,1,0:T(8,128)(2,1)S(1)}, bf16[4,256,128]{2,1,0:T(8,128)(2,1)S(1)}, u32[]{:S(2)}, u32[]{:S(2)}) collective-permute-start(bf16[4,256,128]{2,1,0:T(8,128)(2,1)S(1)} %get-tuple-element.93), channel_id=1, source_target_pairs={{0,4},{4,0},{8,12},{12,8},{16,20},{20,16},{24,28},{28,24},{1,5},{5... | collective-permute-start | bytes 786440 | tf_op jit(solution)/shard_map/ppermute | solution.py:398
  19.3 0.0 collective-permute-done.4.refs_5_
  19.3 0.0 collective-permute-done.5.refs_8_.refs_3_.refs_5_
  19.3 2.1 %conv_chunks.10 = (f32[4,256,128]{2,1,0:T(8,128)S(1)}, f32[4,256,128]{2,1,0:T(8,128)S(1)}, f32[8,128]{1,0:T(8,128)S(1)}) custom-call(s32[1]{0:T(128)} %bitcast.5.refs_0_.refs_1_, s32[1]{0:T(128)} %bitcast.8.refs_1_, bf16[32,256,128]{2,1,0:T(8,128)(2,1)S(1)} %bitcast.15, bf16[3,3,256,256]{3,2,1,0:T(8,128)(2,1)S(1)} %copy-done, f32[1,256]{1,0:T(1,128)S(1)} %copy-done.2, ...), custom_call_target="tpu_custom_call" | custom-call | flops 1 | bytes 1 | tf_op jit(solution)/shard_map/conv_chunks/pallas_call | solution.py:68
  21.4 0.1 carry_on.14
  21.5 1.1 %collective-permute-start.6 = (bf16[4,256,128]{2,1,0:T(8,128)(2,1)S(1)}, bf16[4,256,128]{2,1,0:T(8,128)(2,1)S(1)}, u32[]{:S(2)}, u32[]{:S(2)}) collective-permute-start(bf16[4,256,128]{2,1,0:T(8,128)(2,1)S(1)} %get-tuple-element.92), channel_id=1, source_target_pairs={{0,8},{4,12},{8,0},{12,4},{16,24},{20,28},{24,16},{28,20},{1,9},{5... | collective-permute-start | bytes 786440 | tf_op jit(solution)/shard_map/ppermute | solution.py:395
  22.7 1.5 %collective-permute-start.3 = (bf16[4,256,128]{2,1,0:T(8,128)(2,1)S(1)}, bf16[4,256,128]{2,1,0:T(8,128)(2,1)S(1)}, u32[]{:S(2)}, u32[]{:S(2)}) collective-permute-start(bf16[4,256,128]{2,1,0:T(8,128)(2,1)S(1)} %get-tuple-element.86), channel_id=1, source_target_pairs={{0,4},{4,0},{8,12},{12,8},{16,20},{20,16},{24,28},{28,24},{1,5},{5... | collective-permute-start | bytes 786440 | tf_op jit(solution)/shard_map/ppermute | solution.py:398
  24.2 0.1 collective-permute-start.8
  24.3 1.2 %collective-permute-done.7.refs_5_ = bf16[4,256,128]{2,1,0:T(8,128)(2,1)S(1)} collective-permute-done((bf16[4,256,128]{2,1,0:T(8,128)(2,1)S(1)}, bf16[4,256,128]{2,1,0:T(8,128)(2,1)S(1)}, u32[]{:S(2)}, u32[]{:S(2)}) %collective-permute-start.7) | collective-permute-done | bytes 262176 | tf_op jit(solution)/shard_map/ppermute | solution.py:398
  25.5 1.2 %conv_chunks.11 = (f32[4,256,128]{2,1,0:T(8,128)S(1)}, f32[4,256,128]{2,1,0:T(8,128)S(1)}, f32[8,128]{1,0:T(8,128)S(1)}) custom-call(s32[1]{0:T(128)} %bitcast.5.refs_0_.refs_1_, s32[1]{0:T(128)} %bitcast.8.refs_1_, bf16[32,256,128]{2,1,0:T(8,128)(2,1)S(1)} %bitcast.16, bf16[3,3,256,256]{3,2,1,0:T(8,128)(2,1)S(1)} %copy-done, f32[1,256]{1,0:T(1,128)S(1)} %copy-done.2, ...), custom_call_target="tpu_custom_call" | custom-call | flops 1 | bytes 1 | tf_op jit(solution)/shard_map/conv_chunks/pallas_call | solution.py:68
  26.6 0.1 carry_on.16
  26.7 2.0 %collective-permute-start.11 = (bf16[4,256,128]{2,1,0:T(8,128)(2,1)S(1)}, bf16[4,256,128]{2,1,0:T(8,128)(2,1)S(1)}, u32[]{:S(2)}, u32[]{:S(2)}) collective-permute-start(bf16[4,256,128]{2,1,0:T(8,128)(2,1)S(1)} %get-tuple-element.107), channel_id=1, source_target_pairs={{0,8},{4,12},{8,0},{12,4},{16,24},{20,28},{24,16},{28,20},{1,9},{5... | collective-permute-start | bytes 786440 | tf_op jit(solution)/shard_map/ppermute | solution.py:395
  28.7 0.0 collective-permute-done.6.refs_3_.refs_5_
  28.8 0.1 collective-permute-start.12
  28.8 1.4 %collective-permute-done.3.refs_5_ = bf16[4,256,128]{2,1,0:T(8,128)(2,1)S(1)} collective-permute-done((bf16[4,256,128]{2,1,0:T(8,128)(2,1)S(1)}, bf16[4,256,128]{2,1,0:T(8,128)(2,1)S(1)}, u32[]{:S(2)}, u32[]{:S(2)}) %collective-permute-start.3) | collective-permute-done | bytes 262176 | tf_op jit(solution)/shard_map/ppermute | solution.py:398
  30.3 1.2 %conv_chunks.12 = (f32[4,256,128]{2,1,0:T(8,128)S(1)}, f32[4,256,128]{2,1,0:T(8,128)S(1)}, f32[8,128]{1,0:T(8,128)S(1)}) custom-call(s32[1]{0:T(128)} %bitcast.5.refs_0_.refs_1_, s32[1]{0:T(128)} %bitcast.8.refs_1_, bf16[32,256,128]{2,1,0:T(8,128)(2,1)S(1)} %bitcast.17, bf16[3,3,256,256]{3,2,1,0:T(8,128)(2,1)S(1)} %copy-done, f32[1,256]{1,0:T(1,128)S(1)} %copy-done.2, ...), custom_call_target="tpu_custom_call" | custom-call | flops 1 | bytes 1 | tf_op jit(solution)/shard_map/conv_chunks/pallas_call | solution.py:68
  31.5 0.1 carry_on.18
  31.5 1.9 %collective-permute-start.9 = (bf16[4,256,128]{2,1,0:T(8,128)(2,1)S(1)}, bf16[4,256,128]{2,1,0:T(8,128)(2,1)S(1)}, u32[]{:S(2)}, u32[]{:S(2)}) collective-permute-start(bf16[4,256,128]{2,1,0:T(8,128)(2,1)S(1)} %get-tuple-element.104), channel_id=1, source_target_pairs={{0,8},{4,12},{8,0},{12,4},{16,24},{20,28},{24,16},{28,20},{1,9},{5... | collective-permute-start | bytes 786440 | tf_op jit(solution)/shard_map/ppermute | solution.py:395
  33.4 1.4 %collective-permute-start.10 = (bf16[2,256,128]{2,1,0:T(8,128)(2,1)S(1)}, bf16[2,256,128]{2,1,0:T(8,128)(2,1)S(1)}, u32[]{:S(2)}, u32[]{:S(2)}) collective-permute-start(bf16[2,256,128]{2,1,0:T(8,128)(2,1)S(1)} %get-tuple-element.106), channel_id=1, source_target_pairs={{0,4},{4,0},{8,12},{12,8},{16,20},{20,16},{24,28},{28,24},{1,5},{5... | collective-permute-start | bytes 393224 | tf_op jit(solution)/shard_map/ppermute | solution.py:398
  34.8 0.4 collective-permute-done.11.refs_3_.refs_5_
  35.3 0.1 collective-permute-start.15
  35.4 3.0 %collective-permute-done.10.refs_7_ = bf16[2,256,128]{2,1,0:T(8,128)(2,1)S(1)} collective-permute-done((bf16[2,256,128]{2,1,0:T(8,128)(2,1)S(1)}, bf16[2,256,128]{2,1,0:T(8,128)(2,1)S(1)}, u32[]{:S(2)}, u32[]{:S(2)}) %collective-permute-start.10) | collective-permute-done | bytes 131104 | tf_op jit(solution)/shard_map/ppermute | solution.py:398
  38.4 0.8 %conv_chunks.13 = (f32[2,256,128]{2,1,0:T(8,128)S(1)}, f32[2,256,128]{2,1,0:T(8,128)S(1)}, f32[8,128]{1,0:T(8,128)S(1)}) custom-call(s32[1]{0:T(128)} %bitcast.5.refs_0_.refs_1_, s32[1]{0:T(128)} %bitcast.8.refs_1_, bf16[32,256,128]{2,1,0:T(8,128)(2,1)S(1)} %bitcast.18, bf16[3,3,256,256]{3,2,1,0:T(8,128)(2,1)S(1)} %copy-done, f32[1,256]{1,0:T(1,128)S(1)} %copy-done.2, ...), custom_call_target="tpu_custom_call" | custom-call | flops 1 | bytes 1 | tf_op jit(solution)/shard_map/conv_chunks/pallas_call | solution.py:68
  39.2 0.1 carry_on.20
  39.2 0.2 collective-permute-start.14
  39.5 0.7 collective-permute-done.9.refs_7_.refs_3_.refs_5_
  40.2 0.1 states_of.5
  40.3 0.2 carry_on.21
  40.5 0.1 collective-permute-start.13
  40.6 1.4 %collective-permute-start.16 = (bf16[2,256,128]{2,1,0:T(8,128)(2,1)S(1)}, bf16[2,256,128]{2,1,0:T(8,128)(2,1)S(1)}, u32[]{:S(2)}, u32[]{:S(2)}) collective-permute-start(bf16[2,256,128]{2,1,0:T(8,128)(2,1)S(1)} %get-tuple-element.122), channel_id=1, source_target_pairs={{0,4},{4,0},{8,12},{12,8},{16,20},{20,16},{24,28},{28,24},{1,5},{5... | collective-permute-start | bytes 393224 | tf_op jit(solution)/shard_map/ppermute | solution.py:408
  42.0 3.1 %collective-permute-start.19 = (bf16[4,256,128]{2,1,0:T(8,128)(2,1)S(1)}, bf16[4,256,128]{2,1,0:T(8,128)(2,1)S(1)}, u32[]{:S(2)}, u32[]{:S(2)}) collective-permute-start(bf16[4,256,128]{2,1,0:T(8,128)(2,1)S(1)} %get-tuple-element.127), channel_id=1, source_target_pairs={{0,8},{4,12},{8,0},{12,4},{16,24},{20,28},{24,16},{28,20},{1,9},{5... | collective-permute-start | bytes 786440 | tf_op jit(solution)/shard_map/ppermute | solution.py:395
  45.1 1.3 %collective-permute-done.14.refs_7_.refs_3_.refs_5_ = bf16[4,256,128]{2,1,0:T(8,128)(2,1)S(1)} collective-permute-done((bf16[4,256,128]{2,1,0:T(8,128)(2,1)S(1)}, bf16[4,256,128]{2,1,0:T(8,128)(2,1)S(1)}, u32[]{:S(2)}, u32[]{:S(2)}) %collective-permute-start.14) | collective-permute-done | bytes 262176 | tf_op jit(solution)/shard_map/ppermute | solution.py:395
  46.4 0.1 states_of.6
  46.5 2.2 %collective-permute-start.20 = (bf16[4,256,128]{2,1,0:T(8,128)(2,1)S(1)}, bf16[4,256,128]{2,1,0:T(8,128)(2,1)S(1)}, u32[]{:S(2)}, u32[]{:S(2)}) collective-permute-start(bf16[4,256,128]{2,1,0:T(8,128)(2,1)S(1)} %get-tuple-element.130), channel_id=1, source_target_pairs={{0,4},{4,0},{8,12},{12,8},{16,20},{20,16},{24,28},{28,24},{1,5},{5... | collective-permute-start | bytes 786440 | tf_op jit(solution)/shard_map/ppermute | solution.py:408
  48.7 0.0 collective-permute-done.16.refs_5_.refs_4_
  48.8 1.3 %collective-permute-start.17 = (bf16[4,256,128]{2,1,0:T(8,128)(2,1)S(1)}, bf16[4,256,128]{2,1,0:T(8,128)(2,1)S(1)}, u32[]{:S(2)}, u32[]{:S(2)}) collective-permute-start(bf16[4,256,128]{2,1,0:T(8,128)(2,1)S(1)} %get-tuple-element.124), channel_id=1, source_target_pairs={{0,8},{4,12},{8,0},{12,4},{16,24},{20,28},{24,16},{28,20},{1,9},{5... | collective-permute-start | bytes 786440 | tf_op jit(solution)/shard_map/ppermute | solution.py:395
  50.2 2.2 %collective-permute-done.19.refs_7_ = bf16[4,256,128]{2,1,0:T(8,128)(2,1)S(1)} collective-permute-done((bf16[4,256,128]{2,1,0:T(8,128)(2,1)S(1)}, bf16[4,256,128]{2,1,0:T(8,128)(2,1)S(1)}, u32[]{:S(2)}, u32[]{:S(2)}) %collective-permute-start.19) | collective-permute-done | bytes 262176 | tf_op jit(solution)/shard_map/ppermute | solution.py:395
  52.4 0.1 states_of.7
  52.5 1.9 %collective-permute-start.23 = (bf16[4,256,128]{2,1,0:T(8,128)(2,1)S(1)}, bf16[4,256,128]{2,1,0:T(8,128)(2,1)S(1)}, u32[]{:S(2)}, u32[]{:S(2)}) collective-permute-start(bf16[4,256,128]{2,1,0:T(8,128)(2,1)S(1)} %get-tuple-element.136), channel_id=1, source_target_pairs={{0,4},{4,0},{8,12},{12,8},{16,20},{20,16},{24,28},{28,24},{1,5},{5... | collective-permute-start | bytes 786440 | tf_op jit(solution)/shard_map/ppermute | solution.py:408
  54.4 0.0 copy-start.3
  54.4 1.6 %collective-permute-start.22 = (bf16[2,256,128]{2,1,0:T(8,128)(2,1)S(1)}, bf16[2,256,128]{2,1,0:T(8,128)(2,1)S(1)}, u32[]{:S(2)}, u32[]{:S(2)}) collective-permute-start(bf16[2,256,128]{2,1,0:T(8,128)(2,1)S(1)} %get-tuple-element.134), channel_id=1, source_target_pairs={{0,8},{4,12},{8,0},{12,4},{16,24},{20,28},{24,16},{28,20},{1,9},{5... | collective-permute-start | bytes 393224 | tf_op jit(solution)/shard_map/ppermute | solution.py:395
  56.0 2.1 %collective-permute-done.17.refs_7_ = bf16[4,256,128]{2,1,0:T(8,128)(2,1)S(1)} collective-permute-done((bf16[4,256,128]{2,1,0:T(8,128)(2,1)S(1)}, bf16[4,256,128]{2,1,0:T(8,128)(2,1)S(1)}, u32[]{:S(2)}, u32[]{:S(2)}) %collective-permute-start.17) | collective-permute-done | bytes 262176 | tf_op jit(solution)/shard_map/ppermute | solution.py:395
  58.1 0.1 states_of.8
  58.3 1.6 %collective-permute-start.21 = (bf16[4,256,128]{2,1,0:T(8,128)(2,1)S(1)}, bf16[4,256,128]{2,1,0:T(8,128)(2,1)S(1)}, u32[]{:S(2)}, u32[]{:S(2)}) collective-permute-start(bf16[4,256,128]{2,1,0:T(8,128)(2,1)S(1)} %get-tuple-element.132), channel_id=1, source_target_pairs={{0,4},{4,0},{8,12},{12,8},{16,20},{20,16},{24,28},{28,24},{1,5},{5... | collective-permute-start | bytes 786440 | tf_op jit(solution)/shard_map/ppermute | solution.py:408
  59.9 0.0 collective-permute-done.22.refs_7_
  59.9 0.0 collective-permute-done.23.refs_9_.refs_6_
  59.9 0.1 states_of.9
  60.0 1.9 %collective-permute-start.24 = (bf16[2,256,128]{2,1,0:T(8,128)(2,1)S(1)}, bf16[2,256,128]{2,1,0:T(8,128)(2,1)S(1)}, u32[]{:S(2)}, u32[]{:S(2)}) collective-permute-start(bf16[2,256,128]{2,1,0:T(8,128)(2,1)S(1)} %get-tuple-element.137), channel_id=1, source_target_pairs={{0,4},{4,0},{8,12},{12,8},{16,20},{20,16},{24,28},{28,24},{1,5},{5... | collective-permute-start | bytes 393224 | tf_op jit(solution)/shard_map/ppermute | solution.py:408
  61.9 1.6 %output_half.2 = (bf16[256,32,128]{2,1,0:T(8,128)(2,1)}, f32[8,128]{1,0:T(8,128)S(1)}) custom-call(s32[1]{0:T(128)} %bitcast.5.refs_0_.refs_1_, bf16[32,256,128]{2,1,0:T(8,128)(2,1)S(1)} %bitcast.19, bf16[256,256]{1,0:T(8,128)(2,1)S(1)} %copy-done.1, f32[1,256]{1,0:T(1,128)S(1)} %bitcast.22, bf16[2,256,128]{2,1,0:T(8,128)(2,1)S(1)} %get-tuple-element.138.refs_4_, ...), custom_call_target="tpu_custom_call" | custom-call | flops 1 | bytes 1 | tf_op jit(solution)/shard_map/output_half/pallas_call | solution.py:68
  63.5 0.4 output_begun.1
  63.9 3.6 %collective-permute-done.24.refs_5_ = bf16[2,256,128]{2,1,0:T(8,128)(2,1)S(1)} collective-permute-done((bf16[2,256,128]{2,1,0:T(8,128)(2,1)S(1)}, bf16[2,256,128]{2,1,0:T(8,128)(2,1)S(1)}, u32[]{:S(2)}, u32[]{:S(2)}) %collective-permute-start.24) | collective-permute-done | bytes 131104 | tf_op jit(solution)/shard_map/ppermute | solution.py:408
  67.5 2.0 %output_half.3 = (bf16[256,32,128]{2,1,0:T(8,128)(2,1)}, f32[8,128]{1,0:T(8,128)}) custom-call(s32[1]{0:T(128)} %bitcast.refs_0_, bf16[32,256,128]{2,1,0:T(8,128)(2,1)S(1)} %bitcast.21, bf16[256,256]{1,0:T(8,128)(2,1)S(1)} %copy-done.1, f32[1,256]{1,0:T(1,128)S(1)} %bitcast.24, ...), custom_call_target="tpu_custom_call", output_to_operand_aliasing={{0}: (7, {})} | custom-call | flops 1 | bytes 1 | tf_op jit(solution)/shard_map/output_half/pallas_call | solution.py:68
  (24 shorter events, 0.3 us)
Async XLA Ops:
  0.0 2.5 %copy-start = (bf16[3,3,256,256]{3,2,1,0:T(8,128)(2,1)S(1)}, bf16[3,3,256,256]{3,2,1,0:T(8,128)(2,1)}, u32[]{:S(2)}) copy-start(bf16[3,3,256,256]{3,2,1,0:T(8,128)(2,1)} %refs_3_.13) | copy-start | bytes 3538948
  0.0 2.5 %copy-start.2 = (f32[1,256]{1,0:T(1,128)S(1)}, f32[1,256]{1,0:T(1,128)}, u32[]{:S(2)}) copy-start(f32[1,256]{1,0:T(1,128)} %refs_4_.13) | copy-start | bytes 3076
  4.7 7.6 %collective-permute-start = (bf16[528,128]{1,0:T(8,128)(2,1)}, bf16[528,128]{1,0:T(8,128)(2,1)S(1)}, u32[]{:S(2)}, u32[]{:S(2)}) collective-permute-start(bf16[528,128]{1,0:T(8,128)(2,1)} %get-tuple-element.77), channel_id=1, source_target_pairs={{0,4},{4,0},{8,12},{12,8},{16,20},{20,16},{24,28},{28,24},{1,5},{5... | collective-permute-start | bytes 405512 | tf_op jit(solution)/shard_map/ppermute | solution.py:364
  7.7 11.6 %collective-permute-start.4 = (bf16[4,256,128]{2,1,0:T(8,128)(2,1)}, bf16[4,256,128]{2,1,0:T(8,128)(2,1)}, u32[]{:S(2)}, u32[]{:S(2)}) collective-permute-start(bf16[4,256,128]{2,1,0:T(8,128)(2,1)} %get-tuple-element.87), channel_id=1, source_target_pairs={{0,4},{4,0},{8,12},{12,8},{16,20},{20,16},{24,28},{28,24},{1,5},{5... | collective-permute-start | bytes 786440 | tf_op jit(solution)/shard_map/ppermute | solution.py:364
  7.7 7.7 %collective-permute-start.1 = (bf16[256,128]{1,0:T(8,128)(2,1)}, bf16[256,128]{1,0:T(8,128)(2,1)S(1)}, u32[]{:S(2)}, u32[]{:S(2)}) collective-permute-start(bf16[256,128]{1,0:T(8,128)(2,1)} %get-tuple-element.80), channel_id=1, source_target_pairs={{0,1},{1,2},{2,3},{3,0},{4,5},{5,6},{6,7},{7,4},{8,9},{9,10},{10,1... | collective-permute-start | bytes 196616 | tf_op jit(solution)/shard_map/ppermute | solution.py:365
  7.7 7.7 %collective-permute-start.2 = (bf16[256,128]{1,0:T(8,128)(2,1)}, bf16[256,128]{1,0:T(8,128)(2,1)S(1)}, u32[]{:S(2)}, u32[]{:S(2)}) collective-permute-start(bf16[256,128]{1,0:T(8,128)(2,1)} %get-tuple-element.81), channel_id=1, source_target_pairs={{0,3},{1,0},{2,1},{3,2},{4,7},{5,4},{6,5},{7,6},{8,11},{9,8},{10,9... | collective-permute-start | bytes 196616 | tf_op jit(solution)/shard_map/ppermute | solution.py:365
  13.3 6.0 %collective-permute-start.5 = (bf16[2,256,128]{2,1,0:T(8,128)(2,1)S(1)}, bf16[2,256,128]{2,1,0:T(8,128)(2,1)S(1)}, u32[]{:S(2)}, u32[]{:S(2)}) collective-permute-start(bf16[2,256,128]{2,1,0:T(8,128)(2,1)S(1)} %get-tuple-element.89), channel_id=1, source_target_pairs={{0,8},{4,12},{8,0},{12,4},{16,24},{20,28},{24,16},{28,20},{1,9},{5... | collective-permute-start | bytes 393224 | tf_op jit(solution)/shard_map/ppermute | solution.py:395
  17.7 7.8 %collective-permute-start.7 = (bf16[4,256,128]{2,1,0:T(8,128)(2,1)S(1)}, bf16[4,256,128]{2,1,0:T(8,128)(2,1)S(1)}, u32[]{:S(2)}, u32[]{:S(2)}) collective-permute-start(bf16[4,256,128]{2,1,0:T(8,128)(2,1)S(1)} %get-tuple-element.93), channel_id=1, source_target_pairs={{0,4},{4,0},{8,12},{12,8},{16,20},{20,16},{24,28},{28,24},{1,5},{5... | collective-permute-start | bytes 786440 | tf_op jit(solution)/shard_map/ppermute | solution.py:398
  21.5 7.2 %collective-permute-start.6 = (bf16[4,256,128]{2,1,0:T(8,128)(2,1)S(1)}, bf16[4,256,128]{2,1,0:T(8,128)(2,1)S(1)}, u32[]{:S(2)}, u32[]{:S(2)}) collective-permute-start(bf16[4,256,128]{2,1,0:T(8,128)(2,1)S(1)} %get-tuple-element.92), channel_id=1, source_target_pairs={{0,8},{4,12},{8,0},{12,4},{16,24},{20,28},{24,16},{28,20},{1,9},{5... | collective-permute-start | bytes 786440 | tf_op jit(solution)/shard_map/ppermute | solution.py:395
  22.7 7.6 %collective-permute-start.3 = (bf16[4,256,128]{2,1,0:T(8,128)(2,1)S(1)}, bf16[4,256,128]{2,1,0:T(8,128)(2,1)S(1)}, u32[]{:S(2)}, u32[]{:S(2)}) collective-permute-start(bf16[4,256,128]{2,1,0:T(8,128)(2,1)S(1)} %get-tuple-element.86), channel_id=1, source_target_pairs={{0,4},{4,0},{8,12},{12,8},{16,20},{20,16},{24,28},{28,24},{1,5},{5... | collective-permute-start | bytes 786440 | tf_op jit(solution)/shard_map/ppermute | solution.py:398
  24.2 7.3 %collective-permute-start.8 = (bf16[2,256,128]{2,1,0:T(8,128)(2,1)S(1)}, bf16[2,256,128]{2,1,0:T(8,128)(2,1)S(1)}, u32[]{:S(2)}, u32[]{:S(2)}) collective-permute-start(bf16[2,256,128]{2,1,0:T(8,128)(2,1)S(1)} %get-tuple-element.102), channel_id=1, source_target_pairs={{0,1},{1,0},{2,3},{3,2},{4,5},{5,4},{6,7},{7,6},{8,16},{9,17},{10,... | collective-permute-start | bytes 393224 | tf_op jit(solution)/shard_map/ppermute | solution.py:416
  26.7 8.6 %collective-permute-start.11 = (bf16[4,256,128]{2,1,0:T(8,128)(2,1)S(1)}, bf16[4,256,128]{2,1,0:T(8,128)(2,1)S(1)}, u32[]{:S(2)}, u32[]{:S(2)}) collective-permute-start(bf16[4,256,128]{2,1,0:T(8,128)(2,1)S(1)} %get-tuple-element.107), channel_id=1, source_target_pairs={{0,8},{4,12},{8,0},{12,4},{16,24},{20,28},{24,16},{28,20},{1,9},{5... | collective-permute-start | bytes 786440 | tf_op jit(solution)/shard_map/ppermute | solution.py:395
  28.8 10.4 %collective-permute-start.12 = (bf16[4,256,128]{2,1,0:T(8,128)(2,1)S(1)}, bf16[4,256,128]{2,1,0:T(8,128)(2,1)S(1)}, u32[]{:S(2)}, u32[]{:S(2)}) collective-permute-start(bf16[4,256,128]{2,1,0:T(8,128)(2,1)S(1)} %get-tuple-element.111), channel_id=1, source_target_pairs={{0,1},{1,0},{2,3},{3,2},{4,5},{5,4},{6,7},{7,6},{8,16},{9,17},{10,... | collective-permute-start | bytes 786440 | tf_op jit(solution)/shard_map/ppermute | solution.py:416
  31.5 8.6 %collective-permute-start.9 = (bf16[4,256,128]{2,1,0:T(8,128)(2,1)S(1)}, bf16[4,256,128]{2,1,0:T(8,128)(2,1)S(1)}, u32[]{:S(2)}, u32[]{:S(2)}) collective-permute-start(bf16[4,256,128]{2,1,0:T(8,128)(2,1)S(1)} %get-tuple-element.104), channel_id=1, source_target_pairs={{0,8},{4,12},{8,0},{12,4},{16,24},{20,28},{24,16},{28,20},{1,9},{5... | collective-permute-start | bytes 786440 | tf_op jit(solution)/shard_map/ppermute | solution.py:395
  33.4 5.0 %collective-permute-start.10 = (bf16[2,256,128]{2,1,0:T(8,128)(2,1)S(1)}, bf16[2,256,128]{2,1,0:T(8,128)(2,1)S(1)}, u32[]{:S(2)}, u32[]{:S(2)}) collective-permute-start(bf16[2,256,128]{2,1,0:T(8,128)(2,1)S(1)} %get-tuple-element.106), channel_id=1, source_target_pairs={{0,4},{4,0},{8,12},{12,8},{16,20},{20,16},{24,28},{28,24},{1,5},{5... | collective-permute-start | bytes 393224 | tf_op jit(solution)/shard_map/ppermute | solution.py:398
  35.3 6.7 %collective-permute-start.15 = (bf16[4,256,128]{2,1,0:T(8,128)(2,1)S(1)}, bf16[4,256,128]{2,1,0:T(8,128)(2,1)S(1)}, u32[]{:S(2)}, u32[]{:S(2)}) collective-permute-start(bf16[4,256,128]{2,1,0:T(8,128)(2,1)S(1)} %get-tuple-element.118), channel_id=1, source_target_pairs={{0,1},{1,0},{2,3},{3,2},{4,5},{5,4},{6,7},{7,6},{8,16},{9,17},{10,... | collective-permute-start | bytes 786440 | tf_op jit(solution)/shard_map/ppermute | solution.py:416
  39.2 7.2 %collective-permute-start.14 = (bf16[4,256,128]{2,1,0:T(8,128)(2,1)S(1)}, bf16[4,256,128]{2,1,0:T(8,128)(2,1)S(1)}, u32[]{:S(2)}, u32[]{:S(2)}) collective-permute-start(bf16[4,256,128]{2,1,0:T(8,128)(2,1)S(1)} %get-tuple-element.116), channel_id=1, source_target_pairs={{0,8},{4,12},{8,0},{12,4},{16,24},{20,28},{24,16},{28,20},{1,9},{5... | collective-permute-start | bytes 786440 | tf_op jit(solution)/shard_map/ppermute | solution.py:395
  40.5 8.3 %collective-permute-start.13 = (bf16[4,256,128]{2,1,0:T(8,128)(2,1)S(1)}, bf16[4,256,128]{2,1,0:T(8,128)(2,1)S(1)}, u32[]{:S(2)}, u32[]{:S(2)}) collective-permute-start(bf16[4,256,128]{2,1,0:T(8,128)(2,1)S(1)} %get-tuple-element.115), channel_id=1, source_target_pairs={{0,1},{1,0},{2,3},{3,2},{4,5},{5,4},{6,7},{7,6},{8,16},{9,17},{10,... | collective-permute-start | bytes 786440 | tf_op jit(solution)/shard_map/ppermute | solution.py:416
  40.6 8.2 %collective-permute-start.16 = (bf16[2,256,128]{2,1,0:T(8,128)(2,1)S(1)}, bf16[2,256,128]{2,1,0:T(8,128)(2,1)S(1)}, u32[]{:S(2)}, u32[]{:S(2)}) collective-permute-start(bf16[2,256,128]{2,1,0:T(8,128)(2,1)S(1)} %get-tuple-element.122), channel_id=1, source_target_pairs={{0,4},{4,0},{8,12},{12,8},{16,20},{20,16},{24,28},{28,24},{1,5},{5... | collective-permute-start | bytes 393224 | tf_op jit(solution)/shard_map/ppermute | solution.py:408
  42.0 10.3 %collective-permute-start.19 = (bf16[4,256,128]{2,1,0:T(8,128)(2,1)S(1)}, bf16[4,256,128]{2,1,0:T(8,128)(2,1)S(1)}, u32[]{:S(2)}, u32[]{:S(2)}) collective-permute-start(bf16[4,256,128]{2,1,0:T(8,128)(2,1)S(1)} %get-tuple-element.127), channel_id=1, source_target_pairs={{0,8},{4,12},{8,0},{12,4},{16,24},{20,28},{24,16},{28,20},{1,9},{5... | collective-permute-start | bytes 786440 | tf_op jit(solution)/shard_map/ppermute | solution.py:395
  46.5 7.8 %collective-permute-start.20 = (bf16[4,256,128]{2,1,0:T(8,128)(2,1)S(1)}, bf16[4,256,128]{2,1,0:T(8,128)(2,1)S(1)}, u32[]{:S(2)}, u32[]{:S(2)}) collective-permute-start(bf16[4,256,128]{2,1,0:T(8,128)(2,1)S(1)} %get-tuple-element.130), channel_id=1, source_target_pairs={{0,4},{4,0},{8,12},{12,8},{16,20},{20,16},{24,28},{28,24},{1,5},{5... | collective-permute-start | bytes 786440 | tf_op jit(solution)/shard_map/ppermute | solution.py:408
  48.8 9.3 %collective-permute-start.17 = (bf16[4,256,128]{2,1,0:T(8,128)(2,1)S(1)}, bf16[4,256,128]{2,1,0:T(8,128)(2,1)S(1)}, u32[]{:S(2)}, u32[]{:S(2)}) collective-permute-start(bf16[4,256,128]{2,1,0:T(8,128)(2,1)S(1)} %get-tuple-element.124), channel_id=1, source_target_pairs={{0,8},{4,12},{8,0},{12,4},{16,24},{20,28},{24,16},{28,20},{1,9},{5... | collective-permute-start | bytes 786440 | tf_op jit(solution)/shard_map/ppermute | solution.py:395
  50.2 4.2 %collective-permute-start.18 = (bf16[2,256,128]{2,1,0:T(8,128)(2,1)S(1)}, bf16[2,256,128]{2,1,0:T(8,128)(2,1)S(1)}, u32[]{:S(2)}, u32[]{:S(2)}) collective-permute-start(bf16[2,256,128]{2,1,0:T(8,128)(2,1)S(1)} %get-tuple-element.125), channel_id=1, source_target_pairs={{0,1},{1,0},{2,3},{3,2},{4,5},{5,4},{6,7},{7,6},{8,16},{9,17},{10,... | collective-permute-start | bytes 393224 | tf_op jit(solution)/shard_map/ppermute | solution.py:416
  52.5 7.4 %collective-permute-start.23 = (bf16[4,256,128]{2,1,0:T(8,128)(2,1)S(1)}, bf16[4,256,128]{2,1,0:T(8,128)(2,1)S(1)}, u32[]{:S(2)}, u32[]{:S(2)}) collective-permute-start(bf16[4,256,128]{2,1,0:T(8,128)(2,1)S(1)} %get-tuple-element.136), channel_id=1, source_target_pairs={{0,4},{4,0},{8,12},{12,8},{16,20},{20,16},{24,28},{28,24},{1,5},{5... | collective-permute-start | bytes 786440 | tf_op jit(solution)/shard_map/ppermute | solution.py:408
  54.4 7.5 %copy-start.1 = (bf16[256,256]{1,0:T(8,128)(2,1)S(1)}, bf16[256,256]{1,0:T(8,128)(2,1)}, u32[]{:S(2)}) copy-start(bf16[256,256]{1,0:T(8,128)(2,1)} %refs_2_.5) | copy-start | bytes 393220
  54.4 7.5 %copy-start.3 = (f32[256]{0:T(256)S(1)}, f32[256]{0:T(256)}, u32[]{:S(2)}) copy-start(f32[256]{0:T(256)} %param.8) | copy-start | bytes 3076
  54.4 5.5 %collective-permute-start.22 = (bf16[2,256,128]{2,1,0:T(8,128)(2,1)S(1)}, bf16[2,256,128]{2,1,0:T(8,128)(2,1)S(1)}, u32[]{:S(2)}, u32[]{:S(2)}) collective-permute-start(bf16[2,256,128]{2,1,0:T(8,128)(2,1)S(1)} %get-tuple-element.134), channel_id=1, source_target_pairs={{0,8},{4,12},{8,0},{12,4},{16,24},{20,28},{24,16},{28,20},{1,9},{5... | collective-permute-start | bytes 393224 | tf_op jit(solution)/shard_map/ppermute | solution.py:395
  58.3 9.2 %collective-permute-start.21 = (bf16[4,256,128]{2,1,0:T(8,128)(2,1)S(1)}, bf16[4,256,128]{2,1,0:T(8,128)(2,1)S(1)}, u32[]{:S(2)}, u32[]{:S(2)}) collective-permute-start(bf16[4,256,128]{2,1,0:T(8,128)(2,1)S(1)} %get-tuple-element.132), channel_id=1, source_target_pairs={{0,4},{4,0},{8,12},{12,8},{16,20},{20,16},{24,28},{28,24},{1,5},{5... | collective-permute-start | bytes 786440 | tf_op jit(solution)/shard_map/ppermute | solution.py:408
  60.0 7.5 %collective-permute-start.24 = (bf16[2,256,128]{2,1,0:T(8,128)(2,1)S(1)}, bf16[2,256,128]{2,1,0:T(8,128)(2,1)S(1)}, u32[]{:S(2)}, u32[]{:S(2)}) collective-permute-start(bf16[2,256,128]{2,1,0:T(8,128)(2,1)S(1)} %get-tuple-element.137), channel_id=1, source_target_pairs={{0,4},{4,0},{8,12},{12,8},{16,20},{20,16},{24,28},{28,24},{1,5},{5... | collective-permute-start | bytes 393224 | tf_op jit(solution)/shard_map/ppermute | solution.py:408

commit v7 on v6

--- a/solution.py
+++ b/solution.py
@@ -189,7 +189,6 @@
 
     def kernel(group_ref, coefs_ref, *refs):
         out = refs[-1]
-        out[...] = jnp.zeros_like(out)
         for g, ref in zip(groups, refs):
 
             @pl.when(group_ref[0] == g)
@@ -287,7 +286,7 @@
         copies = []
         size = channels // blocks
         for n in range(blocks):
-            lax.fori_loop(n * size // 8, (n + 1) * size // 8, settle, 0, unroll=2)
+            lax.fori_loop(n * size // 8, (n + 1) * size // 8, settle, 0, unroll=4)
             part = pl.ds(n * size, size)
             copies.append(
                 pltpu.make_async_copy(

time: 69.8 us -> 69.6 us (level)
    ppermute x5, starting transfers between devices: 9.05 us -> 10.2 us  [on_device(): back.append(lax.ppermute(theirs, 'tm', swap))]
  transfers between devices with their start and end apart: 25 -> 25, of which waited for: 10 -> 11; matrix products, arithmetic and copies ran while one was open for 0% -> 0% of each run, Pallas kernels for 17% -> 16%
where the time goes in v7:
time: 69.6 us; the launch traced here: 69.5 us
  starting transfers between devices  32.4 us (47%)
  waiting for transfers between devices  18.7 us (27%)
  Pallas kernels  15.4 us (22%)
  local copies, waits for them, and re-layouts  2.52 us (4%)
    pallas_call x29, Pallas kernels, call(): pl.pallas_call(body, out_shape=list(out_shape) + [TOKEN], in_specs=[SMEM]...  15.4 us
    ppermute x8, starting transfers between devices, on_device(): evens[step] = lax.ppermute(value, 'tm', even_hop)  13 us
    ppermute x5, starting transfers between devices, on_device(): back.append(lax.ppermute(theirs, 'tm', swap))  10.2 us
    ppermute x8, waiting for transfers between devices, on_device(): evens[step] = lax.ppermute(value, 'tm', even_hop)  6.54 us
    ppermute x3, waiting for transfers between devices, on_device(): others += [lax.ppermute(value, 'tm', swap) for value in rest]  6.33 us
    ppermute x3, starting transfers between devices, on_device(): others += [lax.ppermute(value, 'tm', swap) for value in rest]  4.39 us
    ppermute x2, starting transfers between devices, on_device(): others = [lax.ppermute(value, 'tm', swap) for value in mine]  3 us
    ppermute x5, waiting for transfers between devices, on_device(): back.append(lax.ppermute(theirs, 'tm', swap))  2.99 us
  transfers between devices with their start and end apart: 25, of which 11 were waited for; matrix products, arithmetic and copies ran while one was open for 0% of the time, Pallas kernels for 16%

profile of v7, /device:TPU:0, one launch (start us, length us, event | category | flops | bytes accessed | tf_op | source)
XLA Modules:
  0.0 69.5 jit_solution(3101185305115558404)
XLA Ops:
  0.0 2.5 %copy.9 = bf16[1,256,32,128]{3,1,2,0:T(8,128)(2,1)S(1)} copy(bf16[1,256,32,128]{3,2,1,0:T(8,128)(2,1)} %param.5) | data formatting | bytes 4194304 | tf_op args[0]
  2.5 2.2 %conv_chunks.7 = (bf16[528,128]{1,0:T(8,128)(2,1)}, bf16[4,256,128]{2,1,0:T(8,128)(2,1)}, bf16[256,128]{1,0:T(8,128)(2,1)}, bf16[256,128]{1,0:T(8,128)(2,1)}, f32[8,128]{1,0:T(8,128)S(1)}) custom-call(s32[1]{0:T(128)} %bitcast.refs_0_, s32[1]{0:T(128)} %bitcast.6.refs_1_, bf16[32,256,128]{2,1,0:T(8,128)(2,1)S(1)} %bitcast.12, ...), custom_call_target="tpu_custom_call" | custom-call | flops 1 | bytes 1 | tf_op jit(solution)/shard_map/conv_chunks/pallas_call | solution.py:68
  4.7 3.0 %collective-permute-start = (bf16[528,128]{1,0:T(8,128)(2,1)}, bf16[528,128]{1,0:T(8,128)(2,1)S(1)}, u32[]{:S(2)}, u32[]{:S(2)}) collective-permute-start(bf16[528,128]{1,0:T(8,128)(2,1)} %get-tuple-element.77), channel_id=1, source_target_pairs={{0,4},{4,0},{8,12},{12,8},{16,20},{20,16},{24,28},{28,24},{1,5},{5... | collective-permute-start | bytes 405512 | tf_op jit(solution)/shard_map/ppermute | solution.py:363
  7.7 0.0 collective-permute-start.4
  7.7 0.0 collective-permute-start.1
  7.7 1.7 %collective-permute-start.2 = (bf16[256,128]{1,0:T(8,128)(2,1)}, bf16[256,128]{1,0:T(8,128)(2,1)S(1)}, u32[]{:S(2)}, u32[]{:S(2)}) collective-permute-start(bf16[256,128]{1,0:T(8,128)(2,1)} %get-tuple-element.81), channel_id=1, source_target_pairs={{0,3},{1,0},{2,1},{3,2},{4,7},{5,4},{6,5},{7,6},{8,11},{9,8},{10,9... | collective-permute-start | bytes 196616 | tf_op jit(solution)/shard_map/ppermute | solution.py:364
  9.5 2.8 %collective-permute-done.refs_2_.refs_5_ = bf16[528,128]{1,0:T(8,128)(2,1)S(1)} collective-permute-done((bf16[528,128]{1,0:T(8,128)(2,1)}, bf16[528,128]{1,0:T(8,128)(2,1)S(1)}, u32[]{:S(2)}, u32[]{:S(2)}) %collective-permute-start) | collective-permute-done | bytes 135200 | tf_op jit(solution)/shard_map/ppermute | solution.py:363
  12.3 0.1 coefficients.1
  12.5 0.8 %conv_chunks.8 = (f32[2,256,128]{2,1,0:T(8,128)S(1)}, f32[2,256,128]{2,1,0:T(8,128)S(1)}, f32[8,128]{1,0:T(8,128)S(1)}) custom-call(s32[1]{0:T(128)} %bitcast.5.refs_0_.refs_1_, s32[1]{0:T(128)} %bitcast.8.refs_1_, bf16[32,256,128]{2,1,0:T(8,128)(2,1)S(1)} %bitcast.13, bf16[3,3,256,256]{3,2,1,0:T(8,128)(2,1)S(1)} %copy-done, f32[1,256]{1,0:T(1,128)S(1)} %copy-done.2, ...), custom_call_target="tpu_custom_call" | custom-call | flops 1 | bytes 1 | tf_op jit(solution)/shard_map/conv_chunks/pallas_call | solution.py:68
  13.2 2.2 %collective-permute-start.5 = (bf16[2,256,128]{2,1,0:T(8,128)(2,1)S(1)}, bf16[2,256,128]{2,1,0:T(8,128)(2,1)S(1)}, u32[]{:S(2)}, u32[]{:S(2)}) collective-permute-start(bf16[2,256,128]{2,1,0:T(8,128)(2,1)S(1)} %get-tuple-element.89), channel_id=1, source_target_pairs={{0,8},{4,12},{8,0},{12,4},{16,24},{20,28},{24,16},{28,20},{1,9},{5... | collective-permute-start | bytes 393224 | tf_op jit(solution)/shard_map/ppermute | solution.py:394
  15.4 0.0 collective-permute-done.1.refs_5_
  15.4 0.0 collective-permute-done.2.refs_6_
  15.4 2.2 %conv_chunks.9 = (bf16[4,256,128]{2,1,0:T(8,128)(2,1)S(1)}, bf16[4,256,128]{2,1,0:T(8,128)(2,1)S(1)}, bf16[2,256,128]{2,1,0:T(8,128)(2,1)S(1)}, f32[8,128]{1,0:T(8,128)S(1)}) custom-call(s32[1]{0:T(128)} %bitcast.refs_0_, s32[1]{0:T(128)} %bitcast.6.refs_1_, bf16[32,256,128]{2,1,0:T(8,128)(2,1)S(1)} %bitcast.14, bf16[3,3,256,256]{3,2,1,0:T(8,128)(2,1)S(1)} %copy-done, ...), custom_call_target="tpu_custom_call" | custom-call | flops 1 | bytes 1 | tf_op jit(solution)/shard_map/conv_chunks/pallas_call | solution.py:68
  17.7 1.6 %collective-permute-start.7 = (bf16[4,256,128]{2,1,0:T(8,128)(2,1)S(1)}, bf16[4,256,128]{2,1,0:T(8,128)(2,1)S(1)}, u32[]{:S(2)}, u32[]{:S(2)}) collective-permute-start(bf16[4,256,128]{2,1,0:T(8,128)(2,1)S(1)} %get-tuple-element.93), channel_id=1, source_target_pairs={{0,4},{4,0},{8,12},{12,8},{16,20},{20,16},{24,28},{28,24},{1,5},{5... | collective-permute-start | bytes 786440 | tf_op jit(solution)/shard_map/ppermute | solution.py:397
  19.3 0.0 collective-permute-done.4.refs_5_
  19.3 0.0 collective-permute-done.5.refs_8_.refs_3_.refs_5_
  19.3 2.1 %conv_chunks.10 = (f32[4,256,128]{2,1,0:T(8,128)S(1)}, f32[4,256,128]{2,1,0:T(8,128)S(1)}, f32[8,128]{1,0:T(8,128)S(1)}) custom-call(s32[1]{0:T(128)} %bitcast.5.refs_0_.refs_1_, s32[1]{0:T(128)} %bitcast.8.refs_1_, bf16[32,256,128]{2,1,0:T(8,128)(2,1)S(1)} %bitcast.15, bf16[3,3,256,256]{3,2,1,0:T(8,128)(2,1)S(1)} %copy-done, f32[1,256]{1,0:T(1,128)S(1)} %copy-done.2, ...), custom_call_target="tpu_custom_call" | custom-call | flops 1 | bytes 1 | tf_op jit(solution)/shard_map/conv_chunks/pallas_call | solution.py:68
  21.4 1.2 %collective-permute-start.6 = (bf16[4,256,128]{2,1,0:T(8,128)(2,1)S(1)}, bf16[4,256,128]{2,1,0:T(8,128)(2,1)S(1)}, u32[]{:S(2)}, u32[]{:S(2)}) collective-permute-start(bf16[4,256,128]{2,1,0:T(8,128)(2,1)S(1)} %get-tuple-element.92), channel_id=1, source_target_pairs={{0,8},{4,12},{8,0},{12,4},{16,24},{20,28},{24,16},{28,20},{1,9},{5... | collective-permute-start | bytes 786440 | tf_op jit(solution)/shard_map/ppermute | solution.py:394
  22.6 1.5 %collective-permute-start.3 = (bf16[4,256,128]{2,1,0:T(8,128)(2,1)S(1)}, bf16[4,256,128]{2,1,0:T(8,128)(2,1)S(1)}, u32[]{:S(2)}, u32[]{:S(2)}) collective-permute-start(bf16[4,256,128]{2,1,0:T(8,128)(2,1)S(1)} %get-tuple-element.86), channel_id=1, source_target_pairs={{0,4},{4,0},{8,12},{12,8},{16,20},{20,16},{24,28},{28,24},{1,5},{5... | collective-permute-start | bytes 786440 | tf_op jit(solution)/shard_map/ppermute | solution.py:397
  24.1 0.0 collective-permute-start.8
  24.1 1.4 %collective-permute-done.7.refs_5_ = bf16[4,256,128]{2,1,0:T(8,128)(2,1)S(1)} collective-permute-done((bf16[4,256,128]{2,1,0:T(8,128)(2,1)S(1)}, bf16[4,256,128]{2,1,0:T(8,128)(2,1)S(1)}, u32[]{:S(2)}, u32[]{:S(2)}) %collective-permute-start.7) | collective-permute-done | bytes 262176 | tf_op jit(solution)/shard_map/ppermute | solution.py:397
  25.5 1.2 %conv_chunks.11 = (f32[4,256,128]{2,1,0:T(8,128)S(1)}, f32[4,256,128]{2,1,0:T(8,128)S(1)}, f32[8,128]{1,0:T(8,128)S(1)}) custom-call(s32[1]{0:T(128)} %bitcast.5.refs_0_.refs_1_, s32[1]{0:T(128)} %bitcast.8.refs_1_, bf16[32,256,128]{2,1,0:T(8,128)(2,1)S(1)} %bitcast.16, bf16[3,3,256,256]{3,2,1,0:T(8,128)(2,1)S(1)} %copy-done, f32[1,256]{1,0:T(1,128)S(1)} %copy-done.2, ...), custom_call_target="tpu_custom_call" | custom-call | flops 1 | bytes 1 | tf_op jit(solution)/shard_map/conv_chunks/pallas_call | solution.py:68
  26.7 1.8 %collective-permute-start.11 = (bf16[4,256,128]{2,1,0:T(8,128)(2,1)S(1)}, bf16[4,256,128]{2,1,0:T(8,128)(2,1)S(1)}, u32[]{:S(2)}, u32[]{:S(2)}) collective-permute-start(bf16[4,256,128]{2,1,0:T(8,128)(2,1)S(1)} %get-tuple-element.107), channel_id=1, source_target_pairs={{0,8},{4,12},{8,0},{12,4},{16,24},{20,28},{24,16},{28,20},{1,9},{5... | collective-permute-start | bytes 786440 | tf_op jit(solution)/shard_map/ppermute | solution.py:394
  28.6 0.0 collective-permute-done.6.refs_3_.refs_5_
  28.6 1.7 %collective-permute-done.3.refs_5_ = bf16[4,256,128]{2,1,0:T(8,128)(2,1)S(1)} collective-permute-done((bf16[4,256,128]{2,1,0:T(8,128)(2,1)S(1)}, bf16[4,256,128]{2,1,0:T(8,128)(2,1)S(1)}, u32[]{:S(2)}, u32[]{:S(2)}) %collective-permute-start.3) | collective-permute-done | bytes 262176 | tf_op jit(solution)/shard_map/ppermute | solution.py:397
  30.3 1.2 %conv_chunks.12 = (f32[4,256,128]{2,1,0:T(8,128)S(1)}, f32[4,256,128]{2,1,0:T(8,128)S(1)}, f32[8,128]{1,0:T(8,128)S(1)}) custom-call(s32[1]{0:T(128)} %bitcast.5.refs_0_.refs_1_, s32[1]{0:T(128)} %bitcast.8.refs_1_, bf16[32,256,128]{2,1,0:T(8,128)(2,1)S(1)} %bitcast.17, bf16[3,3,256,256]{3,2,1,0:T(8,128)(2,1)S(1)} %copy-done, f32[1,256]{1,0:T(1,128)S(1)} %copy-done.2, ...), custom_call_target="tpu_custom_call" | custom-call | flops 1 | bytes 1 | tf_op jit(solution)/shard_map/conv_chunks/pallas_call | solution.py:68
  31.4 0.0 collective-permute-done.8.refs_4_.refs_6_
  31.5 1.9 %collective-permute-start.9 = (bf16[4,256,128]{2,1,0:T(8,128)(2,1)S(1)}, bf16[4,256,128]{2,1,0:T(8,128)(2,1)S(1)}, u32[]{:S(2)}, u32[]{:S(2)}) collective-permute-start(bf16[4,256,128]{2,1,0:T(8,128)(2,1)S(1)} %get-tuple-element.104), channel_id=1, source_target_pairs={{0,8},{4,12},{8,0},{12,4},{16,24},{20,28},{24,16},{28,20},{1,9},{5... | collective-permute-start | bytes 786440 | tf_op jit(solution)/shard_map/ppermute | solution.py:394
  33.4 1.3 %collective-permute-start.10 = (bf16[2,256,128]{2,1,0:T(8,128)(2,1)S(1)}, bf16[2,256,128]{2,1,0:T(8,128)(2,1)S(1)}, u32[]{:S(2)}, u32[]{:S(2)}) collective-permute-start(bf16[2,256,128]{2,1,0:T(8,128)(2,1)S(1)} %get-tuple-element.106), channel_id=1, source_target_pairs={{0,4},{4,0},{8,12},{12,8},{16,20},{20,16},{24,28},{28,24},{1,5},{5... | collective-permute-start | bytes 393224 | tf_op jit(solution)/shard_map/ppermute | solution.py:397
  34.6 0.4 collective-permute-done.11.refs_3_.refs_5_
  35.1 0.0 collective-permute-start.15
  35.1 3.3 %collective-permute-done.10.refs_7_ = bf16[2,256,128]{2,1,0:T(8,128)(2,1)S(1)} collective-permute-done((bf16[2,256,128]{2,1,0:T(8,128)(2,1)S(1)}, bf16[2,256,128]{2,1,0:T(8,128)(2,1)S(1)}, u32[]{:S(2)}, u32[]{:S(2)}) %collective-permute-start.10) | collective-permute-done | bytes 131104 | tf_op jit(solution)/shard_map/ppermute | solution.py:397
  38.3 0.7 %conv_chunks.13 = (f32[2,256,128]{2,1,0:T(8,128)S(1)}, f32[2,256,128]{2,1,0:T(8,128)S(1)}, f32[8,128]{1,0:T(8,128)S(1)}) custom-call(s32[1]{0:T(128)} %bitcast.5.refs_0_.refs_1_, s32[1]{0:T(128)} %bitcast.8.refs_1_, bf16[32,256,128]{2,1,0:T(8,128)(2,1)S(1)} %bitcast.18, bf16[3,3,256,256]{3,2,1,0:T(8,128)(2,1)S(1)} %copy-done, f32[1,256]{1,0:T(1,128)S(1)} %copy-done.2, ...), custom_call_target="tpu_custom_call" | custom-call | flops 1 | bytes 1 | tf_op jit(solution)/shard_map/conv_chunks/pallas_call | solution.py:68
  39.1 0.0 collective-permute-done.12.refs_4_.refs_6_
  39.1 0.3 collective-permute-start.14
  39.4 0.4 collective-permute-done.9.refs_7_.refs_3_.refs_5_
  39.9 0.1 states_of.5
  39.9 0.2 carry_on.21
  40.1 0.1 collective-permute-start.13
  40.2 1.8 %collective-permute-start.16 = (bf16[2,256,128]{2,1,0:T(8,128)(2,1)S(1)}, bf16[2,256,128]{2,1,0:T(8,128)(2,1)S(1)}, u32[]{:S(2)}, u32[]{:S(2)}) collective-permute-start(bf16[2,256,128]{2,1,0:T(8,128)(2,1)S(1)} %get-tuple-element.122), channel_id=1, source_target_pairs={{0,4},{4,0},{8,12},{12,8},{16,20},{20,16},{24,28},{28,24},{1,5},{5... | collective-permute-start | bytes 393224 | tf_op jit(solution)/shard_map/ppermute | solution.py:407
  42.0 0.0 collective-permute-done.15.refs_3_.refs_6_
  42.0 3.0 %collective-permute-start.19 = (bf16[4,256,128]{2,1,0:T(8,128)(2,1)S(1)}, bf16[4,256,128]{2,1,0:T(8,128)(2,1)S(1)}, u32[]{:S(2)}, u32[]{:S(2)}) collective-permute-start(bf16[4,256,128]{2,1,0:T(8,128)(2,1)S(1)} %get-tuple-element.127), channel_id=1, source_target_pairs={{0,8},{4,12},{8,0},{12,4},{16,24},{20,28},{24,16},{28,20},{1,9},{5... | collective-permute-start | bytes 786440 | tf_op jit(solution)/shard_map/ppermute | solution.py:394
  45.0 1.3 %collective-permute-done.14.refs_7_.refs_3_.refs_5_ = bf16[4,256,128]{2,1,0:T(8,128)(2,1)S(1)} collective-permute-done((bf16[4,256,128]{2,1,0:T(8,128)(2,1)S(1)}, bf16[4,256,128]{2,1,0:T(8,128)(2,1)S(1)}, u32[]{:S(2)}, u32[]{:S(2)}) %collective-permute-start.14) | collective-permute-done | bytes 262176 | tf_op jit(solution)/shard_map/ppermute | solution.py:394
  46.3 0.1 states_of.6
  46.4 2.4 %collective-permute-start.20 = (bf16[4,256,128]{2,1,0:T(8,128)(2,1)S(1)}, bf16[4,256,128]{2,1,0:T(8,128)(2,1)S(1)}, u32[]{:S(2)}, u32[]{:S(2)}) collective-permute-start(bf16[4,256,128]{2,1,0:T(8,128)(2,1)S(1)} %get-tuple-element.130), channel_id=1, source_target_pairs={{0,4},{4,0},{8,12},{12,8},{16,20},{20,16},{24,28},{28,24},{1,5},{5... | collective-permute-start | bytes 786440 | tf_op jit(solution)/shard_map/ppermute | solution.py:407
  48.8 1.2 %collective-permute-start.17 = (bf16[4,256,128]{2,1,0:T(8,128)(2,1)S(1)}, bf16[4,256,128]{2,1,0:T(8,128)(2,1)S(1)}, u32[]{:S(2)}, u32[]{:S(2)}) collective-permute-start(bf16[4,256,128]{2,1,0:T(8,128)(2,1)S(1)} %get-tuple-element.124), channel_id=1, source_target_pairs={{0,8},{4,12},{8,0},{12,4},{16,24},{20,28},{24,16},{28,20},{1,9},{5... | collective-permute-start | bytes 786440 | tf_op jit(solution)/shard_map/ppermute | solution.py:394
  50.0 0.0 collective-permute-start.18
  50.0 2.3 %collective-permute-done.19.refs_7_ = bf16[4,256,128]{2,1,0:T(8,128)(2,1)S(1)} collective-permute-done((bf16[4,256,128]{2,1,0:T(8,128)(2,1)S(1)}, bf16[4,256,128]{2,1,0:T(8,128)(2,1)S(1)}, u32[]{:S(2)}, u32[]{:S(2)}) %collective-permute-start.19) | collective-permute-done | bytes 262176 | tf_op jit(solution)/shard_map/ppermute | solution.py:394
  52.3 0.1 states_of.7
  52.4 2.1 %collective-permute-start.23 = (bf16[4,256,128]{2,1,0:T(8,128)(2,1)S(1)}, bf16[4,256,128]{2,1,0:T(8,128)(2,1)S(1)}, u32[]{:S(2)}, u32[]{:S(2)}) collective-permute-start(bf16[4,256,128]{2,1,0:T(8,128)(2,1)S(1)} %get-tuple-element.136), channel_id=1, source_target_pairs={{0,4},{4,0},{8,12},{12,8},{16,20},{20,16},{24,28},{28,24},{1,5},{5... | collective-permute-start | bytes 786440 | tf_op jit(solution)/shard_map/ppermute | solution.py:407
  54.4 0.0 collective-permute-done.18.refs_3_.refs_6_
  54.4 0.0 collective-permute-done.20.refs_5_
  54.4 0.0 copy-start.3
  54.5 1.5 %collective-permute-start.22 = (bf16[2,256,128]{2,1,0:T(8,128)(2,1)S(1)}, bf16[2,256,128]{2,1,0:T(8,128)(2,1)S(1)}, u32[]{:S(2)}, u32[]{:S(2)}) collective-permute-start(bf16[2,256,128]{2,1,0:T(8,128)(2,1)S(1)} %get-tuple-element.134), channel_id=1, source_target_pairs={{0,8},{4,12},{8,0},{12,4},{16,24},{20,28},{24,16},{28,20},{1,9},{5... | collective-permute-start | bytes 393224 | tf_op jit(solution)/shard_map/ppermute | solution.py:394
  56.0 2.2 %collective-permute-done.17.refs_7_ = bf16[4,256,128]{2,1,0:T(8,128)(2,1)S(1)} collective-permute-done((bf16[4,256,128]{2,1,0:T(8,128)(2,1)S(1)}, bf16[4,256,128]{2,1,0:T(8,128)(2,1)S(1)}, u32[]{:S(2)}, u32[]{:S(2)}) %collective-permute-start.17) | collective-permute-done | bytes 262176 | tf_op jit(solution)/shard_map/ppermute | solution.py:394
  58.2 0.1 states_of.8
  58.3 1.4 %collective-permute-start.21 = (bf16[4,256,128]{2,1,0:T(8,128)(2,1)S(1)}, bf16[4,256,128]{2,1,0:T(8,128)(2,1)S(1)}, u32[]{:S(2)}, u32[]{:S(2)}) collective-permute-start(bf16[4,256,128]{2,1,0:T(8,128)(2,1)S(1)} %get-tuple-element.132), channel_id=1, source_target_pairs={{0,4},{4,0},{8,12},{12,8},{16,20},{20,16},{24,28},{28,24},{1,5},{5... | collective-permute-start | bytes 786440 | tf_op jit(solution)/shard_map/ppermute | solution.py:407
  59.7 0.2 collective-permute-done.23.refs_9_.refs_6_
  59.9 0.1 states_of.9
  59.9 2.5 %collective-permute-start.24 = (bf16[2,256,128]{2,1,0:T(8,128)(2,1)S(1)}, bf16[2,256,128]{2,1,0:T(8,128)(2,1)S(1)}, u32[]{:S(2)}, u32[]{:S(2)}) collective-permute-start(bf16[2,256,128]{2,1,0:T(8,128)(2,1)S(1)} %get-tuple-element.137), channel_id=1, source_target_pairs={{0,4},{4,0},{8,12},{12,8},{16,20},{20,16},{24,28},{28,24},{1,5},{5... | collective-permute-start | bytes 393224 | tf_op jit(solution)/shard_map/ppermute | solution.py:407
  62.5 1.6 %output_half.2 = (bf16[256,32,128]{2,1,0:T(8,128)(2,1)}, f32[8,128]{1,0:T(8,128)S(1)}) custom-call(s32[1]{0:T(128)} %bitcast.5.refs_0_.refs_1_, bf16[32,256,128]{2,1,0:T(8,128)(2,1)S(1)} %bitcast.19, bf16[256,256]{1,0:T(8,128)(2,1)S(1)} %copy-done.1, f32[1,256]{1,0:T(1,128)S(1)} %bitcast.22, bf16[2,256,128]{2,1,0:T(8,128)(2,1)S(1)} %get-tuple-element.138.refs_4_, ...), custom_call_target="tpu_custom_call" | custom-call | flops 1 | bytes 1 | tf_op jit(solution)/shard_map/output_half/pallas_call | solution.py:68
  64.1 0.4 output_begun.1
  64.5 2.8 %collective-permute-done.24.refs_5_ = bf16[2,256,128]{2,1,0:T(8,128)(2,1)S(1)} collective-permute-done((bf16[2,256,128]{2,1,0:T(8,128)(2,1)S(1)}, bf16[2,256,128]{2,1,0:T(8,128)(2,1)S(1)}, u32[]{:S(2)}, u32[]{:S(2)}) %collective-permute-start.24) | collective-permute-done | bytes 131104 | tf_op jit(solution)/shard_map/ppermute | solution.py:407
  67.3 2.0 %output_half.3 = (bf16[256,32,128]{2,1,0:T(8,128)(2,1)}, f32[8,128]{1,0:T(8,128)}) custom-call(s32[1]{0:T(128)} %bitcast.refs_0_, bf16[32,256,128]{2,1,0:T(8,128)(2,1)S(1)} %bitcast.21, bf16[256,256]{1,0:T(8,128)(2,1)S(1)} %copy-done.1, f32[1,256]{1,0:T(1,128)S(1)} %bitcast.24, ...), custom_call_target="tpu_custom_call", output_to_operand_aliasing={{0}: (7, {})} | custom-call | flops 1 | bytes 1 | tf_op jit(solution)/shard_map/output_half/pallas_call | solution.py:68
  (24 shorter events, 0.2 us)
Async XLA Ops:
  0.0 2.5 %copy-start = (bf16[3,3,256,256]{3,2,1,0:T(8,128)(2,1)S(1)}, bf16[3,3,256,256]{3,2,1,0:T(8,128)(2,1)}, u32[]{:S(2)}) copy-start(bf16[3,3,256,256]{3,2,1,0:T(8,128)(2,1)} %refs_3_.13) | copy-start | bytes 3538948
  0.0 2.5 %copy-start.2 = (f32[1,256]{1,0:T(1,128)S(1)}, f32[1,256]{1,0:T(1,128)}, u32[]{:S(2)}) copy-start(f32[1,256]{1,0:T(1,128)} %refs_4_.13) | copy-start | bytes 3076
  4.7 7.6 %collective-permute-start = (bf16[528,128]{1,0:T(8,128)(2,1)}, bf16[528,128]{1,0:T(8,128)(2,1)S(1)}, u32[]{:S(2)}, u32[]{:S(2)}) collective-permute-start(bf16[528,128]{1,0:T(8,128)(2,1)} %get-tuple-element.77), channel_id=1, source_target_pairs={{0,4},{4,0},{8,12},{12,8},{16,20},{20,16},{24,28},{28,24},{1,5},{5... | collective-permute-start | bytes 405512 | tf_op jit(solution)/shard_map/ppermute | solution.py:363
  7.7 11.6 %collective-permute-start.4 = (bf16[4,256,128]{2,1,0:T(8,128)(2,1)}, bf16[4,256,128]{2,1,0:T(8,128)(2,1)}, u32[]{:S(2)}, u32[]{:S(2)}) collective-permute-start(bf16[4,256,128]{2,1,0:T(8,128)(2,1)} %get-tuple-element.87), channel_id=1, source_target_pairs={{0,4},{4,0},{8,12},{12,8},{16,20},{20,16},{24,28},{28,24},{1,5},{5... | collective-permute-start | bytes 786440 | tf_op jit(solution)/shard_map/ppermute | solution.py:363
  7.7 7.7 %collective-permute-start.1 = (bf16[256,128]{1,0:T(8,128)(2,1)}, bf16[256,128]{1,0:T(8,128)(2,1)S(1)}, u32[]{:S(2)}, u32[]{:S(2)}) collective-permute-start(bf16[256,128]{1,0:T(8,128)(2,1)} %get-tuple-element.80), channel_id=1, source_target_pairs={{0,1},{1,2},{2,3},{3,0},{4,5},{5,6},{6,7},{7,4},{8,9},{9,10},{10,1... | collective-permute-start | bytes 196616 | tf_op jit(solution)/shard_map/ppermute | solution.py:364
  7.7 7.7 %collective-permute-start.2 = (bf16[256,128]{1,0:T(8,128)(2,1)}, bf16[256,128]{1,0:T(8,128)(2,1)S(1)}, u32[]{:S(2)}, u32[]{:S(2)}) collective-permute-start(bf16[256,128]{1,0:T(8,128)(2,1)} %get-tuple-element.81), channel_id=1, source_target_pairs={{0,3},{1,0},{2,1},{3,2},{4,7},{5,4},{6,5},{7,6},{8,11},{9,8},{10,9... | collective-permute-start | bytes 196616 | tf_op jit(solution)/shard_map/ppermute | solution.py:364
  13.2 6.0 %collective-permute-start.5 = (bf16[2,256,128]{2,1,0:T(8,128)(2,1)S(1)}, bf16[2,256,128]{2,1,0:T(8,128)(2,1)S(1)}, u32[]{:S(2)}, u32[]{:S(2)}) collective-permute-start(bf16[2,256,128]{2,1,0:T(8,128)(2,1)S(1)} %get-tuple-element.89), channel_id=1, source_target_pairs={{0,8},{4,12},{8,0},{12,4},{16,24},{20,28},{24,16},{28,20},{1,9},{5... | collective-permute-start | bytes 393224 | tf_op jit(solution)/shard_map/ppermute | solution.py:394
  17.7 7.8 %collective-permute-start.7 = (bf16[4,256,128]{2,1,0:T(8,128)(2,1)S(1)}, bf16[4,256,128]{2,1,0:T(8,128)(2,1)S(1)}, u32[]{:S(2)}, u32[]{:S(2)}) collective-permute-start(bf16[4,256,128]{2,1,0:T(8,128)(2,1)S(1)} %get-tuple-element.93), channel_id=1, source_target_pairs={{0,4},{4,0},{8,12},{12,8},{16,20},{20,16},{24,28},{28,24},{1,5},{5... | collective-permute-start | bytes 786440 | tf_op jit(solution)/shard_map/ppermute | solution.py:397
  21.4 7.1 %collective-permute-start.6 = (bf16[4,256,128]{2,1,0:T(8,128)(2,1)S(1)}, bf16[4,256,128]{2,1,0:T(8,128)(2,1)S(1)}, u32[]{:S(2)}, u32[]{:S(2)}) collective-permute-start(bf16[4,256,128]{2,1,0:T(8,128)(2,1)S(1)} %get-tuple-element.92), channel_id=1, source_target_pairs={{0,8},{4,12},{8,0},{12,4},{16,24},{20,28},{24,16},{28,20},{1,9},{5... | collective-permute-start | bytes 786440 | tf_op jit(solution)/shard_map/ppermute | solution.py:394
  22.6 7.7 %collective-permute-start.3 = (bf16[4,256,128]{2,1,0:T(8,128)(2,1)S(1)}, bf16[4,256,128]{2,1,0:T(8,128)(2,1)S(1)}, u32[]{:S(2)}, u32[]{:S(2)}) collective-permute-start(bf16[4,256,128]{2,1,0:T(8,128)(2,1)S(1)} %get-tuple-element.86), channel_id=1, source_target_pairs={{0,4},{4,0},{8,12},{12,8},{16,20},{20,16},{24,28},{28,24},{1,5},{5... | collective-permute-start | bytes 786440 | tf_op jit(solution)/shard_map/ppermute | solution.py:397
  24.1 7.3 %collective-permute-start.8 = (bf16[2,256,128]{2,1,0:T(8,128)(2,1)S(1)}, bf16[2,256,128]{2,1,0:T(8,128)(2,1)S(1)}, u32[]{:S(2)}, u32[]{:S(2)}) collective-permute-start(bf16[2,256,128]{2,1,0:T(8,128)(2,1)S(1)} %get-tuple-element.102), channel_id=1, source_target_pairs={{0,1},{1,0},{2,3},{3,2},{4,5},{5,4},{6,7},{7,6},{8,16},{9,17},{10,... | collective-permute-start | bytes 393224 | tf_op jit(solution)/shard_map/ppermute | solution.py:415
  26.7 8.3 %collective-permute-start.11 = (bf16[4,256,128]{2,1,0:T(8,128)(2,1)S(1)}, bf16[4,256,128]{2,1,0:T(8,128)(2,1)S(1)}, u32[]{:S(2)}, u32[]{:S(2)}) collective-permute-start(bf16[4,256,128]{2,1,0:T(8,128)(2,1)S(1)} %get-tuple-element.107), channel_id=1, source_target_pairs={{0,8},{4,12},{8,0},{12,4},{16,24},{20,28},{24,16},{28,20},{1,9},{5... | collective-permute-start | bytes 786440 | tf_op jit(solution)/shard_map/ppermute | solution.py:394
  28.6 10.5 %collective-permute-start.12 = (bf16[4,256,128]{2,1,0:T(8,128)(2,1)S(1)}, bf16[4,256,128]{2,1,0:T(8,128)(2,1)S(1)}, u32[]{:S(2)}, u32[]{:S(2)}) collective-permute-start(bf16[4,256,128]{2,1,0:T(8,128)(2,1)S(1)} %get-tuple-element.111), channel_id=1, source_target_pairs={{0,1},{1,0},{2,3},{3,2},{4,5},{5,4},{6,7},{7,6},{8,16},{9,17},{10,... | collective-permute-start | bytes 786440 | tf_op jit(solution)/shard_map/ppermute | solution.py:415
  31.5 8.3 %collective-permute-start.9 = (bf16[4,256,128]{2,1,0:T(8,128)(2,1)S(1)}, bf16[4,256,128]{2,1,0:T(8,128)(2,1)S(1)}, u32[]{:S(2)}, u32[]{:S(2)}) collective-permute-start(bf16[4,256,128]{2,1,0:T(8,128)(2,1)S(1)} %get-tuple-element.104), channel_id=1, source_target_pairs={{0,8},{4,12},{8,0},{12,4},{16,24},{20,28},{24,16},{28,20},{1,9},{5... | collective-permute-start | bytes 786440 | tf_op jit(solution)/shard_map/ppermute | solution.py:394
  33.4 5.0 %collective-permute-start.10 = (bf16[2,256,128]{2,1,0:T(8,128)(2,1)S(1)}, bf16[2,256,128]{2,1,0:T(8,128)(2,1)S(1)}, u32[]{:S(2)}, u32[]{:S(2)}) collective-permute-start(bf16[2,256,128]{2,1,0:T(8,128)(2,1)S(1)} %get-tuple-element.106), channel_id=1, source_target_pairs={{0,4},{4,0},{8,12},{12,8},{16,20},{20,16},{24,28},{28,24},{1,5},{5... | collective-permute-start | bytes 393224 | tf_op jit(solution)/shard_map/ppermute | solution.py:397
  35.1 6.9 %collective-permute-start.15 = (bf16[4,256,128]{2,1,0:T(8,128)(2,1)S(1)}, bf16[4,256,128]{2,1,0:T(8,128)(2,1)S(1)}, u32[]{:S(2)}, u32[]{:S(2)}) collective-permute-start(bf16[4,256,128]{2,1,0:T(8,128)(2,1)S(1)} %get-tuple-element.118), channel_id=1, source_target_pairs={{0,1},{1,0},{2,3},{3,2},{4,5},{5,4},{6,7},{7,6},{8,16},{9,17},{10,... | collective-permute-start | bytes 786440 | tf_op jit(solution)/shard_map/ppermute | solution.py:415
  39.1 7.2 %collective-permute-start.14 = (bf16[4,256,128]{2,1,0:T(8,128)(2,1)S(1)}, bf16[4,256,128]{2,1,0:T(8,128)(2,1)S(1)}, u32[]{:S(2)}, u32[]{:S(2)}) collective-permute-start(bf16[4,256,128]{2,1,0:T(8,128)(2,1)S(1)} %get-tuple-element.116), channel_id=1, source_target_pairs={{0,8},{4,12},{8,0},{12,4},{16,24},{20,28},{24,16},{28,20},{1,9},{5... | collective-permute-start | bytes 786440 | tf_op jit(solution)/shard_map/ppermute | solution.py:394
  40.1 8.7 %collective-permute-start.13 = (bf16[4,256,128]{2,1,0:T(8,128)(2,1)S(1)}, bf16[4,256,128]{2,1,0:T(8,128)(2,1)S(1)}, u32[]{:S(2)}, u32[]{:S(2)}) collective-permute-start(bf16[4,256,128]{2,1,0:T(8,128)(2,1)S(1)} %get-tuple-element.115), channel_id=1, source_target_pairs={{0,1},{1,0},{2,3},{3,2},{4,5},{5,4},{6,7},{7,6},{8,16},{9,17},{10,... | collective-permute-start | bytes 786440 | tf_op jit(solution)/shard_map/ppermute | solution.py:415
  40.2 8.6 %collective-permute-start.16 = (bf16[2,256,128]{2,1,0:T(8,128)(2,1)S(1)}, bf16[2,256,128]{2,1,0:T(8,128)(2,1)S(1)}, u32[]{:S(2)}, u32[]{:S(2)}) collective-permute-start(bf16[2,256,128]{2,1,0:T(8,128)(2,1)S(1)} %get-tuple-element.122), channel_id=1, source_target_pairs={{0,4},{4,0},{8,12},{12,8},{16,20},{20,16},{24,28},{28,24},{1,5},{5... | collective-permute-start | bytes 393224 | tf_op jit(solution)/shard_map/ppermute | solution.py:407
  42.0 10.3 %collective-permute-start.19 = (bf16[4,256,128]{2,1,0:T(8,128)(2,1)S(1)}, bf16[4,256,128]{2,1,0:T(8,128)(2,1)S(1)}, u32[]{:S(2)}, u32[]{:S(2)}) collective-permute-start(bf16[4,256,128]{2,1,0:T(8,128)(2,1)S(1)} %get-tuple-element.127), channel_id=1, source_target_pairs={{0,8},{4,12},{8,0},{12,4},{16,24},{20,28},{24,16},{28,20},{1,9},{5... | collective-permute-start | bytes 786440 | tf_op jit(solution)/shard_map/ppermute | solution.py:394
  46.4 8.0 %collective-permute-start.20 = (bf16[4,256,128]{2,1,0:T(8,128)(2,1)S(1)}, bf16[4,256,128]{2,1,0:T(8,128)(2,1)S(1)}, u32[]{:S(2)}, u32[]{:S(2)}) collective-permute-start(bf16[4,256,128]{2,1,0:T(8,128)(2,1)S(1)} %get-tuple-element.130), channel_id=1, source_target_pairs={{0,4},{4,0},{8,12},{12,8},{16,20},{20,16},{24,28},{28,24},{1,5},{5... | collective-permute-start | bytes 786440 | tf_op jit(solution)/shard_map/ppermute | solution.py:407
  48.8 9.3 %collective-permute-start.17 = (bf16[4,256,128]{2,1,0:T(8,128)(2,1)S(1)}, bf16[4,256,128]{2,1,0:T(8,128)(2,1)S(1)}, u32[]{:S(2)}, u32[]{:S(2)}) collective-permute-start(bf16[4,256,128]{2,1,0:T(8,128)(2,1)S(1)} %get-tuple-element.124), channel_id=1, source_target_pairs={{0,8},{4,12},{8,0},{12,4},{16,24},{20,28},{24,16},{28,20},{1,9},{5... | collective-permute-start | bytes 786440 | tf_op jit(solution)/shard_map/ppermute | solution.py:394
  50.0 4.4 %collective-permute-start.18 = (bf16[2,256,128]{2,1,0:T(8,128)(2,1)S(1)}, bf16[2,256,128]{2,1,0:T(8,128)(2,1)S(1)}, u32[]{:S(2)}, u32[]{:S(2)}) collective-permute-start(bf16[2,256,128]{2,1,0:T(8,128)(2,1)S(1)} %get-tuple-element.125), channel_id=1, source_target_pairs={{0,1},{1,0},{2,3},{3,2},{4,5},{5,4},{6,7},{7,6},{8,16},{9,17},{10,... | collective-permute-start | bytes 393224 | tf_op jit(solution)/shard_map/ppermute | solution.py:415
  52.4 7.5 %collective-permute-start.23 = (bf16[4,256,128]{2,1,0:T(8,128)(2,1)S(1)}, bf16[4,256,128]{2,1,0:T(8,128)(2,1)S(1)}, u32[]{:S(2)}, u32[]{:S(2)}) collective-permute-start(bf16[4,256,128]{2,1,0:T(8,128)(2,1)S(1)} %get-tuple-element.136), channel_id=1, source_target_pairs={{0,4},{4,0},{8,12},{12,8},{16,20},{20,16},{24,28},{28,24},{1,5},{5... | collective-permute-start | bytes 786440 | tf_op jit(solution)/shard_map/ppermute | solution.py:407
  54.4 8.1 %copy-start.1 = (bf16[256,256]{1,0:T(8,128)(2,1)S(1)}, bf16[256,256]{1,0:T(8,128)(2,1)}, u32[]{:S(2)}) copy-start(bf16[256,256]{1,0:T(8,128)(2,1)} %refs_2_.5) | copy-start | bytes 393220
  54.4 8.1 %copy-start.3 = (f32[256]{0:T(256)S(1)}, f32[256]{0:T(256)}, u32[]{:S(2)}) copy-start(f32[256]{0:T(256)} %param.8) | copy-start | bytes 3076
  54.5 5.2 %collective-permute-start.22 = (bf16[2,256,128]{2,1,0:T(8,128)(2,1)S(1)}, bf16[2,256,128]{2,1,0:T(8,128)(2,1)S(1)}, u32[]{:S(2)}, u32[]{:S(2)}) collective-permute-start(bf16[2,256,128]{2,1,0:T(8,128)(2,1)S(1)} %get-tuple-element.134), channel_id=1, source_target_pairs={{0,8},{4,12},{8,0},{12,4},{16,24},{20,28},{24,16},{28,20},{1,9},{5... | collective-permute-start | bytes 393224 | tf_op jit(solution)/shard_map/ppermute | solution.py:394
  58.3 9.1 %collective-permute-start.21 = (bf16[4,256,128]{2,1,0:T(8,128)(2,1)S(1)}, bf16[4,256,128]{2,1,0:T(8,128)(2,1)S(1)}, u32[]{:S(2)}, u32[]{:S(2)}) collective-permute-start(bf16[4,256,128]{2,1,0:T(8,128)(2,1)S(1)} %get-tuple-element.132), channel_id=1, source_target_pairs={{0,4},{4,0},{8,12},{12,8},{16,20},{20,16},{24,28},{28,24},{1,5},{5... | collective-permute-start | bytes 786440 | tf_op jit(solution)/shard_map/ppermute | solution.py:407
  59.9 7.4 %collective-permute-start.24 = (bf16[2,256,128]{2,1,0:T(8,128)(2,1)S(1)}, bf16[2,256,128]{2,1,0:T(8,128)(2,1)S(1)}, u32[]{:S(2)}, u32[]{:S(2)}) collective-permute-start(bf16[2,256,128]{2,1,0:T(8,128)(2,1)S(1)} %get-tuple-element.137), channel_id=1, source_target_pairs={{0,4},{4,0},{8,12},{12,8},{16,20},{20,16},{24,28},{28,24},{1,5},{5... | collective-permute-start | bytes 393224 | tf_op jit(solution)/shard_map/ppermute | solution.py:407
